TPU v7x, 256 devices: a whole 4x4x8 slice. The times are simulated.
256 devices in a mesh: group: 2 (over core), tensor: 8 (over x, y_lo), seq: 16 (over y_hi, z).
Axes of the slice: x: 4, y: 4 (y_hi: 2, y_lo: 2; y = y_hi * 2 + y_lo), z: 8, core: 2. Of those that a mesh axis runs over, the one named last changes fastest.
Arguments:
- teacher_query: bfloat16 [2, 4096, 8192], P('group', 'seq', 'tensor'), may hold values from -150 to 150
- teacher_keyval: bfloat16 [2, 4096, 2048], P('group', 'seq', 'tensor'), may hold values from -5 to 5
- segment_ids: int32 [4096], P('seq'), may hold values from 0 to 7, never falling along the last dimension, each value on 1 to 2304 neighbouring positions
- projector: bfloat16 [8192, 4096], P('tensor'), may hold values from -0.5 to 0.5
- owner_table: int32 [4096, 1], replicated, may hold values from 0 to 15; in each aligned block of 256 rows (0 to 255, 256 to 511, ...) at most 24 rows name the same one
- student_context: bfloat16 [6144, 4096], P('seq'), may hold values from -6 to 6
- student_out_weight: bfloat16 [4096, 4096], P('seq', 'tensor'), may hold values from -0.09375 to 0.09375
Outputs:
- student_grad: float32 [2, 4096, 4096], P('group', 'seq', 'tensor')
Inputs may be any that keep to these rules, and one draw needn't show every extreme that they name: `owner_table`: in each aligned block of 256 rows (the tokens of one teacher shard) no owner appears more than 24 times, and some owner appears exactly 24 times in some block; every owner appears somewhere.
All inputs are finite; a program needn't handle non-finite values.
Results may differ from a plain program's by a relative error of at most 0.025.
Values may be sent and summed in bfloat16 or wider, within the bound.
No kernel may reach another device: no remote copies, remote signals or barrier semaphores. Data moves between devices by JAX's collectives and lax.ppermute only.
A program may use at most 128 MiB of HBM per device.

v0:
```python
import jax
import jax.numpy as jnp
from jax import lax
from jax.sharding import PartitionSpec as P

HD = 128


block_keys = 1024
neg_large = -1e30


def spread(value, axis, source):
    kept = jnp.where(lax.axis_index(axis) == source, value, 0).astype(value.dtype)
    return lax.psum(kept, axis)


def bucket_rows(row_block, owners, capacity, owner_count):
    onehot = (owners[:, None] == jnp.arange(owner_count, dtype=jnp.int32)[None, :]).astype(
        jnp.int32
    )
    ranking = jnp.sum((jnp.cumsum(onehot, axis=0) - onehot) * onehot, axis=1)
    target_slot = owners * capacity + ranking
    route_tokens = (
        jnp.arange(owner_count * capacity, dtype=jnp.int32)[:, None] == target_slot[None, :]
    ).astype(jnp.bfloat16)
    return jnp.dot(route_tokens, row_block, preferred_element_type=jnp.float32).astype(jnp.bfloat16)


def attend(teacher_query, teacher_keyval, segment_ids):
    tok_rows = teacher_query.shape[0]
    heads_local = teacher_query.shape[1] // HD
    groups_local = teacher_keyval.shape[1] // (2 * HD)
    per_group = heads_local // groups_local
    query_matrix = teacher_query.reshape(tok_rows, groups_local, per_group, HD)
    first_row = lax.axis_index("seq") * tok_rows
    query_pos = first_row + jnp.arange(tok_rows, dtype=jnp.int32)
    scaling = HD ** (-0.5)
    start = jnp.int32(0)
    running_top = jnp.full((groups_local, per_group, tok_rows), neg_large, jnp.float32)
    running_total = jnp.zeros((groups_local, per_group, tok_rows), jnp.float32)
    running_sum = jnp.zeros((groups_local, per_group, tok_rows, HD), jnp.float32)
    kv_piece = lax.all_gather(teacher_keyval, "seq", axis=0, tiled=True)
    seg_piece = lax.all_gather(segment_ids, "seq", axis=0, tiled=True)
    piece_rows = kv_piece.shape[0]
    for offset in range(0, piece_rows, block_keys):
        finish = min(piece_rows, offset + block_keys)
        width_rows = finish - offset
        divide_parts = kv_piece[offset:finish].reshape(width_rows, groups_local, 2, HD)
        scores = (
            jnp.einsum(
                "hnpz,fnz->nphf",
                query_matrix,
                divide_parts[:, :, 0],
                preferred_element_type=jnp.float32,
            )
            * scaling
        )
        key_pos = start + offset + jnp.arange(width_rows, dtype=jnp.int32)
        allowed = (key_pos[None, :] <= query_pos[:, None]) & (
            seg_piece[offset:finish][None, :] == segment_ids[:, None]
        )
        masked = jnp.where(allowed, scores, neg_large)
        new_top = jnp.maximum(running_top, jnp.max(masked, axis=-1))
        old_scale = jnp.exp(running_top - new_top)
        weights = jnp.where(allowed, jnp.exp(scores - new_top[..., None]), 0.0)
        running_total = running_total * old_scale + jnp.sum(weights, axis=-1)
        running_sum = running_sum * old_scale[..., None] + jnp.einsum(
            "vwkn,nvb->vwkb",
            weights.astype(jnp.bfloat16),
            divide_parts[:, :, 1],
            preferred_element_type=jnp.float32,
        )
        running_top = new_top
    running_top, running_total, running_sum = (running_top, running_total, running_sum)
    context = running_sum / running_total[..., None]
    return (
        jnp.transpose(context, (2, 0, 1, 3))
        .reshape(tok_rows, heads_local * HD)
        .astype(jnp.bfloat16)
    )


def shards(
    teacher_query,
    teacher_keyval,
    segment_ids,
    projector,
    owner_table,
    student_context,
    student_out_weight,
):
    query_rows = teacher_query[0]
    keyval_rows = teacher_keyval[0]
    tok_rows = query_rows.shape[0]
    seq_count = lax.axis_size("seq")
    slot_count = student_context.shape[0]
    capacity = slot_count // seq_count
    owners_all = owner_table[:, 0]
    own_owners = lax.dynamic_slice_in_dim(owners_all, lax.axis_index("seq") * tok_rows, tok_rows)
    context = attend(query_rows, keyval_rows, segment_ids)
    partial_sums = jnp.dot(context, projector, preferred_element_type=jnp.float32)
    row_block = lax.psum_scatter(
        partial_sums.astype(jnp.bfloat16), "tensor", scatter_dimension=1, tiled=True
    )
    row_block = lax.all_to_all(
        bucket_rows(row_block, own_owners, capacity, seq_count),
        "seq",
        split_axis=0,
        concat_axis=0,
        tiled=True,
    )
    arrived = spread(row_block, "group", 0)
    row_block = arrived
    counts = jnp.sum(
        (owners_all.reshape(seq_count, tok_rows) == lax.axis_index("seq")).astype(jnp.int32), axis=1
    )
    live = (
        (jnp.arange(capacity, dtype=jnp.int32)[None, :] < counts[:, None])
        .reshape(slot_count)
        .astype(jnp.float32)
    )
    feature_vectors = student_context
    student_out = jnp.dot(
        feature_vectors,
        lax.all_gather(student_out_weight, "seq", axis=0, tiled=True),
        preferred_element_type=jnp.float32,
    )
    residual = ((student_out - row_block.astype(jnp.float32)) * live[:, None] / tok_rows).astype(
        jnp.bfloat16
    )
    feature_vectors = student_context
    gradient = lax.psum_scatter(
        lax.dot_general(
            feature_vectors, residual, (((0,), (0,)), ((), ())), preferred_element_type=jnp.float32
        ).astype(jnp.bfloat16),
        "seq",
        scatter_dimension=0,
        tiled=True,
    ).astype(jnp.float32)
    is_student = lax.axis_index("group") == 1
    return jnp.where(is_student, gradient, 0.0)[None]


def solution(mesh):
    placed = (
        P("group", "seq", "tensor"),
        P("group", "seq", "tensor"),
        P("seq"),
        P("tensor", None),
        P(),
        P("seq", None),
        P("seq", "tensor"),
    )
    return jax.shard_map(
        shards, mesh=mesh, in_specs=placed, out_specs=P("group", "seq", "tensor"), check_vma=False
    )
```

profile of v0, /device:TPU:1, one launch (start us, length us, event | category | flops | bytes accessed | tf_op | source)
XLA Modules:
  0.0 548.2 jit_solution(8253034938887141038)
XLA Ops:
  6.5 1.8 copy.37
  8.4 1.9 copy.60
  10.4 37.9 %all-gather.1 = s32[16,1,256]{2,1,0:T(1,128)S(1)} all-gather(s32[1,1,256]{2,1,0:T(1,128)} %bitcast.243), channel_id=1, replica_groups=mesh['group'=2,'tensor'=8,'seq'=16] {'seq'}, dimensions={0}, use_global_device_ids=true | all-gather | bytes 17408 | tf_op jit(solution)/shard_map/all_gather | solution.py:44
  48.3 3.0 compare_and_fusion.2
  51.3 44.4 %all-gather.7.cloned.1.call-done = bf16[1,4096,256]{1,2,0:T(8,128)(2,1)} async-done(((bf16[1,256,256]{1,2,0:T(8,128)(2,1)}), bf16[1,4096,256]{1,2,0:T(8,128)(2,1)}) %all-gather.7.cloned.1.call-update) | async-done | bytes 2097168 | tf_op jit(solution)/shard_map/all_gather | solution.py:43
  95.7 1.8 fusion.93
  97.5 2.6 fusion.9
  100.2 1.5 fusion
  101.7 1.5 fusion.3
  103.2 4.7 fusion.6
  107.9 5.7 %fusion.12 = (f32[8,256]{1,0:T(8,128)S(1)}, f32[8,256]{1,0:T(8,128)S(1)}) fusion(f32[1024,256,8]{1,0,2:T(8,128)S(1)} %get-tuple-element.33, f32[8,256]{1,0:T(8,128)S(1)} %get-tuple-element.21, pred[256,1024]{0,1:T(8,128)(4,1)S(1)} %copy-done.4, f32[8,256]{1,0:T(8,128)S(1)} %get-tuple-element.11, f32[1024,256,8]{1,0,2:T(8,128)} %get-tuple-element.31, ...), kind=kLoop, calls=%fused_computation.20 | loop fusion | flops 16773120 | bytes 17334272 | tf_op jit(solution)/shard_map/reduce_sum | solution.py:67
  113.6 3.7 fusion.16
  117.3 1.9 fusion.49
  119.3 5.3 fusion.52
  124.5 1.9 fusion.55
  126.4 1.9 divide_convert_fusion
  128.6 1.3 slice-done.1
  129.9 3.8 convolution_convert_fusion.1
  133.8 0.7 all-gather.5.cloned.1.call-update
  134.5 0.6 reduce-window.6
  135.5 51.0 %reduce-scatter.3.cloned.1.call-done = bf16[256,512]{1,0:T(8,128)(2,1)} async-done(((bf16[256,4096]{1,0:T(8,128)(2,1)}), bf16[256,512]{1,0:T(8,128)(2,1)}) %reduce-scatter.3.cloned.1.call-update) | async-done | bytes 262160 | tf_op jit(solution)/shard_map/reduce_scatter | solution.py:103
  186.5 2.0 convolution_convert_fusion.2
  188.5 10.0 %all-to-all-start = ((bf16[16,24,512]{2,1,0:T(8,128)(2,1)}), bf16[16,24,512]{2,1,0:T(8,128)(2,1)}, u32[]{:S(2)}, u32[]{:S(2)}) async-start(bf16[16,24,512]{2,1,0:T(8,128)(2,1)} %bitcast.224), calls=%async_computation.1 | async-start | bytes 786432 | tf_op jit(solution)/shard_map/all_to_all | solution.py:106
  198.5 12.4 %all-to-all-done = bf16[16,24,512]{2,1,0:T(8,128)(2,1)} async-done(((bf16[16,24,512]{2,1,0:T(8,128)(2,1)}), bf16[16,24,512]{2,1,0:T(8,128)(2,1)}, u32[]{:S(2)}, u32[]{:S(2)}) %all-to-all-start) | async-done | bytes 393248 | tf_op jit(solution)/shard_map/all_to_all | solution.py:106
  210.9 0.8 broadcast_select_fusion
  211.7 0.3 reduce-scatter.5.cloned.1.call-start
  212.3 75.9 %all-gather.5.cloned.1.call-done = bf16[4096,512]{1,0:T(8,128)(2,1)} async-done(((bf16[256,512]{1,0:T(8,128)(2,1)}), bf16[4096,512]{1,0:T(8,128)(2,1)}) %all-gather.5.cloned.1.call-update) | async-done | bytes 4194320 | tf_op jit(solution)/shard_map/all_gather | solution.py:126
  288.2 32.2 %all-reduce.2.cloned.1.call-done = bf16[384,512]{1,0:T(8,128)(2,1)} async-done(((bf16[384,512]{1,0:T(8,128)(2,1)}), bf16[384,512]{1,0:T(8,128)(2,1)}) %all-reduce.2.cloned.1.call-update) | async-done | bytes 393232 | tf_op jit(solution)/shard_map/psum | solution.py:15
  320.5 8.4 %fusion.20 = bf16[4096,512]{0,1:T(8,128)(2,1)} fusion(bf16[384,4096]{1,0:T(8,128)(2,1)S(1)} %copy-done, bf16[4096,512]{1,0:T(8,128)(2,1)} %all-gather.5.cloned.1.call-done, bf16[384,512]{1,0:T(8,128)(2,1)} %all-reduce.2.cloned.1.call-done, f32[384]{0:T(512)S(1)} %reshape.346), kind=kOutput, calls=%fused_computation.29 | convolution fusion | flops 3224305664 | bytes 11929088 | tf_op jit(solution)/shard_map/dot_general | solution.py:134
  328.9 209.0 %reduce-scatter.5.cloned.1.call-done = bf16[256,512]{0,1:T(8,128)(2,1)} async-done(((bf16[4096,512]{0,1:T(8,128)(2,1)}), bf16[256,512]{0,1:T(8,128)(2,1)}) %reduce-scatter.5.cloned.1.call-update) | async-done | bytes 262160 | tf_op jit(solution)/shard_map/reduce_scatter | solution.py:133
  537.9 1.8 select_bitcast_fusion
  539.7 2.0 copy.50
  (43 shorter events, 1.2 us)
Async XLA Ops:
  6.5 313.9 %copy-start = (bf16[384,4096]{1,0:T(8,128)(2,1)S(1)}, bf16[384,4096]{1,0:T(8,128)(2,1)}, u32[]{:S(2)}) copy-start(bf16[384,4096]{1,0:T(8,128)(2,1)} %param.12) | copy-start | bytes 9437188
  6.5 89.2 %all-gather.7.cloned.1.call-start = ((), (), s32[]{:S(2)}) async-start(), calls=%async_computation.7 | async-start | bytes 2228224 | tf_op jit(solution)/shard_map/all_gather | solution.py:43
  8.4 178.1 %reduce-scatter.3.cloned.1.call-start = ((), (), s32[]{:S(2)}) async-start(), calls=%async_computation.4 | async-start | bytes 2359296 | tf_op jit(solution)/shard_map/reduce_scatter | solution.py:103
  95.7 4.4 copy-start.1
  97.5 4.2 copy-start.2
  100.1 3.0 copy-start.3
  101.7 6.2 %copy-start.4 = (pred[256,1024]{0,1:T(8,128)(4,1)S(1)}, pred[256,1024]{0,1:T(8,128)(4,1)}, u32[]{:S(2)}) copy-start(pred[256,1024]{0,1:T(8,128)(4,1)} %get-tuple-element.25) | copy-start | bytes 786436
  126.4 2.2 slice-start
  126.4 3.5 slice-start.1
  128.4 6.1 %copy-start.5 = (s32[4096,1]{0,1:T(1,128)S(1)}, s32[4096,1]{0,1:T(1,128)}, u32[]{:S(2)}) copy-start(s32[4096,1]{0,1:T(1,128)} %param.11) | copy-start | bytes 49156
  133.8 154.5 %all-gather.5.cloned.1.call-start = ((), (), s32[]{:S(2)}) async-start(), calls=%async_computation.3 | async-start | bytes 4456448 | tf_op jit(solution)/shard_map/all_gather | solution.py:126
  188.5 22.4 %all-to-all-start = ((bf16[16,24,512]{2,1,0:T(8,128)(2,1)}), bf16[16,24,512]{2,1,0:T(8,128)(2,1)}, u32[]{:S(2)}, u32[]{:S(2)}) async-start(bf16[16,24,512]{2,1,0:T(8,128)(2,1)} %bitcast.224), calls=%async_computation.1 | async-start | bytes 786432 | tf_op jit(solution)/shard_map/all_to_all | solution.py:106
  198.5 122.0 %all-reduce.2.cloned.1.call-start = ((), (), s32[]{:S(2)}) async-start(), calls=%async_computation.5 | async-start | bytes 786432 | tf_op jit(solution)/shard_map/psum | solution.py:15
  211.7 326.2 %reduce-scatter.5.cloned.1.call-start = ((), (), s32[]{:S(2)}) async-start(), calls=%async_computation.6 | async-start | bytes 4456448 | tf_op jit(solution)/shard_map/reduce_scatter | solution.py:133
Sparse Core Ops, SparseCore 0:
  9.8 85.8 all-gather.6
  133.9 52.5 reduce-scatter.2
  189.1 99.1 all-gather.4
  290.7 29.7 all-reduce.1
  329.0 208.8 reduce-scatter.4
where the time goes:
time: 552 us; the launch traced here: 548 us
  waiting for transfers between devices  426 us (77%)
  blocking collectives  37.9 us (7%)
  matrix products  35.5 us (6%)
  other arithmetic  16 us (3%)
  between operations  13.4 us (2%)
  starting transfers between devices  10.4 us (2%)
  local copies, waits for them, and re-layouts  9.35 us (2%)
    reduce_scatter x1, waiting for transfers between devices, shards(): lax.psum_scatter(lax.dot_general(feature_vectors, residual, (((0,), (0,))...  209 us
    all_gather x1, waiting for transfers between devices, shards(): lax.all_gather(student_out_weight, 'seq', axis=0, tiled=True)  75.9 us
    reduce_scatter x1, waiting for transfers between devices, shards(): lax.psum_scatter(partial_sums.astype(jnp.bfloat16), 'tensor', scatter_dim...  51 us
    all_gather x1, waiting for transfers between devices, attend(): kv_piece = lax.all_gather(teacher_keyval, 'seq', axis=0, tiled=True)  44.4 us
    all_gather x1, blocking collectives, attend(): seg_piece = lax.all_gather(segment_ids, 'seq', axis=0, tiled=True)  37.9 us
    psum x1, waiting for transfers between devices, spread(): return lax.psum(kept, axis)  32.2 us
    all_to_all x1, waiting for transfers between devices, shards(): lax.all_to_all(bucket_rows(row_block, own_owners, capacity, seq_count), '...  12.4 us
  transfers between devices with their start and end apart: 6, of which 6 were waited for; matrix products, arithmetic and copies ran while one was open for 2% of the time, Pallas kernels for 0%

commit v1 on v0

v1 whole, which is shorter than its diff:
```python
import functools

import jax
import jax.numpy as jnp
from jax import lax
from jax.experimental import pallas as pl
from jax.experimental.pallas import tpu as pltpu
from jax.sharding import PartitionSpec as P

HD = 128
ZN = 8
WINDOW = 9
PIECE = 272
LOW = -1e30


def ring_pairs(step, base, reps):
    return [
        (base + rep * ZN + z, base + rep * ZN + (z + step) % ZN)
        for rep in range(reps)
        for z in range(ZN)
    ]


def partner_pairs(base):
    return [(base + i, base + (i + ZN) % (2 * ZN)) for i in range(2 * ZN)]


def attention_kernel(info, query, seg_query, pieces, out, acc, top):
    shard = info[0]
    teacher = info[1]
    tok = query.shape[0]
    heads = query.shape[1] // HD
    high = shard // ZN
    ring = lax.rem(shard, ZN)
    scale = (HD**-0.5) * 1.4426950408889634
    count = pieces.shape[0] // PIECE
    seg_q = seg_query[...]
    first_seg = seg_q[0:1, :][0, 0]

    @pl.when(teacher == 0)
    def _():
        top[...] = jnp.full_like(top, LOW)
        acc[...] = jnp.zeros_like(acc)

        def one_block(index, carry):
            pair = index // 2
            other = lax.rem(index, 2)
            dist = (pair + 1) // 2
            sign = 1 - 2 * lax.rem(pair, 2)
            source = lax.rem(ring + sign * dist + ZN, ZN)
            block = (high + other - 2 * high * other) * ZN + source
            start = pl.multiple_of(index * PIECE, 16)
            seg_k = pieces[pl.ds(start + 256, 16), :][0:1, :].astype(jnp.float32)
            last_seg = seg_k[:, 255:256][0, 0]

            @pl.when((block <= shard) & (block >= shard - WINDOW) & (last_seg >= first_seg))
            def _():
                keys = pieces[pl.ds(start, 256), 0:HD]
                values = pieces[pl.ds(start, 256), HD : 2 * HD]
                values = jnp.concatenate([values, jnp.ones_like(values)], axis=1)
                rows = lax.broadcasted_iota(jnp.int32, (tok, 256), 0) + shard * tok
                cols = lax.broadcasted_iota(jnp.int32, (tok, 256), 1) + block * 256
                allowed = (seg_k == seg_q) & (cols <= rows)

                def one_head(head, carry):
                    lanes = pl.ds(pl.multiple_of(head * HD, HD), HD)
                    scores = lax.dot_general(
                        query[:, lanes],
                        keys,
                        (((1,), (1,)), ((), ())),
                        preferred_element_type=jnp.float32,
                    )
                    scores = jnp.where(allowed, scores, LOW)
                    old = top[head]
                    new = jnp.maximum(old, jnp.max(scores, axis=1, keepdims=True))
                    weights = jnp.exp2((scores - new) * scale)
                    fade = jnp.exp2((old - new) * scale)
                    top[head] = new
                    acc[head] = acc[head] * fade + jnp.dot(
                        weights.astype(jnp.bfloat16), values, preferred_element_type=jnp.float32
                    )
                    return carry

                lax.fori_loop(0, heads, one_head, 0, unroll=2)

            return carry

        lax.fori_loop(0, count, one_block, 0)
        for head in range(heads):
            mixed = acc[head]
            out[:, head * HD : (head + 1) * HD] = (mixed[:, :HD] / mixed[:, HD:]).astype(
                jnp.bfloat16
            )


def attend(info, query, seg_query, pieces):
    tok, width = query.shape
    heads = width // HD
    return pl.pallas_call(
        attention_kernel,
        out_shape=jax.ShapeDtypeStruct((tok, width), jnp.bfloat16),
        in_specs=[
            pl.BlockSpec(memory_space=pltpu.SMEM),
            pl.BlockSpec(memory_space=pltpu.VMEM),
            pl.BlockSpec(memory_space=pltpu.VMEM),
            pl.BlockSpec(memory_space=pltpu.VMEM),
        ],
        out_specs=pl.BlockSpec(memory_space=pltpu.VMEM),
        scratch_shapes=[
            pltpu.VMEM((heads, tok, 2 * HD), jnp.float32),
            pltpu.VMEM((heads, tok, 1), jnp.float32),
        ],
        compiler_params=pltpu.CompilerParams(vmem_limit_bytes=32 * 1024 * 1024),
        cost_estimate=pl.CostEstimate(
            flops=8 * tok * width * 2560, bytes_accessed=4 << 20, transcendentals=tok * 8 * 2560
        ),
        name="attend",
    )(info, query, seg_query, pieces)


def gather_keyval(keyval, segments):
    both = ("group", "seq")
    seg_row = jnp.broadcast_to(segments.astype(jnp.bfloat16)[None, :], (16, segments.shape[0]))
    own = jnp.concatenate([keyval, seg_row], axis=0)
    lower = lax.ppermute(own, both, [(z, ZN + z) for z in range(ZN)])
    pair = jnp.concatenate([own, lower], axis=0)
    forward = backward = pair
    found = [pair]
    for _ in range(3):
        forward = lax.ppermute(forward, both, ring_pairs(1, 0, 2))
        backward = lax.ppermute(backward, both, ring_pairs(-1, 0, 2))
        found += [forward, backward]
    found.append(lax.ppermute(forward[:PIECE], both, ring_pairs(1, 0, 2)))
    found.append(lax.ppermute(backward[PIECE:], both, ring_pairs(-1, 0, 2)))
    return jnp.concatenate(found, axis=0)


def shards(
    teacher_query,
    teacher_keyval,
    segment_ids,
    projector,
    owner_table,
    student_context,
    student_out_weight,
):
    group = lax.axis_index("group")
    seq = lax.axis_index("seq")
    high = seq // ZN
    ring = seq % ZN
    query = teacher_query[0]
    tok = query.shape[0]
    slots, model = student_context.shape
    owners_n = 2 * ZN
    capacity = slots // owners_n
    half = model // 2
    feats = student_out_weight.shape[1] // 2
    tensor_n = model // (2 * feats)
    z_groups = [[h * ZN + z for z in range(ZN)] for h in range(2)]

    weight = lax.dynamic_slice_in_dim(student_out_weight, group * feats, feats, axis=1)
    weight = lax.all_gather(weight, "seq", axis=0, tiled=True, axis_index_groups=z_groups)

    pieces = gather_keyval(teacher_keyval[0], segment_ids)

    sent = lax.dynamic_slice_in_dim(
        student_context, (1 - high) * half + group * (half // 2), half // 2, axis=1
    )
    core_swap = [(0, 1), (1, 0)]
    all_pairs = partner_pairs(0) + partner_pairs(owners_n)
    came = lax.ppermute(sent, ("group", "seq"), all_pairs)
    came_other = lax.ppermute(came, "group", core_swap)
    theirs = jnp.where(
        group == 0,
        jnp.concatenate([came, came_other], axis=1),
        jnp.concatenate([came_other, came], axis=1),
    )
    ours = lax.dynamic_slice_in_dim(student_context, high * half, half, axis=1)
    ours = ours.reshape(owners_n, capacity, half)
    theirs = theirs.reshape(owners_n, capacity, half)
    rows = jnp.where(
        high == 0,
        jnp.concatenate([ours, theirs], axis=1),
        jnp.concatenate([theirs, ours], axis=1),
    ).reshape(2 * slots, half)

    info = jnp.stack([seq, group]).astype(jnp.int32)
    seg_query = segment_ids.astype(jnp.float32)[:, None]
    context = attend(info, query, seg_query, pieces)
    passed = lax.ppermute(context, "group", [(0, 1)])
    context = jnp.where(group == 0, context, passed)

    own_projector = lax.dynamic_index_in_dim(
        projector.reshape(projector.shape[0], tensor_n, 2, feats), group, axis=2, keepdims=False
    )
    partial = lax.dot_general(
        context, own_projector, (((1,), (0,)), ((), ())), preferred_element_type=jnp.float32
    ).astype(jnp.bfloat16)
    partial = jnp.transpose(partial, (1, 0, 2))
    partial = lax.all_to_all(partial, "tensor", split_axis=0, concat_axis=0, tiled=True)
    target = jnp.sum(partial.astype(jnp.float32), axis=0).astype(jnp.bfloat16)

    owners_all = owner_table[:, 0]
    owners = lax.dynamic_slice_in_dim(owners_all, seq * tok, tok)
    index = jnp.arange(tok, dtype=jnp.int32)
    ranks = jnp.sum(
        ((owners[:, None] == owners[None, :]) & (index[None, :] < index[:, None])).astype(
            jnp.int32
        ),
        axis=1,
    )
    place = (owners % ZN) * (2 * capacity) + (owners // ZN) * capacity + ranks
    route = (jnp.arange(slots, dtype=jnp.int32)[:, None] == place[None, :]).astype(jnp.bfloat16)
    routed = jnp.dot(route, target, preferred_element_type=jnp.float32).astype(jnp.bfloat16)
    routed = routed.reshape(ZN, 2 * capacity, feats)
    routed = lax.all_to_all(
        jnp.concatenate([routed, routed], axis=0), "seq", split_axis=0, concat_axis=0, tiled=True
    ).reshape(2 * slots, feats)

    output = jnp.dot(rows, weight, preferred_element_type=jnp.float32)
    output = output + lax.ppermute(
        output.astype(jnp.bfloat16), ("group", "seq"), all_pairs
    ).astype(jnp.float32)

    pair_owners = jnp.stack([ring, ring + ZN])
    counts = jnp.sum(
        (owners_all.reshape(owners_n, tok, 1) == pair_owners[None, None, :]).astype(jnp.int32),
        axis=1,
    )
    live = (jnp.arange(capacity, dtype=jnp.int32)[None, None, :] < counts[:, :, None]).reshape(
        2 * slots
    )
    scale = live.astype(jnp.float32)[:, None] / tok
    residual = ((output - routed.astype(jnp.float32)) * scale).astype(jnp.bfloat16)

    gradient = lax.dot_general(
        rows, residual, (((0,), (0,)), ((), ())), preferred_element_type=jnp.float32
    ).astype(jnp.bfloat16)
    gradient = lax.all_to_all(
        gradient.reshape(ZN, half // ZN, feats),
        "seq",
        split_axis=0,
        concat_axis=0,
        tiled=True,
        axis_index_groups=z_groups,
    )
    gradient = jnp.sum(gradient.astype(jnp.float32), axis=0)
    passed = lax.ppermute(gradient, "group", [(0, 1)])
    whole = jnp.concatenate([passed, gradient], axis=1)
    return jnp.where(group == 1, whole, 0.0)[None]


def solution(mesh):
    placed = (
        P("group", "seq", "tensor"),
        P("group", "seq", "tensor"),
        P("seq"),
        P("tensor", None),
        P(),
        P("seq", None),
        P("seq", "tensor"),
    )
    return jax.shard_map(
        shards, mesh=mesh, in_specs=placed, out_specs=P("group", "seq", "tensor"), check_vma=False
    )
```

time: 552 us -> 227 us (0.41)
  waiting for transfers between devices: 426 us -> 21.3 us
  starting transfers between devices: 10.4 us -> 98.3 us
  matrix products: 35.5 us -> 12.4 us
  local copies, waits for them, and re-layouts: 9.35 us -> 30.3 us
  blocking collectives: 37.9 us -> 30.2 us
    reduce_scatter x2 -> x0, waiting for transfers between devices: 260 us -> none  [the longest x1 209 us: shards(): lax.psum_scatter(lax.dot_general(feature_vectors, residual, (((0,), (0,))...]
    all_gather x2 -> x1, waiting for transfers between devices: 120 us -> 0.02 us  [shards(): lax.all_gather(weight, 'seq', axis=0, tiled=True, axis_index_groups=z_gro...]
    ppermute x0 -> x14, starting transfers between devices: none -> 55.1 us  [the longest x1 37.1 us: shards(): came_other = lax.ppermute(came, 'group', core_swap)]
    all_gather x1 -> x0, blocking collectives: 37.9 us -> none  [attend(): seg_piece = lax.all_gather(segment_ids, 'seq', axis=0, tiled=True)]
    all_to_all x1 -> x2, starting transfers between devices: 10 us -> 43.3 us  [the longest x1 39 us: shards(): lax.all_to_all(jnp.concatenate([routed, routed], axis=0), 'seq', split_ax...]
    psum x1 -> x0, waiting for transfers between devices: 32.2 us -> none  [spread(): return lax.psum(kept, axis)]
    all_to_all x0 -> x1, blocking collectives: none -> 30.2 us  [shards(): lax.all_to_all(gradient.reshape(ZN, half // ZN, feats), 'seq', split_axis...]
    dot_general x11 -> x4, matrix products: 35.5 us -> 12.4 us  [the longest x1 4.62 us: shards(): lax.dot_general(context, own_projector, (((1,), (0,)), ((), ())), preferr...]
  transfers between devices with their start and end apart: 6 -> 17, of which waited for: 6 -> 3; matrix products, arithmetic and copies ran while one was open for 2% -> 22% of each run, Pallas kernels for 0% -> 1%
where the time goes in v1:
time: 227 us; the launch traced here: 224 us
  starting transfers between devices  98.3 us (43%)
  local copies, waits for them, and re-layouts  30.3 us (13%)
  blocking collectives  30.2 us (13%)
  waiting for transfers between devices  21.3 us (9%)
  other arithmetic  16.7 us (7%)
  between operations  13.7 us (6%)
  matrix products  12.4 us (5%)
    all_to_all x1, starting transfers between devices, shards(): lax.all_to_all(jnp.concatenate([routed, routed], axis=0), 'seq', split_ax...  39 us
    ppermute x1, starting transfers between devices, shards(): came_other = lax.ppermute(came, 'group', core_swap)  37.1 us
    all_to_all x1, blocking collectives, shards(): lax.all_to_all(gradient.reshape(ZN, half // ZN, feats), 'seq', split_axis...  30.2 us
    unnamed x24, local copies, waits for them, and re-layouts  25 us
    all_to_all x1, waiting for transfers between devices, shards(): lax.all_to_all(partial, 'tensor', split_axis=0, concat_axis=0, tiled=True)  11.5 us
    ppermute x1, waiting for transfers between devices, shards(): passed = lax.ppermute(gradient, 'group', [(0, 1)])  5.13 us
    dot_general x1, matrix products, shards(): lax.dot_general(context, own_projector, (((1,), (0,)), ((), ())), preferr...  4.62 us
    ppermute x1, waiting for transfers between devices, shards(): lax.ppermute(output.astype(jnp.bfloat16), ('group', 'seq'), all_pairs)  4.58 us
  transfers between devices with their start and end apart: 17, of which 3 were waited for; matrix products, arithmetic and copies ran while one was open for 22% of the time, Pallas kernels for 1%

profile of v1, /device:TPU:1, one launch (start us, length us, event | category | flops | bytes accessed | tf_op | source)
XLA Modules:
  0.0 224.3 jit_solution(12703903626902095849)
XLA Ops:
  7.4 1.7 pad_maximum_fusion.2
  10.8 3.7 %collective-permute-start = (bf16[384,1024]{1,0:T(8,128)(2,1)}, bf16[384,1024]{1,0:T(8,128)(2,1)}, u32[]{:S(2)}, u32[]{:S(2)}) collective-permute-start(bf16[384,1024]{1,0:T(8,128)(2,1)} %constant_dynamic-slice_fusion.2), channel_id=1, source_target_pairs={{0,8},{1,9},{2,10},{3,11},{4,12},{5,13},{6,14},{7,15},{8,0},{9,1},... | collective-permute-start | bytes 2359304 | tf_op jit(solution)/shard_map/ppermute | solution.py:172
  15.5 1.4 collective-permute-start.4
  16.9 1.4 collective-permute-start.5
  19.5 1.4 collective-permute-start.6
  20.9 1.4 collective-permute-start.7
  23.1 1.7 constant_dynamic-update-slice_fusion.7
  26.2 1.7 constant_dynamic-update-slice_fusion.6
  27.9 1.7 constant_dynamic-update-slice_fusion.5
  29.6 1.7 constant_dynamic-update-slice_fusion.4
  35.5 1.6 copy-done.1
  37.1 1.4 attend.1
  38.5 1.3 collective-permute-start.12
  40.5 12.0 %copy.14 = bf16[1024,4096]{0,1:T(8,128)(2,1)} copy(bf16[1024,4096]{1,0:T(8,128)(2,1)} %param.10) | data formatting | bytes 16777216 | tf_op args[3]
  52.7 37.1 %collective-permute-start.1 = (bf16[384,1024]{1,0:T(8,128)(2,1)}, bf16[384,1024]{1,0:T(8,128)(2,1)}, u32[]{:S(2)}, u32[]{:S(2)}) collective-permute-start(bf16[384,1024]{1,0:T(8,128)(2,1)} %collective-permute-done), channel_id=1, source_target_pairs={{0,128},{128,0},{1,129},{129,1},{2,130},{130,2},{3,131},{131,3},{4... | collective-permute-start | bytes 2359304 | tf_op jit(solution)/shard_map/ppermute | solution.py:173
  89.7 4.6 %fusion.6 = bf16[8,256,256]{2,1,0:T(8,128)(2,1)} fusion(bf16[1024,8,2,256]{0,3,2,1:T(8,128)(2,1)} %bitcast.38, s32[]{:T(128)S(6)} %select_n.105, bf16[256,1024]{1,0:T(8,128)(2,1)} %attend.1, bf16[256,1024]{1,0:T(8,128)(2,1)} %collective-permute-done.12, pred[]{:T(512)S(6)} %eq.57), kind=kOutput, calls=%fused_computation.8 | convolution fusion | flops 1074528256 | bytes 6291461 | tf_op jit(solution)/shard_map/dot_general | solution.py:197
  94.4 4.3 %all-to-all-start = ((bf16[8,256,256]{2,1,0:T(8,128)(2,1)}), bf16[8,256,256]{2,1,0:T(8,128)(2,1)}, u32[]{:S(2)}, u32[]{:S(2)}) async-start(bf16[8,256,256]{2,1,0:T(8,128)(2,1)} %fusion.6), calls=%async_computation | async-start | bytes 2097152 | tf_op jit(solution)/shard_map/all_to_all | solution.py:201
  98.8 2.5 %maximum_select_fusion.1 = bf16[16,24,2048]{2,1,0:T(8,128)(2,1)S(1)} fusion(bf16[16,24,1024]{2,1,0:T(8,128)(2,1)} %bitcast.2, bf16[16,24,1024]{2,1,0:T(8,128)(2,1)} %bitcast.1, pred[]{:T(512)S(6)} %eq.57), kind=kLoop, calls=%fused_computation.6 | loop fusion | flops 7077888 | bytes 3145729 | tf_op jit(solution)/shard_map/jit(_where)/select_n | solution.py:174
  101.4 2.4 %maximum_select_fusion = bf16[16,48,2048]{2,1,0:T(8,128)(2,1)} fusion(bf16[16,24,2048]{2,1,0:T(8,128)(2,1)S(1)} %maximum_select_fusion.1, bf16[16,24,2048]{2,1,0:T(8,128)(2,1)S(1)} %bitcast.39, pred[]{:T(512)S(6)} %eq.56), kind=kLoop, calls=%fused_computation.3 | loop fusion | flops 14155776 | bytes 6291457 | tf_op jit(solution)/shard_map/jit(_where)/select_n | solution.py:182
  103.7 11.5 %all-to-all-done = bf16[8,256,256]{2,1,0:T(8,128)(2,1)} async-done(((bf16[8,256,256]{2,1,0:T(8,128)(2,1)}), bf16[8,256,256]{2,1,0:T(8,128)(2,1)}, u32[]{:S(2)}, u32[]{:S(2)}) %all-to-all-start) | async-done | bytes 1048608 | tf_op jit(solution)/shard_map/all_to_all | solution.py:201
  115.2 1.4 reduce_sum.40
  117.6 39.0 %all-to-all-start.1 = ((bf16[16,48,256]{2,1,0:T(8,128)(2,1)}), bf16[16,48,256]{2,1,0:T(8,128)(2,1)S(1)}, u32[]{:S(2)}, u32[]{:S(2)}) async-start(bf16[16,48,256]{2,1,0:T(8,128)(2,1)} %pad_maximum_fusion), calls=%async_computation.1 | async-start | bytes 786432 | tf_op jit(solution)/shard_map/all_to_all | solution.py:217
  156.6 4.2 %fusion.23 = (bf16[768,256]{1,0:T(8,128)(2,1)}, f32[768,256]{1,0:T(8,128)}) fusion(bf16[768,2048]{1,0:T(8,128)(2,1)} %bitcast.40, bf16[2048,256]{1,0:T(8,128)(2,1)} %all-gather.2.cloned.1.call-done), kind=kOutput, calls=%fused_computation.55 | convolution fusion | flops 805502976 | bytes 5373952 | tf_op jit(solution)/shard_map/dot_general | solution.py:221
  160.8 2.9 %collective-permute-start.2 = (bf16[768,256]{1,0:T(8,128)(2,1)}, bf16[768,256]{1,0:T(8,128)(2,1)}, u32[]{:S(2)}, u32[]{:S(2)}) collective-permute-start(bf16[768,256]{1,0:T(8,128)(2,1)} %get-tuple-element.7), channel_id=1, source_target_pairs={{0,8},{1,9},{2,10},{3,11},{4,12},{5,13},{6,14},{7,15},{8,0},{9,1},... | collective-permute-start | bytes 1179656 | tf_op jit(solution)/shard_map/ppermute | solution.py:222
  166.8 1.4 convert_reduce_fusion.2
  168.2 1.3 copy.17
  170.9 4.6 %collective-permute-done.2 = bf16[768,256]{1,0:T(8,128)(2,1)} collective-permute-done((bf16[768,256]{1,0:T(8,128)(2,1)}, bf16[768,256]{1,0:T(8,128)(2,1)}, u32[]{:S(2)}, u32[]{:S(2)}) %collective-permute-start.2) | collective-permute-done | bytes 393248 | tf_op jit(solution)/shard_map/ppermute | solution.py:222
  175.5 3.3 %convolution_convert_fusion = bf16[2048,256]{1,0:T(8,128)(2,1)S(1)} fusion(bf16[768,2048]{1,0:T(8,128)(2,1)} %bitcast.41, bf16[768,256]{1,0:T(8,128)(2,1)S(1)} %bitcast.47, f32[768,256]{1,0:T(8,128)} %get-tuple-element.8, bf16[768,256]{1,0:T(8,128)(2,1)} %collective-permute-done.2, f32[768]{0:T(1024)} %div.37), kind=kOutput, calls=%fused_computation.4 | convolution fusion | flops 807010304 | bytes 5770240 | tf_op jit(solution)/shard_map/dot_general | solution.py:237
  178.9 30.2 %all_to_all.15 = bf16[8,256,256]{2,1,0:T(8,128)(2,1)S(1)} all-to-all(bf16[8,256,256]{2,1,0:T(8,128)(2,1)S(1)} %bitcast.44), channel_id=1, replica_groups={{0,1,2,3,4,5,6,7},{8,9,10,11,12,13,14,15},{16,17,18,19,20,21,22,23},{24..., dimensions={0} | all-to-all | bytes 2097152 | tf_op jit(solution)/shard_map/all_to_all | solution.py:240
  209.2 1.3 collective-permute-start.13
  210.5 5.1 %collective-permute-done.13 = f32[256,256]{1,0:T(8,128)} collective-permute-done((f32[256,256]{1,0:T(8,128)S(1)}, f32[256,256]{1,0:T(8,128)}, u32[]{:S(2)}, u32[]{:S(2)}) %collective-permute-start.13) | collective-permute-done | bytes 262176 | tf_op jit(solution)/shard_map/ppermute | solution.py:249
  215.6 1.8 maximum_select_fusion.2
  (61 shorter events, 17.8 us)
Async XLA Ops:
  6.5 3.3 %copy-start = (bf16[384,4096]{1,0:T(8,128)(2,1)S(1)}, bf16[384,4096]{1,0:T(8,128)(2,1)}, u32[]{:S(2)}) copy-start(bf16[384,4096]{1,0:T(8,128)(2,1)} %param.12) | copy-start | bytes 9437188
  6.5 11.7 %copy-start.3 = (bf16[1,256,256]{2,1,0:T(8,128)(2,1)S(1)}, bf16[1,256,256]{2,1,0:T(8,128)(2,1)}, u32[]{:S(2)}) copy-start(bf16[1,256,256]{2,1,0:T(8,128)(2,1)} %param.8) | copy-start | bytes 393220
  6.5 150.1 %all-gather.2.cloned.1.call-start = ((), (), s32[]{:S(2)}) async-start(), calls=%async_computation.3 | async-start | bytes 1179648 | tf_op jit(solution)/shard_map/all_gather | solution.py:163
  9.1 5.4 %collective-permute-start.3 = (bf16[272,256]{1,0:T(8,128)(2,1)}, bf16[272,256]{1,0:T(8,128)(2,1)S(1)}, u32[]{:S(2)}, u32[]{:S(2)}) collective-permute-start(bf16[272,256]{1,0:T(8,128)(2,1)} %pad_maximum_fusion.2), channel_id=1, source_target_pairs={{0,8},{1,9},{2,10},{3,11},{4,12},{5,13},{6,14},{7,15},{16,24},{17,... | collective-permute-start | bytes 417800 | tf_op jit(solution)/shard_map/ppermute | solution.py:126
  10.8 41.9 %collective-permute-start = (bf16[384,1024]{1,0:T(8,128)(2,1)}, bf16[384,1024]{1,0:T(8,128)(2,1)}, u32[]{:S(2)}, u32[]{:S(2)}) collective-permute-start(bf16[384,1024]{1,0:T(8,128)(2,1)} %constant_dynamic-slice_fusion.2), channel_id=1, source_target_pairs={{0,8},{1,9},{2,10},{3,11},{4,12},{5,13},{6,14},{7,15},{8,0},{9,1},... | collective-permute-start | bytes 2359304 | tf_op jit(solution)/shard_map/ppermute | solution.py:172
  15.5 4.0 %collective-permute-start.4 = (bf16[544,256]{1,0:T(8,128)(2,1)S(1)}, bf16[544,256]{1,0:T(8,128)(2,1)}, u32[]{:S(2)}, u32[]{:S(2)}) collective-permute-start(bf16[544,256]{1,0:T(8,128)(2,1)S(1)} %pad_maximum_fusion.1), channel_id=1, source_target_pairs={{0,1},{1,2},{2,3},{3,4},{4,5},{5,6},{6,7},{7,0},{8,9},{9,10},{10,1... | collective-permute-start | bytes 835592 | tf_op jit(solution)/shard_map/ppermute | solution.py:131
  16.9 4.0 %collective-permute-start.5 = (bf16[544,256]{1,0:T(8,128)(2,1)S(1)}, bf16[544,256]{1,0:T(8,128)(2,1)}, u32[]{:S(2)}, u32[]{:S(2)}) collective-permute-start(bf16[544,256]{1,0:T(8,128)(2,1)S(1)} %pad_maximum_fusion.1), channel_id=1, source_target_pairs={{0,7},{1,0},{2,1},{3,2},{4,3},{5,4},{6,5},{7,6},{8,15},{9,8},{10,9... | collective-permute-start | bytes 835592 | tf_op jit(solution)/shard_map/ppermute | solution.py:132
  19.5 5.4 %collective-permute-start.6 = (bf16[544,256]{1,0:T(8,128)(2,1)}, bf16[544,256]{1,0:T(8,128)(2,1)}, u32[]{:S(2)}, u32[]{:S(2)}) collective-permute-start(bf16[544,256]{1,0:T(8,128)(2,1)} %collective-permute-done.4), channel_id=1, source_target_pairs={{0,1},{1,2},{2,3},{3,4},{4,5},{5,6},{6,7},{7,0},{8,9},{9,10},{10,1... | collective-permute-start | bytes 835592 | tf_op jit(solution)/shard_map/ppermute | solution.py:131
  20.9 4.7 %collective-permute-start.7 = (bf16[544,256]{1,0:T(8,128)(2,1)}, bf16[544,256]{1,0:T(8,128)(2,1)}, u32[]{:S(2)}, u32[]{:S(2)}) collective-permute-start(bf16[544,256]{1,0:T(8,128)(2,1)} %collective-permute-done.5), channel_id=1, source_target_pairs={{0,7},{1,0},{2,1},{3,2},{4,3},{5,4},{6,5},{7,6},{8,15},{9,8},{10,9... | collective-permute-start | bytes 835592 | tf_op jit(solution)/shard_map/ppermute | solution.py:132
  23.1 12.4 %copy-start.2 = (bf16[1,256,1024]{2,1,0:T(8,128)(2,1)S(1)}, bf16[1,256,1024]{2,1,0:T(8,128)(2,1)}, u32[]{:S(2)}) copy-start(bf16[1,256,1024]{2,1,0:T(8,128)(2,1)} %param.7) | copy-start | bytes 1572868
  24.9 6.4 %collective-permute-start.8 = (bf16[544,256]{1,0:T(8,128)(2,1)}, bf16[544,256]{1,0:T(8,128)(2,1)S(1)}, u32[]{:S(2)}, u32[]{:S(2)}) collective-permute-start(bf16[544,256]{1,0:T(8,128)(2,1)} %collective-permute-done.6), channel_id=1, source_target_pairs={{0,1},{1,2},{2,3},{3,4},{4,5},{5,6},{6,7},{7,0},{8,9},{9,10},{10,1... | collective-permute-start | bytes 835592 | tf_op jit(solution)/shard_map/ppermute | solution.py:131
  25.5 6.5 %collective-permute-start.9 = (bf16[544,256]{1,0:T(8,128)(2,1)}, bf16[544,256]{1,0:T(8,128)(2,1)S(1)}, u32[]{:S(2)}, u32[]{:S(2)}) collective-permute-start(bf16[544,256]{1,0:T(8,128)(2,1)} %collective-permute-done.7), channel_id=1, source_target_pairs={{0,7},{1,0},{2,1},{3,2},{4,3},{5,4},{6,5},{7,6},{8,15},{9,8},{10,9... | collective-permute-start | bytes 835592 | tf_op jit(solution)/shard_map/ppermute | solution.py:132
  31.3 2.8 %collective-permute-start.10 = (bf16[272,256]{1,0:T(8,128)(2,1)S(1)}, bf16[272,256]{1,0:T(8,128)(2,1)S(1)}, u32[]{:S(2)}, u32[]{:S(2)}) collective-permute-start(bf16[272,256]{1,0:T(8,128)(2,1)S(1)} %slice.8), channel_id=1, source_target_pairs={{0,1},{1,2},{2,3},{3,4},{4,5},{5,6},{6,7},{7,0},{8,9},{9,10},{10,1... | collective-permute-start | bytes 417800 | tf_op jit(solution)/shard_map/ppermute | solution.py:134
  32.0 2.8 %collective-permute-start.11 = (bf16[272,256]{1,0:T(8,128)(2,1)S(1)}, bf16[272,256]{1,0:T(8,128)(2,1)S(1)}, u32[]{:S(2)}, u32[]{:S(2)}) collective-permute-start(bf16[272,256]{1,0:T(8,128)(2,1)S(1)} %slice.9), channel_id=1, source_target_pairs={{0,7},{1,0},{2,1},{3,2},{4,3},{5,4},{6,5},{7,6},{8,15},{9,8},{10,9... | collective-permute-start | bytes 417800 | tf_op jit(solution)/shard_map/ppermute | solution.py:135
  35.5 1.6 copy-start.1
  37.1 2.7 %copy-start.4 = (bf16[256,512]{1,0:T(8,128)(2,1)S(1)}, bf16[256,512]{1,0:T(8,128)(2,1)}, u32[]{:S(2)}) copy-start(bf16[256,512]{1,0:T(8,128)(2,1)} %param.13) | copy-start | bytes 786436
  38.5 51.3 %collective-permute-start.12 = (bf16[256,1024]{1,0:T(8,128)(2,1)}, bf16[256,1024]{1,0:T(8,128)(2,1)}, u32[]{:S(2)}, u32[]{:S(2)}) collective-permute-start(bf16[256,1024]{1,0:T(8,128)(2,1)} %attend.1), channel_id=1, source_target_pairs={{0,128},{1,129},{2,130},{3,131},{4,132},{5,133},{6,134},{7,135},{8... | collective-permute-start | bytes 1572872 | tf_op jit(solution)/shard_map/ppermute | solution.py:191
  40.5 12.0 %copy-start.5 = (s32[4096,1]{0,1:T(1,128)S(1)}, s32[4096,1]{0,1:T(1,128)}, u32[]{:S(2)}) copy-start(s32[4096,1]{0,1:T(1,128)} %param.11) | copy-start | bytes 49156
  52.7 46.2 %collective-permute-start.1 = (bf16[384,1024]{1,0:T(8,128)(2,1)}, bf16[384,1024]{1,0:T(8,128)(2,1)}, u32[]{:S(2)}, u32[]{:S(2)}) collective-permute-start(bf16[384,1024]{1,0:T(8,128)(2,1)} %collective-permute-done), channel_id=1, source_target_pairs={{0,128},{128,0},{1,129},{129,1},{2,130},{130,2},{3,131},{131,3},{4... | collective-permute-start | bytes 2359304 | tf_op jit(solution)/shard_map/ppermute | solution.py:173
  94.4 20.9 %all-to-all-start = ((bf16[8,256,256]{2,1,0:T(8,128)(2,1)}), bf16[8,256,256]{2,1,0:T(8,128)(2,1)}, u32[]{:S(2)}, u32[]{:S(2)}) async-start(bf16[8,256,256]{2,1,0:T(8,128)(2,1)} %fusion.6), calls=%async_computation | async-start | bytes 2097152 | tf_op jit(solution)/shard_map/all_to_all | solution.py:201
  117.6 57.9 %all-to-all-start.1 = ((bf16[16,48,256]{2,1,0:T(8,128)(2,1)}), bf16[16,48,256]{2,1,0:T(8,128)(2,1)S(1)}, u32[]{:S(2)}, u32[]{:S(2)}) async-start(bf16[16,48,256]{2,1,0:T(8,128)(2,1)} %pad_maximum_fusion), calls=%async_computation.1 | async-start | bytes 786432 | tf_op jit(solution)/shard_map/all_to_all | solution.py:217
  160.8 14.7 %collective-permute-start.2 = (bf16[768,256]{1,0:T(8,128)(2,1)}, bf16[768,256]{1,0:T(8,128)(2,1)}, u32[]{:S(2)}, u32[]{:S(2)}) collective-permute-start(bf16[768,256]{1,0:T(8,128)(2,1)} %get-tuple-element.7), channel_id=1, source_target_pairs={{0,8},{1,9},{2,10},{3,11},{4,12},{5,13},{6,14},{7,15},{8,0},{9,1},... | collective-permute-start | bytes 1179656 | tf_op jit(solution)/shard_map/ppermute | solution.py:222
  209.2 6.4 %collective-permute-start.13 = (f32[256,256]{1,0:T(8,128)S(1)}, f32[256,256]{1,0:T(8,128)}, u32[]{:S(2)}, u32[]{:S(2)}) collective-permute-start(f32[256,256]{1,0:T(8,128)S(1)} %convert_reduce_fusion), channel_id=1, source_target_pairs={{0,128},{1,129},{2,130},{3,131},{4,132},{5,133},{6,134},{7,135},{8... | collective-permute-start | bytes 786440 | tf_op jit(solution)/shard_map/ppermute | solution.py:249
Sparse Core Ops, SparseCore 0:
  40.6 101.1 all-gather.1

commit v2 on v1

v2 whole, which is shorter than its diff:
```python
import functools

import jax
import jax.numpy as jnp
from jax import lax
from jax.experimental import pallas as pl
from jax.experimental.pallas import tpu as pltpu
from jax.sharding import PartitionSpec as P

HD = 128
ZN = 8
WINDOW = 9
PIECE = 272
LOW = -1e30


def ring_pairs(step, base, reps):
    return [
        (base + rep * ZN + z, base + rep * ZN + (z + step) % ZN)
        for rep in range(reps)
        for z in range(ZN)
    ]


def partner_pairs(base):
    return [(base + i, base + (i + ZN) % (2 * ZN)) for i in range(2 * ZN)]


def attention_kernel(info, query, seg_query, *refs):
    parts = refs[:9]
    out, kept, ids, scores, acc, top = refs[9:]
    shard = info[0]
    core = info[1]
    tok = query.shape[0]
    heads = query.shape[1] // HD
    high = shard // ZN
    ring = lax.rem(shard, ZN)
    scale = (HD**-0.5) * 1.4426950408889634
    seg_q = seg_query[...]
    first_seg = seg_q[0:1, :][0, 0]
    away = 1 - 2 * core

    count = jnp.int32(0)
    for index in range(16):
        place = index // 2 if index < 14 else index - 7
        ref = parts[place]
        start = (index % 2) * PIECE if index < 14 else 0
        dist = (place + 1) // 2 if index < 14 else 4
        if index < 14:
            other = jnp.int32(index % 2)
            step = -dist * away if place % 2 == 1 else dist * away
        else:
            other = core if index == 14 else 1 - core
            step = 4
        source = lax.rem(ring + step + ZN, ZN)
        block = (high + other - 2 * high * other) * ZN + source
        last_seg = ref[start + 256 : start + 272, 128:256].astype(jnp.float32)[0:1, 127:128][0, 0]
        wanted = (block <= shard) & (block >= shard - WINDOW) & (last_seg >= first_seg)

        @pl.when(wanted)
        def _(ref=ref, start=start, block=block, count=count):
            kept[count] = ref[start : start + PIECE, :]
            ids[count] = block

        count = count + wanted.astype(jnp.int32)

    top[...] = jnp.full_like(top, LOW)
    acc[...] = jnp.zeros_like(acc)

    def score_block(index, carry):
        keys = kept[index, 0:256, 0:HD]
        seg_k = kept[index, 256:272, :].astype(jnp.float32)[0:1, :]
        rows = lax.broadcasted_iota(jnp.int32, (tok, 256), 0) + shard * tok
        cols = lax.broadcasted_iota(jnp.int32, (tok, 256), 1) + ids[index] * 256
        allowed = (seg_k == seg_q) & (cols <= rows)
        for head in range(heads):
            found = lax.dot_general(
                query[:, head * HD : (head + 1) * HD],
                keys,
                (((1,), (1,)), ((), ())),
                preferred_element_type=jnp.float32,
            )
            found = jnp.where(allowed, found, LOW)
            scores[index, head] = found
            top[head] = jnp.maximum(top[head], jnp.maximum(found[:, :HD], found[:, HD:]))
        return carry

    lax.fori_loop(0, count, score_block, 0)
    for head in range(heads):
        best = jnp.max(top[head], axis=1, keepdims=True)
        top[head] = jnp.broadcast_to(best, (tok, HD))

    def mix_block(index, carry):
        values = kept[index, 0:256, HD : 2 * HD]
        values = jnp.concatenate([values, jnp.ones_like(values)], axis=1)
        for head in range(heads):
            best = top[head]
            shifted = scores[index, head] - jnp.concatenate([best, best], axis=1)
            weights = jnp.exp2(shifted * scale).astype(jnp.bfloat16)
            acc[head] += jnp.dot(weights, values, preferred_element_type=jnp.float32)
        return carry

    lax.fori_loop(0, count, mix_block, 0)
    for head in range(heads):
        mixed = acc[head]
        out[:, head * HD : (head + 1) * HD] = (mixed[:, :HD] / mixed[:, HD:]).astype(jnp.bfloat16)


def attend(info, query, seg_query, parts):
    tok, width = query.shape
    heads = width // HD
    vmem = pl.BlockSpec(memory_space=pltpu.VMEM)
    return pl.pallas_call(
        attention_kernel,
        out_shape=jax.ShapeDtypeStruct((tok, width), jnp.bfloat16),
        in_specs=[pl.BlockSpec(memory_space=pltpu.SMEM)] + [vmem] * (2 + len(parts)),
        out_specs=vmem,
        scratch_shapes=[
            pltpu.VMEM((16, PIECE, 2 * HD), jnp.bfloat16),
            pltpu.SMEM((16,), jnp.int32),
            pltpu.VMEM((16, heads, tok, 256), jnp.float32),
            pltpu.VMEM((heads, tok, 2 * HD), jnp.float32),
            pltpu.VMEM((heads, tok, HD), jnp.float32),
        ],
        compiler_params=pltpu.CompilerParams(vmem_limit_bytes=40 * 1024 * 1024),
        cost_estimate=pl.CostEstimate(
            flops=8 * tok * width * 2560,
            bytes_accessed=4 << 20,
            transcendentals=tok * heads * 2560,
        ),
        name="attend",
    )(info, query, seg_query, *parts)


def project_kernel(core, context, weight, out):
    out[0] = jnp.dot(context[...], weight[...], preferred_element_type=jnp.float32).astype(
        jnp.bfloat16
    )


def project(core, context, projector, tensor_n):
    tok, width = context.shape
    feats = projector.shape[1] // (2 * tensor_n)
    return pl.pallas_call(
        project_kernel,
        out_shape=jax.ShapeDtypeStruct((tensor_n, tok, feats), jnp.bfloat16),
        grid_spec=pltpu.PrefetchScalarGridSpec(
            num_scalar_prefetch=1,
            grid=(tensor_n,),
            in_specs=[
                pl.BlockSpec((tok, width), lambda i, core: (0, 0)),
                pl.BlockSpec((width, feats), lambda i, core: (0, 2 * i + core[0])),
            ],
            out_specs=pl.BlockSpec((1, tok, feats), lambda i, core: (i, 0, 0)),
        ),
        compiler_params=pltpu.CompilerParams(vmem_limit_bytes=16 * 1024 * 1024),
        cost_estimate=pl.CostEstimate(
            flops=2 * tok * width * feats * tensor_n,
            bytes_accessed=2 * width * feats * tensor_n,
            transcendentals=0,
        ),
        name="project",
    )(core, context, projector)


def gather_keyval(group, keyval, query, segments):
    both = ("group", "seq")
    tok, width = query.shape
    seg_row = jnp.broadcast_to(segments.astype(jnp.bfloat16)[None, :], (16, segments.shape[0]))
    own = jnp.concatenate([keyval, seg_row], axis=0)
    lower = lax.ppermute(own, both, [(z, ZN + z) for z in range(ZN)])
    own = jnp.where(group == 0, own, lax.ppermute(own, "group", [(0, 1)]))
    other_query = lax.ppermute(query[:, width // 2 :], "group", [(0, 1)])
    query = jnp.where(group == 0, query[:, : width // 2], other_query)
    lower = jnp.where(group == 0, lower, lax.ppermute(lower, "group", [(0, 1)]))
    moving = jnp.concatenate([own, lower], axis=0)
    pairs = ring_pairs(1, 0, 2) + ring_pairs(-1, 2 * ZN, 2)
    swap = [(0, 1), (1, 0)]
    found = [moving]
    for _ in range(3):
        moving = lax.ppermute(moving, both, pairs)
        found += [moving, lax.ppermute(moving, "group", swap)]
    moving = jnp.where(group == 0, moving[:PIECE], moving[PIECE:])
    moving = lax.ppermute(moving, both, pairs)
    found += [moving, lax.ppermute(moving, "group", swap)]
    return query, found


def shards(
    teacher_query,
    teacher_keyval,
    segment_ids,
    projector,
    owner_table,
    student_context,
    student_out_weight,
):
    group = lax.axis_index("group")
    seq = lax.axis_index("seq")
    high = seq // ZN
    ring = seq % ZN
    query = teacher_query[0]
    tok = query.shape[0]
    slots, model = student_context.shape
    owners_n = 2 * ZN
    capacity = slots // owners_n
    half = model // 2
    feats = student_out_weight.shape[1] // 2
    tensor_n = model // (2 * feats)
    z_groups = [[h * ZN + z for z in range(ZN)] for h in range(2)]

    weight = lax.dynamic_slice_in_dim(student_out_weight, group * feats, feats, axis=1)
    weight, keyval = lax.optimization_barrier((weight, teacher_keyval[0]))
    weight = lax.all_gather(weight, "seq", axis=0, tiled=True, axis_index_groups=z_groups)

    query, parts = gather_keyval(group, keyval, query, segment_ids)

    sent = lax.dynamic_slice_in_dim(
        student_context, (1 - high) * half + group * (half // 2), half // 2, axis=1
    )
    core_swap = [(0, 1), (1, 0)]
    all_pairs = partner_pairs(0) + partner_pairs(owners_n)
    came = lax.ppermute(sent, ("group", "seq"), all_pairs)
    came_other = lax.ppermute(came, "group", core_swap)
    theirs = jnp.where(
        group == 0,
        jnp.concatenate([came, came_other], axis=1),
        jnp.concatenate([came_other, came], axis=1),
    )
    ours = lax.dynamic_slice_in_dim(student_context, high * half, half, axis=1)
    ours = ours.reshape(owners_n, capacity, half)
    theirs = theirs.reshape(owners_n, capacity, half)
    rows = jnp.where(
        high == 0,
        jnp.concatenate([ours, theirs], axis=1),
        jnp.concatenate([theirs, ours], axis=1),
    ).reshape(2 * slots, half)

    info = jnp.stack([seq, group]).astype(jnp.int32)
    seg_query = segment_ids.astype(jnp.float32)[:, None]
    context = attend(info, query, seg_query, parts)

    owners_all = owner_table[:, 0]
    owners = lax.dynamic_slice_in_dim(owners_all, seq * tok, tok)
    index = jnp.arange(tok, dtype=jnp.int32)
    ranks = jnp.sum(
        ((owners[:, None] == owners[None, :]) & (index[None, :] < index[:, None])).astype(
            jnp.int32
        ),
        axis=1,
    )
    place = (owners % ZN) * (2 * capacity) + (owners // ZN) * capacity + ranks
    route = (jnp.arange(slots, dtype=jnp.int32)[:, None] == place[None, :]).astype(jnp.bfloat16)
    pair_owners = jnp.stack([ring, ring + ZN])
    counts = jnp.sum(
        (owners_all.reshape(owners_n, tok, 1) == pair_owners[None, None, :]).astype(jnp.int32),
        axis=1,
    )
    live = (jnp.arange(capacity, dtype=jnp.int32)[None, None, :] < counts[:, :, None]).reshape(
        2 * slots
    )
    scale = live.astype(jnp.float32)[:, None] / tok
    context, route, scale = lax.optimization_barrier((context, route, scale))

    other_context = lax.ppermute(context, "group", core_swap)
    context = jnp.where(
        group == 0,
        jnp.concatenate([context, other_context], axis=1),
        jnp.concatenate([other_context, context], axis=1),
    )
    partial = project(group[None].astype(jnp.int32), context, projector, tensor_n)
    partial = lax.all_to_all(partial, "tensor", split_axis=0, concat_axis=0, tiled=True)
    target = jnp.sum(partial.astype(jnp.float32), axis=0).astype(jnp.bfloat16)

    output = jnp.dot(rows, weight, preferred_element_type=jnp.float32)
    output = output + lax.ppermute(
        output.astype(jnp.bfloat16), ("group", "seq"), all_pairs
    ).astype(jnp.float32)

    output, target = lax.optimization_barrier((output, target))

    routed = jnp.dot(route, target, preferred_element_type=jnp.float32).astype(jnp.bfloat16)
    routed = routed.reshape(ZN, 2 * capacity, feats)
    routed = lax.all_to_all(
        jnp.concatenate([routed, routed], axis=0), "seq", split_axis=0, concat_axis=0, tiled=True
    ).reshape(2 * slots, feats)

    residual = ((output - routed.astype(jnp.float32)) * scale).astype(jnp.bfloat16)

    gradient = lax.dot_general(
        rows, residual, (((0,), (0,)), ((), ())), preferred_element_type=jnp.float32
    ).astype(jnp.bfloat16)
    gradient = lax.all_to_all(
        gradient.reshape(ZN, half // ZN, feats),
        "seq",
        split_axis=0,
        concat_axis=0,
        tiled=True,
        axis_index_groups=z_groups,
    )
    gradient = jnp.sum(gradient.astype(jnp.float32), axis=0)
    passed = lax.ppermute(gradient, "group", [(0, 1)])
    whole = jnp.concatenate([passed, gradient], axis=1)
    return jnp.where(group == 1, whole, 0.0)[None]


def solution(mesh):
    placed = (
        P("group", "seq", "tensor"),
        P("group", "seq", "tensor"),
        P("seq"),
        P("tensor", None),
        P(),
        P("seq", None),
        P("seq", "tensor"),
    )
    return jax.shard_map(
        shards, mesh=mesh, in_specs=placed, out_specs=P("group", "seq", "tensor"), check_vma=False
    )
```

time: 227 us -> 184 us (0.81)
  starting transfers between devices: 98.3 us -> 47.8 us
  waiting for transfers between devices: 21.3 us -> 46.3 us
  local copies, waits for them, and re-layouts: 30.3 us -> 11.8 us
  Pallas kernels: 1.37 us -> 7.37 us
  matrix products: 12.4 us -> 6.59 us
    ppermute x1, starting transfers between devices: 37.1 us -> 1.57 us  [shards(): came_other = lax.ppermute(came, 'group', core_swap)]
    all_to_all x1, starting transfers between devices: 39 us -> 3.55 us  [shards(): lax.all_to_all(jnp.concatenate([routed, routed], axis=0), 'seq', split_ax...]
    unnamed x24 -> x23, local copies, waits for them, and re-layouts: 25 us -> 3.08 us
    ppermute x9 -> x12, starting transfers between devices: 9.45 us -> 25.2 us  [the longest x4 15.8 us: gather_keyval(): moving = lax.ppermute(moving, both, pairs)]
    ppermute x1, waiting for transfers between devices: 4.58 us -> 17.2 us  [shards(): lax.ppermute(output.astype(jnp.bfloat16), ('group', 'seq'), all_pairs)]
    all_to_all x1, waiting for transfers between devices: 0.01 us -> 12.2 us  [shards(): lax.all_to_all(jnp.concatenate([routed, routed], axis=0), 'seq', split_ax...]
    ppermute x9 -> x12, waiting for transfers between devices: 0.02 us -> 11.7 us  [the longest x4 8.77 us: gather_keyval(): moving = lax.ppermute(moving, both, pairs)]
    all_to_all x1, waiting for transfers between devices: 11.5 us -> 0.01 us  [shards(): lax.all_to_all(partial, 'tensor', split_axis=0, concat_axis=0, tiled=True)]
  transfers between devices with their start and end apart: 17 -> 20, of which waited for: 3 -> 8; matrix products, arithmetic and copies ran while one was open for 22% -> 12% of each run, Pallas kernels for 1% -> 4%
where the time goes in v2:
time: 184 us; the launch traced here: 183 us
  starting transfers between devices  47.8 us (26%)
  waiting for transfers between devices  46.3 us (25%)
  blocking collectives  30.3 us (16%)
  other arithmetic  18.9 us (10%)
  between operations  13.8 us (8%)
  local copies, waits for them, and re-layouts  11.8 us (6%)
  Pallas kernels  7.37 us (4%)
  matrix products  6.59 us (4%)
    all_to_all x1, blocking collectives, shards(): lax.all_to_all(gradient.reshape(ZN, half // ZN, feats), 'seq', split_axis...  30.3 us
    ppermute x1, waiting for transfers between devices, shards(): lax.ppermute(output.astype(jnp.bfloat16), ('group', 'seq'), all_pairs)  17.2 us
    ppermute x4, starting transfers between devices, gather_keyval(): moving = lax.ppermute(moving, both, pairs)  15.8 us
    all_to_all x1, waiting for transfers between devices, shards(): lax.all_to_all(jnp.concatenate([routed, routed], axis=0), 'seq', split_ax...  12.2 us
    ppermute x4, waiting for transfers between devices, gather_keyval(): moving = lax.ppermute(moving, both, pairs)  8.77 us
    ppermute x1, starting transfers between devices, shards(): lax.ppermute(output.astype(jnp.bfloat16), ('group', 'seq'), all_pairs)  7.39 us
    ppermute x1, waiting for transfers between devices, shards(): passed = lax.ppermute(gradient, 'group', [(0, 1)])  5.15 us
    ppermute x4, starting transfers between devices, gather_keyval(): found += [moving, lax.ppermute(moving, 'group', swap)]  5.12 us
  transfers between devices with their start and end apart: 20, of which 8 were waited for; matrix products, arithmetic and copies ran while one was open for 12% of the time, Pallas kernels for 4%

profile of v2, /device:TPU:1, one launch (start us, length us, event | category | flops | bytes accessed | tf_op | source)
XLA Modules:
  0.0 182.8 jit_solution(4891413531949850100)
XLA Ops:
  6.5 1.7 constant_dynamic-slice_fusion.1
  9.6 1.6 pad_maximum_fusion.2
  13.1 1.7 slice.17
  17.1 3.7 %collective-permute-start = (bf16[384,1024]{1,0:T(8,128)(2,1)}, bf16[384,1024]{1,0:T(8,128)(2,1)}, u32[]{:S(2)}, u32[]{:S(2)}) collective-permute-start(bf16[384,1024]{1,0:T(8,128)(2,1)} %constant_dynamic-slice_fusion.2), channel_id=1, source_target_pairs={{0,8},{1,9},{2,10},{3,11},{4,12},{5,13},{6,14},{7,15},{8,0},{9,1},... | collective-permute-start | bytes 2359304 | tf_op jit(solution)/shard_map/ppermute | solution.py:223
  23.8 2.7 %collective-permute-done.6 = bf16[272,256]{1,0:T(8,128)(2,1)S(1)} collective-permute-done((bf16[272,256]{1,0:T(8,128)(2,1)S(1)}, bf16[272,256]{1,0:T(8,128)(2,1)S(1)}, u32[]{:S(2)}, u32[]{:S(2)}) %collective-permute-start.6) | collective-permute-done | bytes 139296 | tf_op jit(solution)/shard_map/ppermute | solution.py:175
  26.6 5.7 %collective-permute-start.7 = (bf16[544,256]{1,0:T(8,128)(2,1)S(1)}, bf16[544,256]{1,0:T(8,128)(2,1)}, u32[]{:S(2)}, u32[]{:S(2)}) collective-permute-start(bf16[544,256]{1,0:T(8,128)(2,1)S(1)} %pad_maximum_fusion.1.refs_0_), channel_id=1, source_target_pairs={{0,1},{1,2},{2,3},{3,4},{4,5},{5,6},{6,7},{7,0},{8,9},{9,10},{10,1... | collective-permute-start | bytes 835592 | tf_op jit(solution)/shard_map/ppermute | solution.py:181
  32.5 3.3 %collective-permute-done.7.refs_1_ = bf16[544,256]{1,0:T(8,128)(2,1)} collective-permute-done((bf16[544,256]{1,0:T(8,128)(2,1)S(1)}, bf16[544,256]{1,0:T(8,128)(2,1)}, u32[]{:S(2)}, u32[]{:S(2)}) %collective-permute-start.7) | collective-permute-done | bytes 278560 | tf_op jit(solution)/shard_map/ppermute | solution.py:181
  35.8 3.5 %collective-permute-start.9 = (bf16[544,256]{1,0:T(8,128)(2,1)}, bf16[544,256]{1,0:T(8,128)(2,1)}, u32[]{:S(2)}, u32[]{:S(2)}) collective-permute-start(bf16[544,256]{1,0:T(8,128)(2,1)} %collective-permute-done.7.refs_1_), channel_id=1, source_target_pairs={{0,1},{1,2},{2,3},{3,4},{4,5},{5,6},{6,7},{7,0},{8,9},{9,10},{10,1... | collective-permute-start | bytes 835592 | tf_op jit(solution)/shard_map/ppermute | solution.py:181
  41.2 2.0 %collective-permute-done.9.refs_3_ = bf16[544,256]{1,0:T(8,128)(2,1)} collective-permute-done((bf16[544,256]{1,0:T(8,128)(2,1)}, bf16[544,256]{1,0:T(8,128)(2,1)}, u32[]{:S(2)}, u32[]{:S(2)}) %collective-permute-start.9) | collective-permute-done | bytes 278560 | tf_op jit(solution)/shard_map/ppermute | solution.py:181
  43.3 3.1 %collective-permute-start.11 = (bf16[544,256]{1,0:T(8,128)(2,1)}, bf16[544,256]{1,0:T(8,128)(2,1)S(1)}, u32[]{:S(2)}, u32[]{:S(2)}) collective-permute-start(bf16[544,256]{1,0:T(8,128)(2,1)} %collective-permute-done.9.refs_3_), channel_id=1, source_target_pairs={{0,1},{1,2},{2,3},{3,4},{4,5},{5,6},{6,7},{7,0},{8,9},{9,10},{10,1... | collective-permute-start | bytes 835592 | tf_op jit(solution)/shard_map/ppermute | solution.py:181
  46.7 1.4 constant_dynamic-slice_fusion.3
  48.0 1.6 collective-permute-start.1
  49.6 3.5 %collective-permute-done.11.refs_5_ = bf16[544,256]{1,0:T(8,128)(2,1)S(1)} collective-permute-done((bf16[544,256]{1,0:T(8,128)(2,1)}, bf16[544,256]{1,0:T(8,128)(2,1)S(1)}, u32[]{:S(2)}, u32[]{:S(2)}) %collective-permute-start.11) | collective-permute-done | bytes 278560 | tf_op jit(solution)/shard_map/ppermute | solution.py:181
  53.7 3.5 %collective-permute-start.13 = (bf16[272,256]{1,0:T(8,128)(2,1)}, bf16[272,256]{1,0:T(8,128)(2,1)}, u32[]{:S(2)}, u32[]{:S(2)}) collective-permute-start(bf16[272,256]{1,0:T(8,128)(2,1)} %slice_select_fusion.1), channel_id=1, source_target_pairs={{0,1},{1,2},{2,3},{3,4},{4,5},{5,6},{6,7},{7,0},{8,9},{9,10},{10,1... | collective-permute-start | bytes 417800 | tf_op jit(solution)/shard_map/ppermute | solution.py:184
  57.9 1.8 %collective-permute-start.8 = (bf16[544,256]{1,0:T(8,128)(2,1)}, bf16[544,256]{1,0:T(8,128)(2,1)}, u32[]{:S(2)}, u32[]{:S(2)}) collective-permute-start(bf16[544,256]{1,0:T(8,128)(2,1)} %collective-permute-done.7.refs_1_), channel_id=1, source_target_pairs={{0,128},{128,0},{1,129},{129,1},{2,130},{130,2},{3,131},{131,3},{4... | collective-permute-start | bytes 835592 | tf_op jit(solution)/shard_map/ppermute | solution.py:182
  61.6 1.4 div.37
  63.0 2.8 %collective-permute-start.14 = (bf16[272,256]{1,0:T(8,128)(2,1)}, bf16[272,256]{1,0:T(8,128)(2,1)S(1)}, u32[]{:S(2)}, u32[]{:S(2)}) collective-permute-start(bf16[272,256]{1,0:T(8,128)(2,1)} %collective-permute-done.13.refs_7_), channel_id=1, source_target_pairs={{0,128},{128,0},{1,129},{129,1},{2,130},{130,2},{3,131},{131,3},{4... | collective-permute-start | bytes 417800 | tf_op jit(solution)/shard_map/ppermute | solution.py:185
  68.6 4.2 %attend.1 = bf16[256,512]{1,0:T(8,128)(2,1)S(1)} custom-call(s32[2]{0:T(128)S(1)} %copy-done.4, bf16[256,512]{1,0:T(8,128)(2,1)S(1)} %slice_select_fusion.query, f32[256,1]{1,0:T(8,128)S(1)} %copy.9.seg_query, bf16[544,256]{1,0:T(8,128)(2,1)S(1)} %copy-done.3, bf16[544,256]{1,0:T(8,128)(2,1)} %collective-permute-done.7.refs_1_, ...), custom_call_target="tpu_custom_call" | custom-call | flops 2684354560 | bytes 4194304 | tf_op jit(solution)/shard_map/attend/pallas_call | solution.py:113
  73.3 2.7 %maximum_select_fusion.1 = bf16[16,24,2048]{2,1,0:T(8,128)(2,1)S(1)} fusion(bf16[16,24,1024]{2,1,0:T(8,128)(2,1)} %bitcast.2, bf16[16,24,1024]{2,1,0:T(8,128)(2,1)} %bitcast.1, pred[]{:T(512)S(6)} %eq.32), kind=kLoop, calls=%fused_computation.3 | loop fusion | flops 7077888 | bytes 3145729 | tf_op jit(solution)/shard_map/jit(_where)/select_n | solution.py:225
  75.9 2.4 %maximum_select_fusion = bf16[16,48,2048]{2,1,0:T(8,128)(2,1)} fusion(bf16[16,24,2048]{2,1,0:T(8,128)(2,1)S(1)} %maximum_select_fusion.1, bf16[16,24,2048]{2,1,0:T(8,128)(2,1)S(1)} %bitcast.26, pred[]{:T(512)S(6)} %eq.31), kind=kLoop, calls=%fused_computation | loop fusion | flops 14155776 | bytes 6291457 | tf_op jit(solution)/shard_map/jit(_where)/select_n | solution.py:233
  78.5 3.1 %project.1 = bf16[8,256,256]{2,1,0:T(8,128)(2,1)S(1)} custom-call(s32[1]{0:T(128)} %bitcast.5.core, bf16[256,1024]{1,0:T(8,128)(2,1)S(1)} %maximum_select_fusion.2.context, bf16[1024,4096]{1,0:T(8,128)(2,1)S(1)} %bitcast.25), custom_call_target="tpu_custom_call" | custom-call | flops 1073741824 | bytes 4194304 | tf_op jit(solution)/shard_map/project/pallas_call | solution.py:144
  82.6 4.4 %all-to-all-start = ((bf16[8,256,256]{2,1,0:T(8,128)(2,1)}), bf16[8,256,256]{2,1,0:T(8,128)(2,1)}, u32[]{:S(2)}, u32[]{:S(2)}) async-start(bf16[8,256,256]{2,1,0:T(8,128)(2,1)} %copy-done.1), calls=%async_computation | async-start | bytes 2097152 | tf_op jit(solution)/shard_map/all_to_all | solution.py:272
  87.1 3.2 %fusion.10 = (bf16[768,256]{1,0:T(8,128)(2,1)S(1)}, f32[768,256]{1,0:T(8,128)S(1)}) fusion(bf16[768,2048]{1,0:T(8,128)(2,1)} %bitcast.27, bf16[2048,256]{1,0:T(8,128)(2,1)} %all-gather.2.cloned.1.call-done), kind=kOutput, calls=%fused_computation.41 | convolution fusion | flops 805502976 | bytes 5373952 | tf_op jit(solution)/shard_map/dot_general | solution.py:275
  90.3 7.4 %collective-permute-start.2 = (bf16[768,256]{1,0:T(8,128)(2,1)S(1)}, bf16[768,256]{1,0:T(8,128)(2,1)S(1)}, u32[]{:S(2)}, u32[]{:S(2)}) collective-permute-start(bf16[768,256]{1,0:T(8,128)(2,1)S(1)} %get-tuple-element.21), channel_id=1, source_target_pairs={{0,8},{1,9},{2,10},{3,11},{4,12},{5,13},{6,14},{7,15},{8,0},{9,1},... | collective-permute-start | bytes 1179656 | tf_op jit(solution)/shard_map/ppermute | solution.py:276
  97.7 17.2 %collective-permute-done.2 = bf16[768,256]{1,0:T(8,128)(2,1)S(1)} collective-permute-done((bf16[768,256]{1,0:T(8,128)(2,1)S(1)}, bf16[768,256]{1,0:T(8,128)(2,1)S(1)}, u32[]{:S(2)}, u32[]{:S(2)}) %collective-permute-start.2) | collective-permute-done | bytes 393248 | tf_op jit(solution)/shard_map/ppermute | solution.py:276
  115.9 1.4 reduce_sum.41
  118.3 3.6 %all-to-all-start.1 = ((bf16[16,48,256]{2,1,0:T(8,128)(2,1)}), bf16[16,48,256]{2,1,0:T(8,128)(2,1)S(1)}, u32[]{:S(2)}, u32[]{:S(2)}) async-start(bf16[16,48,256]{2,1,0:T(8,128)(2,1)} %pad_maximum_fusion), calls=%async_computation.1 | async-start | bytes 786432 | tf_op jit(solution)/shard_map/all_to_all | solution.py:284
  121.9 12.2 %all-to-all-done.1 = bf16[16,48,256]{2,1,0:T(8,128)(2,1)S(1)} async-done(((bf16[16,48,256]{2,1,0:T(8,128)(2,1)}), bf16[16,48,256]{2,1,0:T(8,128)(2,1)S(1)}, u32[]{:S(2)}, u32[]{:S(2)}) %all-to-all-start.1) | async-done | bytes 393248 | tf_op jit(solution)/shard_map/all_to_all | solution.py:284
  134.0 3.2 %convolution_convert_fusion = bf16[2048,256]{1,0:T(8,128)(2,1)S(1)} fusion(bf16[768,2048]{1,0:T(8,128)(2,1)} %bitcast.28, f32[768,256]{1,0:T(8,128)} %convert_add_fusion, bf16[768,256]{1,0:T(8,128)(2,1)S(1)} %bitcast.36, f32[768]{0:T(1024)S(1)} %reduce.2), kind=kOutput, calls=%fused_computation.1 | convolution fusion | flops 806617088 | bytes 5377024 | tf_op jit(solution)/shard_map/dot_general | solution.py:290
  137.3 30.3 %all_to_all.15 = bf16[8,256,256]{2,1,0:T(8,128)(2,1)S(1)} all-to-all(bf16[8,256,256]{2,1,0:T(8,128)(2,1)S(1)} %bitcast.29), channel_id=1, replica_groups={{0,1,2,3,4,5,6,7},{8,9,10,11,12,13,14,15},{16,17,18,19,20,21,22,23},{24..., dimensions={0} | all-to-all | bytes 2097152 | tf_op jit(solution)/shard_map/all_to_all | solution.py:293
  169.0 5.2 %collective-permute-done.16 = f32[256,256]{1,0:T(8,128)} collective-permute-done((f32[256,256]{1,0:T(8,128)S(1)}, f32[256,256]{1,0:T(8,128)}, u32[]{:S(2)}, u32[]{:S(2)}) %collective-permute-start.16) | collective-permute-done | bytes 262176 | tf_op jit(solution)/shard_map/ppermute | solution.py:302
  174.1 1.8 maximum_select_fusion.3
  (73 shorter events, 21.9 us)
Async XLA Ops:
  6.5 9.6 %copy-start = (bf16[384,4096]{1,0:T(8,128)(2,1)S(1)}, bf16[384,4096]{1,0:T(8,128)(2,1)}, u32[]{:S(2)}) copy-start(bf16[384,4096]{1,0:T(8,128)(2,1)} %param.12) | copy-start | bytes 9437188
  6.5 33.3 %copy-start.7 = (s32[4096,1]{0,1:T(1,128)S(1)}, s32[4096,1]{0,1:T(1,128)}, u32[]{:S(2)}) copy-start(s32[4096,1]{0,1:T(1,128)} %param.11) | copy-start | bytes 49156
  6.5 80.5 %all-gather.2.cloned.1.call-start = ((), (), s32[]{:S(2)}) async-start(), calls=%async_computation.3 | async-start | bytes 1179648 | tf_op jit(solution)/shard_map/all_gather | solution.py:214
  11.2 10.4 %collective-permute-start.5 = (bf16[272,256]{1,0:T(8,128)(2,1)}, bf16[272,256]{1,0:T(8,128)(2,1)S(1)}, u32[]{:S(2)}, u32[]{:S(2)}) collective-permute-start(bf16[272,256]{1,0:T(8,128)(2,1)} %pad_maximum_fusion.2), channel_id=1, source_target_pairs={{0,8},{1,9},{2,10},{3,11},{4,12},{5,13},{6,14},{7,15},{16,24},{17,... | collective-permute-start | bytes 417800 | tf_op jit(solution)/shard_map/ppermute | solution.py:171
  11.8 11.0 %collective-permute-start.4 = (bf16[272,256]{1,0:T(8,128)(2,1)}, bf16[272,256]{1,0:T(8,128)(2,1)S(1)}, u32[]{:S(2)}, u32[]{:S(2)}) collective-permute-start(bf16[272,256]{1,0:T(8,128)(2,1)} %pad_maximum_fusion.2), channel_id=1, source_target_pairs={{0,128},{1,129},{2,130},{3,131},{4,132},{5,133},{6,134},{7,135},{8... | collective-permute-start | bytes 417800 | tf_op jit(solution)/shard_map/ppermute | solution.py:172
  14.8 44.9 %collective-permute-start.3 = (bf16[256,512]{1,0:T(8,128)(2,1)}, bf16[256,512]{1,0:T(8,128)(2,1)}, u32[]{:S(2)}, u32[]{:S(2)}) collective-permute-start(bf16[256,512]{1,0:T(8,128)(2,1)} %slice.17), channel_id=1, source_target_pairs={{0,128},{1,129},{2,130},{3,131},{4,132},{5,133},{6,134},{7,135},{8... | collective-permute-start | bytes 786440 | tf_op jit(solution)/shard_map/ppermute | solution.py:173
  17.1 30.9 %collective-permute-start = (bf16[384,1024]{1,0:T(8,128)(2,1)}, bf16[384,1024]{1,0:T(8,128)(2,1)}, u32[]{:S(2)}, u32[]{:S(2)}) collective-permute-start(bf16[384,1024]{1,0:T(8,128)(2,1)} %constant_dynamic-slice_fusion.2), channel_id=1, source_target_pairs={{0,8},{1,9},{2,10},{3,11},{4,12},{5,13},{6,14},{7,15},{8,0},{9,1},... | collective-permute-start | bytes 2359304 | tf_op jit(solution)/shard_map/ppermute | solution.py:223
  21.6 5.0 %collective-permute-start.6 = (bf16[272,256]{1,0:T(8,128)(2,1)S(1)}, bf16[272,256]{1,0:T(8,128)(2,1)S(1)}, u32[]{:S(2)}, u32[]{:S(2)}) collective-permute-start(bf16[272,256]{1,0:T(8,128)(2,1)S(1)} %collective-permute-done.5), channel_id=1, source_target_pairs={{0,128},{1,129},{2,130},{3,131},{4,132},{5,133},{6,134},{7,135},{8... | collective-permute-start | bytes 417800 | tf_op jit(solution)/shard_map/ppermute | solution.py:175
  26.6 14.6 %copy-start.2 = (bf16[544,256]{1,0:T(8,128)(2,1)}, bf16[544,256]{1,0:T(8,128)(2,1)S(1)}, u32[]{:S(2)}) copy-start(bf16[544,256]{1,0:T(8,128)(2,1)S(1)} %pad_maximum_fusion.1.refs_0_) | copy-start | bytes 835588
  26.6 9.1 %collective-permute-start.7 = (bf16[544,256]{1,0:T(8,128)(2,1)S(1)}, bf16[544,256]{1,0:T(8,128)(2,1)}, u32[]{:S(2)}, u32[]{:S(2)}) collective-permute-start(bf16[544,256]{1,0:T(8,128)(2,1)S(1)} %pad_maximum_fusion.1.refs_0_), channel_id=1, source_target_pairs={{0,1},{1,2},{2,3},{3,4},{4,5},{5,6},{6,7},{7,0},{8,9},{9,10},{10,1... | collective-permute-start | bytes 835592 | tf_op jit(solution)/shard_map/ppermute | solution.py:181
  35.8 7.5 %collective-permute-start.9 = (bf16[544,256]{1,0:T(8,128)(2,1)}, bf16[544,256]{1,0:T(8,128)(2,1)}, u32[]{:S(2)}, u32[]{:S(2)}) collective-permute-start(bf16[544,256]{1,0:T(8,128)(2,1)} %collective-permute-done.7.refs_1_), channel_id=1, source_target_pairs={{0,1},{1,2},{2,3},{3,4},{4,5},{5,6},{6,7},{7,0},{8,9},{9,10},{10,1... | collective-permute-start | bytes 835592 | tf_op jit(solution)/shard_map/ppermute | solution.py:181
  43.3 9.8 %collective-permute-start.11 = (bf16[544,256]{1,0:T(8,128)(2,1)}, bf16[544,256]{1,0:T(8,128)(2,1)S(1)}, u32[]{:S(2)}, u32[]{:S(2)}) collective-permute-start(bf16[544,256]{1,0:T(8,128)(2,1)} %collective-permute-done.9.refs_3_), channel_id=1, source_target_pairs={{0,1},{1,2},{2,3},{3,4},{4,5},{5,6},{6,7},{7,0},{8,9},{9,10},{10,1... | collective-permute-start | bytes 835592 | tf_op jit(solution)/shard_map/ppermute | solution.py:181
  48.0 25.3 %collective-permute-start.1 = (bf16[384,1024]{1,0:T(8,128)(2,1)}, bf16[384,1024]{1,0:T(8,128)(2,1)}, u32[]{:S(2)}, u32[]{:S(2)}) collective-permute-start(bf16[384,1024]{1,0:T(8,128)(2,1)} %collective-permute-done), channel_id=1, source_target_pairs={{0,128},{128,0},{1,129},{129,1},{2,130},{130,2},{3,131},{131,3},{4... | collective-permute-start | bytes 2359304 | tf_op jit(solution)/shard_map/ppermute | solution.py:224
  53.7 9.3 %collective-permute-start.13 = (bf16[272,256]{1,0:T(8,128)(2,1)}, bf16[272,256]{1,0:T(8,128)(2,1)}, u32[]{:S(2)}, u32[]{:S(2)}) collective-permute-start(bf16[272,256]{1,0:T(8,128)(2,1)} %slice_select_fusion.1), channel_id=1, source_target_pairs={{0,1},{1,2},{2,3},{3,4},{4,5},{5,6},{6,7},{7,0},{8,9},{9,10},{10,1... | collective-permute-start | bytes 417800 | tf_op jit(solution)/shard_map/ppermute | solution.py:184
  57.9 9.0 %collective-permute-start.8 = (bf16[544,256]{1,0:T(8,128)(2,1)}, bf16[544,256]{1,0:T(8,128)(2,1)}, u32[]{:S(2)}, u32[]{:S(2)}) collective-permute-start(bf16[544,256]{1,0:T(8,128)(2,1)} %collective-permute-done.7.refs_1_), channel_id=1, source_target_pairs={{0,128},{128,0},{1,129},{129,1},{2,130},{130,2},{3,131},{131,3},{4... | collective-permute-start | bytes 835592 | tf_op jit(solution)/shard_map/ppermute | solution.py:182
  59.7 7.1 %collective-permute-start.10 = (bf16[544,256]{1,0:T(8,128)(2,1)}, bf16[544,256]{1,0:T(8,128)(2,1)}, u32[]{:S(2)}, u32[]{:S(2)}) collective-permute-start(bf16[544,256]{1,0:T(8,128)(2,1)} %collective-permute-done.9.refs_3_), channel_id=1, source_target_pairs={{0,128},{128,0},{1,129},{129,1},{2,130},{130,2},{3,131},{131,3},{4... | collective-permute-start | bytes 835592 | tf_op jit(solution)/shard_map/ppermute | solution.py:182
  59.7 7.3 %collective-permute-start.12 = (bf16[544,256]{1,0:T(8,128)(2,1)S(1)}, bf16[544,256]{1,0:T(8,128)(2,1)}, u32[]{:S(2)}, u32[]{:S(2)}) collective-permute-start(bf16[544,256]{1,0:T(8,128)(2,1)S(1)} %collective-permute-done.11.refs_5_), channel_id=1, source_target_pairs={{0,128},{128,0},{1,129},{129,1},{2,130},{130,2},{3,131},{131,3},{4... | collective-permute-start | bytes 835592 | tf_op jit(solution)/shard_map/ppermute | solution.py:182
  63.0 4.0 %collective-permute-start.14 = (bf16[272,256]{1,0:T(8,128)(2,1)}, bf16[272,256]{1,0:T(8,128)(2,1)S(1)}, u32[]{:S(2)}, u32[]{:S(2)}) collective-permute-start(bf16[272,256]{1,0:T(8,128)(2,1)} %collective-permute-done.13.refs_7_), channel_id=1, source_target_pairs={{0,128},{128,0},{1,129},{129,1},{2,130},{130,2},{3,131},{131,3},{4... | collective-permute-start | bytes 417800 | tf_op jit(solution)/shard_map/ppermute | solution.py:185
  67.0 1.0 copy-start.3
  68.0 0.6 copy-start.4
  68.6 9.9 %slice-start = ((s8[8388608]{0:T(1024)(128)(4,1)}), s8[4194304]{0:T(1024)(128)(4,1)S(1)}, s32[]{:S(2)}) async-start(s8[8388608]{0:T(1024)(128)(4,1)} %bitcast.24), calls=%async_computation.4 | async-start | bytes 8388608
  72.8 3.1 %copy-start.5 = (bf16[384,2048]{1,0:T(8,128)(2,1)S(1)}, bf16[384,2048]{1,0:T(8,128)(2,1)}, u32[]{:S(2)}) copy-start(bf16[384,2048]{1,0:T(8,128)(2,1)} %constant_dynamic-slice_fusion.3) | copy-start | bytes 4718596
  72.8 5.5 %collective-permute-start.15 = (bf16[256,512]{1,0:T(8,128)(2,1)S(1)}, bf16[256,512]{1,0:T(8,128)(2,1)S(1)}, u32[]{:S(2)}, u32[]{:S(2)}) collective-permute-start(bf16[256,512]{1,0:T(8,128)(2,1)S(1)} %attend.1), channel_id=1, source_target_pairs={{0,128},{128,0},{1,129},{129,1},{2,130},{130,2},{3,131},{131,3},{4... | collective-permute-start | bytes 786440 | tf_op jit(solution)/shard_map/ppermute | solution.py:265
  73.3 5.2 %slice-start.1 = ((s8[8388608]{0:T(1024)(128)(4,1)}), s8[4194304]{0:T(1024)(128)(4,1)S(1)}, s32[]{:S(2)}) async-start(s8[8388608]{0:T(1024)(128)(4,1)} %bitcast.24), calls=%async_computation.5 | async-start | bytes 8388608
  81.6 1.0 copy-start.1
  82.6 33.3 %all-to-all-start = ((bf16[8,256,256]{2,1,0:T(8,128)(2,1)}), bf16[8,256,256]{2,1,0:T(8,128)(2,1)}, u32[]{:S(2)}, u32[]{:S(2)}) async-start(bf16[8,256,256]{2,1,0:T(8,128)(2,1)} %copy-done.1), calls=%async_computation | async-start | bytes 2097152 | tf_op jit(solution)/shard_map/all_to_all | solution.py:272
  90.2 27.0 %copy-start.6 = (bf16[384,256]{1,0:T(8,128)(2,1)S(1)}, bf16[384,256]{1,0:T(8,128)(2,1)}, u32[]{:S(2)}) copy-start(bf16[384,256]{1,0:T(8,128)(2,1)} %fusion.4) | copy-start | bytes 589828
  90.3 31.6 %copy-start.8 = (f32[768,1]{0,1:T(1,128)S(1)}, f32[768,1]{0,1:T(1,128)}, u32[]{:S(2)}) copy-start(f32[768,1]{0,1:T(1,128)} %div.37) | copy-start | bytes 9220
  90.3 24.6 %collective-permute-start.2 = (bf16[768,256]{1,0:T(8,128)(2,1)S(1)}, bf16[768,256]{1,0:T(8,128)(2,1)S(1)}, u32[]{:S(2)}, u32[]{:S(2)}) collective-permute-start(bf16[768,256]{1,0:T(8,128)(2,1)S(1)} %get-tuple-element.21), channel_id=1, source_target_pairs={{0,8},{1,9},{2,10},{3,11},{4,12},{5,13},{6,14},{7,15},{8,0},{9,1},... | collective-permute-start | bytes 1179656 | tf_op jit(solution)/shard_map/ppermute | solution.py:276
  118.3 15.8 %all-to-all-start.1 = ((bf16[16,48,256]{2,1,0:T(8,128)(2,1)}), bf16[16,48,256]{2,1,0:T(8,128)(2,1)S(1)}, u32[]{:S(2)}, u32[]{:S(2)}) async-start(bf16[16,48,256]{2,1,0:T(8,128)(2,1)} %pad_maximum_fusion), calls=%async_computation.1 | async-start | bytes 786432 | tf_op jit(solution)/shard_map/all_to_all | solution.py:284
  167.7 6.5 %collective-permute-start.16 = (f32[256,256]{1,0:T(8,128)S(1)}, f32[256,256]{1,0:T(8,128)}, u32[]{:S(2)}, u32[]{:S(2)}) collective-permute-start(f32[256,256]{1,0:T(8,128)S(1)} %convert_reduce_fusion), channel_id=1, source_target_pairs={{0,128},{1,129},{2,130},{3,131},{4,132},{5,133},{6,134},{7,135},{8... | collective-permute-start | bytes 786440 | tf_op jit(solution)/shard_map/ppermute | solution.py:302
Sparse Core Ops, SparseCore 0:
  21.0 40.8 all-gather.1

commit v3 on v2

v3 whole, which is shorter than its diff:
```python
import functools

import jax
import jax.numpy as jnp
from jax import lax
from jax.experimental import pallas as pl
from jax.experimental.pallas import tpu as pltpu
from jax.sharding import PartitionSpec as P

HD = 128
ZN = 8
WINDOW = 9
PIECE = 272
LOW = -1e30


def along_x(step):
    return [(2 * x + y, 2 * ((x + step) % 4) + y) for x in range(4) for y in range(2)]


def partner_pairs(base):
    return [(base + i, base + (i + ZN) % (2 * ZN)) for i in range(2 * ZN)]


def attention_kernel(
    info, query, seg_query, mine, other, out, kept, seg_kept, stacked, scores, acc, top
):
    shard = info[0]
    core = info[1]
    tok = query.shape[0]
    heads = query.shape[1] // HD
    scale = (HD**-0.5) * 1.4426950408889634
    seg_q = seg_query[...]
    first_seg = seg_q[0:1, :][0, 0]

    def keep_block(block, count):
        tail = mine[block, 256:272, :].astype(jnp.float32)
        last_seg = tail[1:2, HD - 1 : HD][0, 0]
        wanted = (block >= shard - WINDOW) & (last_seg >= first_seg)

        @pl.when(wanted)
        def _():
            first = mine[block, 0:256, :]
            second = other[block, 0:256, :]
            rows = pl.ds(pl.multiple_of(count * 256, 256), 256)
            kept[rows, 0:HD] = jnp.where(core == 0, first, second)
            kept[rows, HD : 2 * HD] = jnp.where(core == 0, second, first)
            seg_kept[count] = jnp.concatenate([tail[0:1, :], tail[1:2, :]], axis=1)

        return count + wanted.astype(jnp.int32)

    count = lax.fori_loop(0, shard + 1, keep_block, jnp.int32(0))

    @pl.when(lax.rem(count, 2) == 1)
    def _():
        kept[pl.ds(pl.multiple_of(count * 256, 256), 256), :] = jnp.zeros(
            (256, 2 * HD), jnp.bfloat16
        )
        seg_kept[count] = jnp.full((1, 256), -1.0, jnp.float32)

    for head in range(heads):
        stacked[head * tok : (head + 1) * tok, :] = query[:, head * HD : (head + 1) * HD]
    top[...] = jnp.full_like(top, LOW)
    acc[...] = jnp.zeros_like(acc)
    causal = lax.broadcasted_iota(jnp.int32, (tok, 256), 1) <= lax.broadcasted_iota(
        jnp.int32, (tok, 256), 0
    )

    def score_pair(pair, carry):
        keys = kept[pl.ds(pl.multiple_of(pair * 512, 512), 512), 0:HD]
        found = lax.dot_general(
            stacked[...], keys, (((1,), (1,)), ((), ())), preferred_element_type=jnp.float32
        )
        for side in range(2):
            index = 2 * pair + side
            allowed = (seg_kept[index] == seg_q) & (causal | (index != count - 1))
            for head in range(heads):
                rows = slice(head * tok, (head + 1) * tok)
                part = jnp.where(allowed, found[rows, side * 256 : (side + 1) * 256], LOW)
                scores[index, rows, :] = part
                top[rows, :] = jnp.maximum(top[rows, :], jnp.maximum(part[:, :HD], part[:, HD:]))
        return carry

    pairs = (count + 1) // 2
    lax.fori_loop(0, pairs, score_pair, 0)
    top[...] = jnp.broadcast_to(jnp.max(top[...], axis=1, keepdims=True), top.shape)

    def mix_pair(pair, carry):
        values = kept[pl.ds(pl.multiple_of(pair * 512, 512), 512), HD : 2 * HD]
        values = jnp.concatenate([values, jnp.ones_like(values)], axis=1)
        best = jnp.concatenate([top[...], top[...]], axis=1)
        weights = jnp.concatenate(
            [
                jnp.exp2((scores[2 * pair + side] - best) * scale).astype(jnp.bfloat16)
                for side in range(2)
            ],
            axis=1,
        )
        acc[...] += jnp.dot(weights, values, preferred_element_type=jnp.float32)
        return carry

    lax.fori_loop(0, pairs, mix_pair, 0)
    for head in range(heads):
        mixed = acc[head * tok : (head + 1) * tok, :]
        out[:, head * HD : (head + 1) * HD] = (mixed[:, :HD] / mixed[:, HD:]).astype(jnp.bfloat16)


def attend(info, query, seg_query, mine, other):
    tok, width = query.shape
    heads = width // HD
    blocks = WINDOW + 1
    vmem = pl.BlockSpec(memory_space=pltpu.VMEM)
    return pl.pallas_call(
        attention_kernel,
        out_shape=jax.ShapeDtypeStruct((tok, width), jnp.bfloat16),
        in_specs=[pl.BlockSpec(memory_space=pltpu.SMEM)] + [vmem] * 4,
        out_specs=vmem,
        scratch_shapes=[
            pltpu.VMEM((blocks * 256, 2 * HD), jnp.bfloat16),
            pltpu.VMEM((blocks, 1, 256), jnp.float32),
            pltpu.VMEM((heads * tok, HD), jnp.bfloat16),
            pltpu.VMEM((blocks, heads * tok, 256), jnp.float32),
            pltpu.VMEM((heads * tok, 2 * HD), jnp.float32),
            pltpu.VMEM((heads * tok, HD), jnp.float32),
        ],
        compiler_params=pltpu.CompilerParams(vmem_limit_bytes=40 * 1024 * 1024),
        cost_estimate=pl.CostEstimate(
            flops=8 * tok * width * 2560,
            bytes_accessed=4 << 20,
            transcendentals=tok * heads * 2560,
        ),
        name="attend",
    )(info, query, seg_query, mine, other)


def project_kernel(core, context, weight, out):
    out[0] = jnp.dot(context[...], weight[...], preferred_element_type=jnp.float32).astype(
        jnp.bfloat16
    )


def project(core, context, projector, tensor_n):
    tok, width = context.shape
    feats = projector.shape[1] // (2 * tensor_n)
    return pl.pallas_call(
        project_kernel,
        out_shape=jax.ShapeDtypeStruct((tensor_n, tok, feats), jnp.bfloat16),
        grid_spec=pltpu.PrefetchScalarGridSpec(
            num_scalar_prefetch=1,
            grid=(tensor_n,),
            in_specs=[
                pl.BlockSpec((tok, width), lambda i, core: (0, 0)),
                pl.BlockSpec((width, feats), lambda i, core: (0, 2 * i + core[0])),
            ],
            out_specs=pl.BlockSpec((1, tok, feats), lambda i, core: (i, 0, 0)),
        ),
        compiler_params=pltpu.CompilerParams(vmem_limit_bytes=16 * 1024 * 1024),
        cost_estimate=pl.CostEstimate(
            flops=2 * tok * width * feats * tensor_n,
            bytes_accessed=2 * width * feats * tensor_n,
            transcendentals=0,
        ),
        name="project",
    )(core, context, projector)


def student_kernel(place, ours, near, far, weight, out):
    x_place = place[0]
    core = place[1]
    feats = weight.shape[1]
    out[:, 0:feats] = jnp.dot(
        ours[...], weight[...], preferred_element_type=jnp.float32
    ).astype(jnp.bfloat16)
    total = None
    for step in range(4):
        for blocks, side in ((near, core), (far, 1 - core)):
            start = (lax.rem(x_place + step, 4) * 2 + side) * 256
            part = jnp.dot(
                blocks[step],
                weight[pl.ds(pl.multiple_of(start, 256), 256), :],
                preferred_element_type=jnp.float32,
            )
            total = part if total is None else total + part
    out[:, feats:] = total.astype(jnp.bfloat16)


def gradient_kernel(place, ours, near, far, output, theirs, routed, scale, out):
    x_place = place[0]
    core = place[1]
    feats = output.shape[1] // 2

    def residual(lanes, other_lanes, column):
        whole = output[:, lanes].astype(jnp.float32) + theirs[:, other_lanes].astype(jnp.float32)
        whole = whole - routed[:, lanes].astype(jnp.float32)
        return (whole * scale[:, column : column + 1]).astype(jnp.bfloat16)

    left, right = slice(0, feats), slice(feats, 2 * feats)
    own = residual(left, right, 0)
    partner = residual(right, left, 1)
    over_rows = (((0,), (0,)), ((), ()))
    for step in range(4):
        for blocks, side in ((near, core), (far, 1 - core)):
            index = lax.rem(x_place + step, 4) * 2 + side
            columns = pl.ds(pl.multiple_of(index * 256, 256), 256)
            out[index] = (
                lax.dot_general(
                    ours[:, columns], own, over_rows, preferred_element_type=jnp.float32
                )
                + lax.dot_general(
                    blocks[step], partner, over_rows, preferred_element_type=jnp.float32
                )
            ).astype(jnp.bfloat16)


def on_core(kernel, name, shape, flops, place, *args):
    vmem = pl.BlockSpec(memory_space=pltpu.VMEM)
    return pl.pallas_call(
        kernel,
        out_shape=jax.ShapeDtypeStruct(shape, jnp.bfloat16),
        in_specs=[pl.BlockSpec(memory_space=pltpu.SMEM)] + [vmem] * len(args),
        out_specs=vmem,
        compiler_params=pltpu.CompilerParams(vmem_limit_bytes=32 * 1024 * 1024),
        cost_estimate=pl.CostEstimate(flops=flops, bytes_accessed=6 << 20, transcendentals=0),
        name=name,
    )(place, *args)


def gather_keyval(group, keyval, query, segments, rest):
    tok, width = query.shape
    swap = [(0, 1), (1, 0)]
    seg_rows = segments.astype(jnp.bfloat16).reshape(2, HD)
    seg_rows = jnp.concatenate([seg_rows, jnp.zeros((14, HD), jnp.bfloat16)], axis=0)
    passed = lax.ppermute(keyval, "group", [(0, 1)])
    piece = jnp.where(group == 0, keyval[:, :HD], passed[:, HD:])
    piece = jnp.concatenate([piece, seg_rows], axis=0)
    pieces = jnp.broadcast_to(piece[None], (2 * ZN, PIECE, HD))
    pieces, query = lax.optimization_barrier((pieces, query))
    mine = lax.all_to_all(pieces, "seq", split_axis=0, concat_axis=0, tiled=True)
    other = lax.ppermute(mine, "group", swap)
    after = lax.ppermute(mine[0, :16], "group", swap)
    other_query = lax.ppermute(query[:, width // 2 :], "group", [(0, 1)])
    other_query, rest = lax.optimization_barrier((other_query, rest))
    query = jnp.where(group == 0, query[:, : width // 2], other_query)
    return query, mine, other, after, rest


def shards(
    teacher_query,
    teacher_keyval,
    segment_ids,
    projector,
    owner_table,
    student_context,
    student_out_weight,
):
    group = lax.axis_index("group")
    seq = lax.axis_index("seq")
    high = seq // ZN
    query = teacher_query[0]
    tok = query.shape[0]
    slots, model = student_context.shape
    owners_n = 2 * ZN
    capacity = slots // owners_n
    half = model // 2
    feats = student_out_weight.shape[1] // 2
    tensor_n = model // (2 * feats)
    z_groups = [[h * ZN + z for z in range(ZN)] for h in range(2)]

    query, mine, other, after, (student_context, student_out_weight, owner_table) = gather_keyval(
        group,
        teacher_keyval[0],
        query,
        segment_ids,
        (student_context, student_out_weight, owner_table),
    )
    weight = lax.dynamic_slice_in_dim(student_out_weight, group * feats, feats, axis=1)
    weight = jnp.broadcast_to(weight[None], (ZN,) + weight.shape)
    weight, after = lax.optimization_barrier((weight, after))
    weight = lax.all_to_all(
        weight, "seq", split_axis=0, concat_axis=0, tiled=True, axis_index_groups=z_groups
    ).reshape(half, feats)

    core_swap = [(0, 1), (1, 0)]
    all_pairs = partner_pairs(0) + partner_pairs(owners_n)
    quarter = half // 4
    x_place = lax.axis_index("tensor") // 2
    sent = lax.dynamic_slice_in_dim(
        student_context,
        (1 - high) * half + x_place * quarter + group * (quarter // 2),
        quarter // 2,
        axis=1,
    )
    came = lax.ppermute(sent, ("group", "seq"), all_pairs)
    behind = lax.ppermute(came, "tensor", along_x(1))
    ahead = lax.ppermute(came, "tensor", along_x(-1))
    across = lax.ppermute(came, "tensor", along_x(2))
    near = jnp.stack([came, ahead, across, behind])
    far = lax.ppermute(near, "group", core_swap)
    ours = lax.dynamic_slice_in_dim(student_context, high * half, half, axis=1)
    place = jnp.stack([x_place, group]).astype(jnp.int32)

    info = jnp.stack([seq, group]).astype(jnp.int32)
    seg_query = segment_ids.astype(jnp.float32)[:, None]

    owners_all = owner_table[:, 0]
    owners = lax.dynamic_slice_in_dim(owners_all, seq * tok, tok)
    index = jnp.arange(tok, dtype=jnp.int32)
    ranks = jnp.sum(
        ((owners[:, None] == owners[None, :]) & (index[None, :] < index[:, None])).astype(
            jnp.int32
        ),
        axis=1,
    )
    slot = owners * capacity + ranks
    route = (jnp.arange(slots, dtype=jnp.int32)[:, None] == slot[None, :]).astype(jnp.bfloat16)
    pair_owners = jnp.stack([seq, (seq + ZN) % owners_n])
    counts = jnp.sum(
        (owners_all.reshape(owners_n, tok, 1) == pair_owners[None, None, :]).astype(jnp.int32),
        axis=1,
    )
    live = jnp.arange(capacity, dtype=jnp.int32)[None, :, None] < counts[:, None, :]
    scale = live.reshape(slots, 2).astype(jnp.float32) / tok
    mine, route, scale, near, far, ours = lax.optimization_barrier(
        (mine, route, scale, near, far, ours)
    )
    context = attend(info, query, seg_query, mine, other)

    other_context = lax.ppermute(context, "group", core_swap)
    context = jnp.where(
        group == 0,
        jnp.concatenate([context, other_context], axis=1),
        jnp.concatenate([other_context, context], axis=1),
    )
    partial = project(group[None].astype(jnp.int32), context, projector, tensor_n)
    partial = lax.all_to_all(partial, "tensor", split_axis=0, concat_axis=0, tiled=True)
    output = on_core(
        student_kernel, "student", (slots, 2 * feats), 4 * slots * half * feats,
        place, ours, near, far, weight,
    )
    partial, output = lax.optimization_barrier((partial, output))
    theirs = lax.ppermute(output, ("group", "seq"), all_pairs)
    target = jnp.sum(partial.astype(jnp.float32), axis=0).astype(jnp.bfloat16)

    routed = jnp.dot(route, target, preferred_element_type=jnp.float32).astype(jnp.bfloat16)
    routed = jnp.concatenate([routed, jnp.roll(routed, slots // 2, axis=0)], axis=1)
    routed = lax.all_to_all(
        routed.reshape(owners_n, capacity, 2 * feats),
        "seq",
        split_axis=0,
        concat_axis=0,
        tiled=True,
    ).reshape(slots, 2 * feats)

    gradient = on_core(
        gradient_kernel, "gradient", (ZN, half // ZN, feats), 4 * slots * half * feats,
        place, ours, near, far, output, theirs, routed, scale,
    )
    gradient = lax.all_to_all(
        gradient,
        "seq",
        split_axis=0,
        concat_axis=0,
        tiled=True,
        axis_index_groups=z_groups,
    )
    gradient = jnp.sum(gradient.astype(jnp.float32), axis=0)
    passed = lax.ppermute(gradient, "group", [(0, 1)])
    whole = jnp.concatenate([passed, gradient], axis=1)
    return jnp.where(group == 1, whole, 0.0)[None]


def solution(mesh):
    placed = (
        P("group", "seq", "tensor"),
        P("group", "seq", "tensor"),
        P("seq"),
        P("tensor", None),
        P(),
        P("seq", None),
        P("seq", "tensor"),
    )
    return jax.shard_map(
        shards, mesh=mesh, in_specs=placed, out_specs=P("group", "seq", "tensor"), check_vma=False
    )
```

time: 184 us -> 171 us (0.929)
  between operations: 13.8 us -> 0.31 us
  waiting for transfers between devices: 46.3 us -> 53 us
  other arithmetic: 18.9 us -> 13.3 us
  matrix products: 6.59 us -> 1.2 us
  Pallas kernels: 7.37 us -> 12.1 us
  starting transfers between devices: 47.8 us -> 44.3 us
  blocking collectives: 30.3 us -> 32.4 us
    ppermute x13 -> x7, starting transfers between devices: 33.1 us -> 12 us  [the longest x1 2.87 us: shards(): theirs = lax.ppermute(output, ('group', 'seq'), all_pairs)]
    all_to_all x1 -> x3, starting transfers between devices: 3.55 us -> 22.1 us  [the longest x1 9.68 us: gather_keyval(): lax.all_to_all(pieces, 'seq', split_axis=0, concat_axis=0, tiled=True)]
    ppermute x13 -> x7, waiting for transfers between devices: 28.9 us -> 15.4 us  [the longest x1 12 us: shards(): theirs = lax.ppermute(output, ('group', 'seq'), all_pairs)]
    all_to_all x1, waiting for transfers between devices: 0.01 us -> 9.35 us  [shards(): lax.all_to_all(partial, 'tensor', split_axis=0, concat_axis=0, tiled=True)]
    dot_general x2 -> x0, matrix products: 6.39 us -> none  [the longest x1 3.23 us: shards(): lax.dot_general(rows, residual, (((0,), (0,)), ((), ())), preferred_eleme...]
    select_n x5 -> x1, other arithmetic: 6.66 us -> 0.85 us  [gather_keyval(): piece = jnp.where(group == 0, keyval[:, :HD], passed[:, HD:])]
    pallas_call x0 -> x2, Pallas kernels: none -> 5.6 us  [on_core(): pl.pallas_call(kernel, out_shape=jax.ShapeDtypeStruct(shape, jnp.bfloat16...]
    all_to_all x1 -> x3, waiting for transfers between devices: 12.2 us -> 16.3 us  [the longest x1 9.12 us: shards(): lax.all_to_all(weight, 'seq', split_axis=0, concat_axis=0, tiled=True, ax...]
  transfers between devices with their start and end apart: 20 -> 15, of which waited for: 8 -> 9; matrix products, arithmetic and copies ran while one was open for 12% -> 8% of each run, Pallas kernels for 4% -> 5%
where the time goes in v3:
time: 171 us; the launch traced here: 170 us
  waiting for transfers between devices  53 us (31%)
  starting transfers between devices  44.3 us (26%)
  blocking collectives  32.4 us (19%)
  local copies, waits for them, and re-layouts  13.5 us (8%)
  other arithmetic  13.3 us (8%)
  Pallas kernels  12.1 us (7%)
    all_to_all x1, blocking collectives, shards(): lax.all_to_all(gradient, 'seq', split_axis=0, concat_axis=0, tiled=True,...  32.4 us
    ppermute x1, waiting for transfers between devices, shards(): theirs = lax.ppermute(output, ('group', 'seq'), all_pairs)  12 us
    all_to_all x1, starting transfers between devices, gather_keyval(): lax.all_to_all(pieces, 'seq', split_axis=0, concat_axis=0, tiled=True)  9.68 us
    all_to_all x1, waiting for transfers between devices, shards(): lax.all_to_all(partial, 'tensor', split_axis=0, concat_axis=0, tiled=True)  9.35 us
    all_to_all x1, waiting for transfers between devices, shards(): lax.all_to_all(weight, 'seq', split_axis=0, concat_axis=0, tiled=True, ax...  9.12 us
    all_to_all x1, starting transfers between devices, shards(): lax.all_to_all(routed.reshape(owners_n, capacity, 2 * feats), 'seq', spli...  7.95 us
    all_to_all x1, waiting for transfers between devices, gather_keyval(): lax.all_to_all(pieces, 'seq', split_axis=0, concat_axis=0, tiled=True)  7.17 us
    unnamed x18, local copies, waits for them, and re-layouts  6.46 us
  transfers between devices with their start and end apart: 15, of which 9 were waited for; matrix products, arithmetic and copies ran while one was open for 8% of the time, Pallas kernels for 5%

profile of v3, /device:TPU:1, one launch (start us, length us, event | category | flops | bytes accessed | tf_op | source)
XLA Modules:
  0.0 170.2 jit_solution(12921712574825375850)
XLA Ops:
  0.0 1.5 collective-permute-start
  2.4 3.4 %collective-permute-done = bf16[256,256]{1,0:T(8,128)(2,1)S(1)} collective-permute-done((bf16[256,256]{1,0:T(8,128)(2,1)}, bf16[256,256]{1,0:T(8,128)(2,1)S(1)}, u32[]{:S(2)}, u32[]{:S(2)}) %collective-permute-start) | collective-permute-done | bytes 131104 | tf_op jit(solution)/shard_map/ppermute | solution.py:233
  7.9 9.7 %all-to-all-start = ((bf16[16,272,128]{2,1,0:T(8,128)(2,1)}), bf16[16,272,128]{2,1,0:T(8,128)(2,1)}, u32[]{:S(2)}, u32[]{:S(2)}) async-start(bf16[16,272,128]{2,1,0:T(8,128)(2,1)} %broadcast_in_dim.12), calls=%async_computation | async-start | bytes 2228224 | tf_op jit(solution)/shard_map/all_to_all | solution.py:238
  18.6 1.3 collective-permute-start.1
  20.3 1.8 %collective-permute-done.1 = bf16[256,512]{1,0:T(8,128)(2,1)} collective-permute-done((bf16[256,512]{1,0:T(8,128)(2,1)S(1)}, bf16[256,512]{1,0:T(8,128)(2,1)}, u32[]{:S(2)}, u32[]{:S(2)}) %collective-permute-start.1) | collective-permute-done | bytes 262176 | tf_op jit(solution)/shard_map/ppermute | solution.py:241
  22.7 1.4 reduce.4
  24.1 2.9 %collective-permute-start.2 = (bf16[384,256]{1,0:T(8,128)(2,1)S(1)}, bf16[384,256]{1,0:T(8,128)(2,1)S(1)}, u32[]{:S(2)}, u32[]{:S(2)}) collective-permute-start(bf16[384,256]{1,0:T(8,128)(2,1)S(1)} %constant_dynamic-slice_fusion.2), channel_id=1, source_target_pairs={{0,8},{1,9},{2,10},{3,11},{4,12},{5,13},{6,14},{7,15},{8,0},{9,1},... | collective-permute-start | bytes 589832 | tf_op jit(solution)/shard_map/ppermute | solution.py:293
  29.9 3.9 %collective-permute-done.2 = bf16[384,256]{1,0:T(8,128)(2,1)S(1)} collective-permute-done((bf16[384,256]{1,0:T(8,128)(2,1)S(1)}, bf16[384,256]{1,0:T(8,128)(2,1)S(1)}, u32[]{:S(2)}, u32[]{:S(2)}) %collective-permute-start.2) | collective-permute-done | bytes 196640 | tf_op jit(solution)/shard_map/ppermute | solution.py:293
  33.8 1.2 collective-permute-start.5
  35.0 2.5 %collective-permute-start.4 = (bf16[384,256]{1,0:T(8,128)(2,1)S(1)}, bf16[384,256]{1,0:T(8,128)(2,1)}, u32[]{:S(2)}, u32[]{:S(2)}) collective-permute-start(bf16[384,256]{1,0:T(8,128)(2,1)S(1)} %collective-permute-done.2), channel_id=1, source_target_pairs={{0,64},{16,80},{32,96},{48,112},{64,0},{80,16},{96,32},{112,48},{1... | collective-permute-start | bytes 589832 | tf_op jit(solution)/shard_map/ppermute | solution.py:296
  38.6 7.2 %all-to-all-done.mine = bf16[16,272,128]{2,1,0:T(8,128)(2,1)} async-done(((bf16[16,272,128]{2,1,0:T(8,128)(2,1)}), bf16[16,272,128]{2,1,0:T(8,128)(2,1)}, u32[]{:S(2)}, u32[]{:S(2)}) %all-to-all-start) | async-done | bytes 1114144 | tf_op jit(solution)/shard_map/all_to_all | solution.py:238
  45.8 4.5 %all-to-all-start.2 = ((bf16[8,256,256]{2,1,0:T(8,128)(2,1)}), bf16[8,256,256]{2,1,0:T(8,128)(2,1)}, u32[]{:S(2)}, u32[]{:S(2)}) async-start(bf16[8,256,256]{2,1,0:T(8,128)(2,1)} %broadcast_in_dim.14), calls=%async_computation.2 | async-start | bytes 2097152 | tf_op jit(solution)/shard_map/all_to_all | solution.py:279
  50.3 2.7 %collective-permute-start.7 = (bf16[16,272,128]{2,1,0:T(8,128)(2,1)}, bf16[16,272,128]{2,1,0:T(8,128)(2,1)}, u32[]{:S(2)}, u32[]{:S(2)}) collective-permute-start(bf16[16,272,128]{2,1,0:T(8,128)(2,1)} %all-to-all-done.mine), channel_id=1, source_target_pairs={{0,128},{128,0},{1,129},{129,1},{2,130},{130,2},{3,131},{131,3},{4... | collective-permute-start | bytes 3342344 | tf_op jit(solution)/shard_map/ppermute | solution.py:239
  53.0 2.1 %pad_maximum_fusion.near = bf16[4,384,256]{2,1,0:T(8,128)(2,1)} fusion(bf16[1,384,256]{2,1,0:T(8,128)(2,1)} %bitcast.12, bf16[1,384,256]{2,1,0:T(8,128)(2,1)} %bitcast.11, bf16[1,384,256]{2,1,0:T(8,128)(2,1)} %bitcast.10, bf16[1,384,256]{2,1,0:T(8,128)(2,1)S(1)} %bitcast.32), kind=kLoop, calls=%fused_computation.2 | loop fusion | flops 1179648 | bytes 1572864 | tf_op jit(solution)/shard_map/stack | solution.py:297
  58.0 1.4 constant_dynamic-slice_fusion.1.ours
  59.4 3.4 %attend.1 = bf16[256,512]{1,0:T(8,128)(2,1)S(1)} custom-call(s32[2]{0:T(128)S(1)} %pad_add_fusion.2.info, bf16[256,512]{1,0:T(8,128)(2,1)S(1)} %slice_select_fusion.query, f32[256,1]{1,0:T(8,128)S(1)} %copy.10.seg_query, bf16[16,272,128]{2,1,0:T(8,128)(2,1)} %all-to-all-done.mine, bf16[16,272,128]{2,1,0:T(8,128)(2,1)} %collective-permute-done.7.other), custom_call_target="tpu_custom_call" | custom-call | flops 2684354560 | bytes 4194304 | tf_op jit(solution)/shard_map/attend/pallas_call | solution.py:113
  64.5 3.2 %project.1 = bf16[8,256,256]{2,1,0:T(8,128)(2,1)S(1)} custom-call(s32[1]{0:T(128)} %bitcast.1.core, bf16[256,1024]{1,0:T(8,128)(2,1)S(1)} %maximum_select_fusion.context, bf16[1024,4096]{1,0:T(8,128)(2,1)S(1)} %bitcast.27), custom_call_target="tpu_custom_call" | custom-call | flops 1073741824 | bytes 4194304 | tf_op jit(solution)/shard_map/project/pallas_call | solution.py:145
  68.7 9.1 %all-to-all-done.2 = bf16[8,256,256]{2,1,0:T(8,128)(2,1)} async-done(((bf16[8,256,256]{2,1,0:T(8,128)(2,1)}), bf16[8,256,256]{2,1,0:T(8,128)(2,1)}, u32[]{:S(2)}, u32[]{:S(2)}) %all-to-all-start.2) | async-done | bytes 1048608 | tf_op jit(solution)/shard_map/all_to_all | solution.py:279
  77.8 4.2 %all-to-all-start.1 = ((bf16[8,256,256]{2,1,0:T(8,128)(2,1)}), bf16[8,256,256]{2,1,0:T(8,128)(2,1)}, u32[]{:S(2)}, u32[]{:S(2)}) async-start(bf16[8,256,256]{2,1,0:T(8,128)(2,1)} %copy-done.3), calls=%async_computation.1 | async-start | bytes 2097152 | tf_op jit(solution)/shard_map/all_to_all | solution.py:335
  82.1 1.4 copy-done.1
  83.5 2.7 %student.1.output = bf16[384,512]{1,0:T(8,128)(2,1)S(1)} custom-call(s32[2]{0:T(128)S(1)} %pad_add_fusion.place, bf16[384,2048]{1,0:T(8,128)(2,1)S(1)} %copy-done.1, bf16[4,384,256]{2,1,0:T(8,128)(2,1)} %pad_maximum_fusion.near, bf16[4,384,256]{2,1,0:T(8,128)(2,1)} %collective-permute-done.6.far, bf16[2048,256]{1,0:T(8,128)(2,1)} %bitcast.14.weight), custom_call_target="tpu_custom_call" | custom-call | flops 805306368 | bytes 6291456 | tf_op jit(solution)/shard_map/student/pallas_call | solution.py:217
  86.2 9.4 %all-to-all-done.1 = bf16[8,256,256]{2,1,0:T(8,128)(2,1)} async-done(((bf16[8,256,256]{2,1,0:T(8,128)(2,1)}), bf16[8,256,256]{2,1,0:T(8,128)(2,1)}, u32[]{:S(2)}, u32[]{:S(2)}) %all-to-all-start.1) | async-done | bytes 1048608 | tf_op jit(solution)/shard_map/all_to_all | solution.py:335
  95.6 2.1 %reduce_sum.41 = bf16[256,256]{1,0:T(8,128)(2,1)} reduce(bf16[8,256,256]{2,1,0:T(8,128)(2,1)} %all-to-all-done.1, bf16[]{:T(256)} %constant.60.clone.1), dimensions={0}, to_apply=%region_2.3 | reduce | flops 458752 | bytes 1179650 | tf_op jit(solution)/shard_map/reduce_sum | solution.py:342
  99.6 8.0 %all-to-all-start.3 = ((bf16[16,24,512]{2,1,0:T(8,128)(2,1)}), bf16[16,24,512]{2,1,0:T(8,128)(2,1)}, u32[]{:S(2)}, u32[]{:S(2)}) async-start(bf16[16,24,512]{2,1,0:T(8,128)(2,1)} %bitcast.28), calls=%async_computation.3 | async-start | bytes 786432 | tf_op jit(solution)/shard_map/all_to_all | solution.py:346
  107.6 2.9 %collective-permute-start.9 = (bf16[384,512]{1,0:T(8,128)(2,1)S(1)}, bf16[384,512]{1,0:T(8,128)(2,1)S(1)}, u32[]{:S(2)}, u32[]{:S(2)}) collective-permute-start(bf16[384,512]{1,0:T(8,128)(2,1)S(1)} %student.1.output), channel_id=1, source_target_pairs={{0,8},{1,9},{2,10},{3,11},{4,12},{5,13},{6,14},{7,15},{8,0},{9,1},... | collective-permute-start | bytes 1179656 | tf_op jit(solution)/shard_map/ppermute | solution.py:341
  110.5 12.0 %collective-permute-done.9.theirs = bf16[384,512]{1,0:T(8,128)(2,1)S(1)} collective-permute-done((bf16[384,512]{1,0:T(8,128)(2,1)S(1)}, bf16[384,512]{1,0:T(8,128)(2,1)S(1)}, u32[]{:S(2)}, u32[]{:S(2)}) %collective-permute-start.9) | collective-permute-done | bytes 393248 | tf_op jit(solution)/shard_map/ppermute | solution.py:341
  123.2 1.4 copy-done.2
  126.5 2.9 %gradient.1 = bf16[8,256,256]{2,1,0:T(8,128)(2,1)S(1)} custom-call(s32[2]{0:T(128)S(1)} %pad_add_fusion.place, bf16[384,2048]{1,0:T(8,128)(2,1)S(1)} %copy-done.2, bf16[4,384,256]{2,1,0:T(8,128)(2,1)} %pad_maximum_fusion.near, bf16[4,384,256]{2,1,0:T(8,128)(2,1)} %collective-permute-done.6.far, bf16[384,512]{1,0:T(8,128)(2,1)S(1)} %student.1.output, ...), custom_call_target="tpu_custom_call" | custom-call | flops 805306368 | bytes 6291456 | tf_op jit(solution)/shard_map/gradient/pallas_call | solution.py:217
  129.5 32.4 %all_to_all.25 = bf16[8,256,256]{2,1,0:T(8,128)(2,1)S(1)} all-to-all(bf16[8,256,256]{2,1,0:T(8,128)(2,1)S(1)} %gradient.1), channel_id=1, replica_groups={{0,1,2,3,4,5,6,7},{8,9,10,11,12,13,14,15},{16,17,18,19,20,21,22,23},{24..., dimensions={0} | all-to-all | bytes 2097152 | tf_op jit(solution)/shard_map/all_to_all | solution.py:358
  162.0 1.3 collective-permute-start.10
  163.3 5.1 %collective-permute-done.10 = f32[256,256]{1,0:T(8,128)} collective-permute-done((f32[256,256]{1,0:T(8,128)S(1)}, f32[256,256]{1,0:T(8,128)}, u32[]{:S(2)}, u32[]{:S(2)}) %collective-permute-start.10) | collective-permute-done | bytes 262176 | tf_op jit(solution)/shard_map/ppermute | solution.py:367
  168.4 1.8 %maximum_select_fusion.1 = f32[1,256,512]{2,1,0:T(8,128)} fusion(f32[1,256,256]{2,1,0:T(8,128)S(1)} %bitcast.29, f32[1,256,256]{2,1,0:T(8,128)} %bitcast.17, pred[]{:T(512)S(6)} %eq.26), kind=kLoop, calls=%fused_computation.4 | loop fusion | flops 262144 | bytes 1048577 | tf_op jit(solution)/shard_map/jit(_where)/select_n | solution.py:369
  (58 shorter events, 19.3 us)
Async XLA Ops:
  0.0 24.1 %copy-start = (bf16[384,4096]{1,0:T(8,128)(2,1)S(1)}, bf16[384,4096]{1,0:T(8,128)(2,1)}, u32[]{:S(2)}) copy-start(bf16[384,4096]{1,0:T(8,128)(2,1)} %param.12) | copy-start | bytes 9437188
  0.0 5.8 %collective-permute-start = (bf16[256,256]{1,0:T(8,128)(2,1)}, bf16[256,256]{1,0:T(8,128)(2,1)S(1)}, u32[]{:S(2)}, u32[]{:S(2)}) collective-permute-start(bf16[256,256]{1,0:T(8,128)(2,1)} %bitcast.33), channel_id=1, source_target_pairs={{0,128},{1,129},{2,130},{3,131},{4,132},{5,133},{6,134},{7,135},{8... | collective-permute-start | bytes 393224 | tf_op jit(solution)/shard_map/ppermute | solution.py:233
  7.9 37.9 %all-to-all-start = ((bf16[16,272,128]{2,1,0:T(8,128)(2,1)}), bf16[16,272,128]{2,1,0:T(8,128)(2,1)}, u32[]{:S(2)}, u32[]{:S(2)}) async-start(bf16[16,272,128]{2,1,0:T(8,128)(2,1)} %broadcast_in_dim.12), calls=%async_computation | async-start | bytes 2228224 | tf_op jit(solution)/shard_map/all_to_all | solution.py:238
  18.6 3.6 %collective-permute-start.1 = (bf16[256,512]{1,0:T(8,128)(2,1)S(1)}, bf16[256,512]{1,0:T(8,128)(2,1)}, u32[]{:S(2)}, u32[]{:S(2)}) collective-permute-start(bf16[256,512]{1,0:T(8,128)(2,1)S(1)} %slice.23), channel_id=1, source_target_pairs={{0,128},{1,129},{2,130},{3,131},{4,132},{5,133},{6,134},{7,135},{8... | collective-permute-start | bytes 786440 | tf_op jit(solution)/shard_map/ppermute | solution.py:241
  24.1 9.7 %collective-permute-start.2 = (bf16[384,256]{1,0:T(8,128)(2,1)S(1)}, bf16[384,256]{1,0:T(8,128)(2,1)S(1)}, u32[]{:S(2)}, u32[]{:S(2)}) collective-permute-start(bf16[384,256]{1,0:T(8,128)(2,1)S(1)} %constant_dynamic-slice_fusion.2), channel_id=1, source_target_pairs={{0,8},{1,9},{2,10},{3,11},{4,12},{5,13},{6,14},{7,15},{8,0},{9,1},... | collective-permute-start | bytes 589832 | tf_op jit(solution)/shard_map/ppermute | solution.py:293
  33.8 19.2 %collective-permute-start.5 = (bf16[384,256]{1,0:T(8,128)(2,1)S(1)}, bf16[384,256]{1,0:T(8,128)(2,1)}, u32[]{:S(2)}, u32[]{:S(2)}) collective-permute-start(bf16[384,256]{1,0:T(8,128)(2,1)S(1)} %collective-permute-done.2), channel_id=1, source_target_pairs={{0,32},{16,48},{32,64},{48,80},{64,96},{80,112},{96,0},{112,16},{1... | collective-permute-start | bytes 589832 | tf_op jit(solution)/shard_map/ppermute | solution.py:294
  35.0 18.0 %collective-permute-start.4 = (bf16[384,256]{1,0:T(8,128)(2,1)S(1)}, bf16[384,256]{1,0:T(8,128)(2,1)}, u32[]{:S(2)}, u32[]{:S(2)}) collective-permute-start(bf16[384,256]{1,0:T(8,128)(2,1)S(1)} %collective-permute-done.2), channel_id=1, source_target_pairs={{0,64},{16,80},{32,96},{48,112},{64,0},{80,16},{96,32},{112,48},{1... | collective-permute-start | bytes 589832 | tf_op jit(solution)/shard_map/ppermute | solution.py:296
  37.5 15.5 %collective-permute-start.3 = (bf16[384,256]{1,0:T(8,128)(2,1)S(1)}, bf16[384,256]{1,0:T(8,128)(2,1)}, u32[]{:S(2)}, u32[]{:S(2)}) collective-permute-start(bf16[384,256]{1,0:T(8,128)(2,1)S(1)} %collective-permute-done.2), channel_id=1, source_target_pairs={{0,96},{16,112},{32,0},{48,16},{64,32},{80,48},{96,64},{112,80},{1... | collective-permute-start | bytes 589832 | tf_op jit(solution)/shard_map/ppermute | solution.py:295
  45.8 32.0 %all-to-all-start.2 = ((bf16[8,256,256]{2,1,0:T(8,128)(2,1)}), bf16[8,256,256]{2,1,0:T(8,128)(2,1)}, u32[]{:S(2)}, u32[]{:S(2)}) async-start(bf16[8,256,256]{2,1,0:T(8,128)(2,1)} %broadcast_in_dim.14), calls=%async_computation.2 | async-start | bytes 2097152 | tf_op jit(solution)/shard_map/all_to_all | solution.py:279
  50.3 9.1 %collective-permute-start.7 = (bf16[16,272,128]{2,1,0:T(8,128)(2,1)}, bf16[16,272,128]{2,1,0:T(8,128)(2,1)}, u32[]{:S(2)}, u32[]{:S(2)}) collective-permute-start(bf16[16,272,128]{2,1,0:T(8,128)(2,1)} %all-to-all-done.mine), channel_id=1, source_target_pairs={{0,128},{128,0},{1,129},{129,1},{2,130},{130,2},{3,131},{131,3},{4... | collective-permute-start | bytes 3342344 | tf_op jit(solution)/shard_map/ppermute | solution.py:239
  55.1 4.2 %collective-permute-start.6 = (bf16[4,384,256]{2,1,0:T(8,128)(2,1)}, bf16[4,384,256]{2,1,0:T(8,128)(2,1)}, u32[]{:S(2)}, u32[]{:S(2)}) collective-permute-start(bf16[4,384,256]{2,1,0:T(8,128)(2,1)} %pad_maximum_fusion.near), channel_id=1, source_target_pairs={{0,128},{128,0},{1,129},{129,1},{2,130},{130,2},{3,131},{131,3},{4... | collective-permute-start | bytes 2359304 | tf_op jit(solution)/shard_map/ppermute | solution.py:298
  55.4 9.1 %slice-start = ((s8[8388608]{0:T(1024)(128)(4,1)}), s8[4194304]{0:T(1024)(128)(4,1)S(1)}, s32[]{:S(2)}) async-start(s8[8388608]{0:T(1024)(128)(4,1)} %bitcast.26), calls=%async_computation.5 | async-start | bytes 8388608
  59.4 5.2 %slice-start.1 = ((s8[8388608]{0:T(1024)(128)(4,1)}), s8[4194304]{0:T(1024)(128)(4,1)S(1)}, s32[]{:S(2)}) async-start(s8[8388608]{0:T(1024)(128)(4,1)} %bitcast.26), calls=%async_computation.6 | async-start | bytes 8388608
  62.7 1.6 collective-permute-start.8
  67.7 1.0 copy-start.3
  77.8 17.8 %all-to-all-start.1 = ((bf16[8,256,256]{2,1,0:T(8,128)(2,1)}), bf16[8,256,256]{2,1,0:T(8,128)(2,1)}, u32[]{:S(2)}, u32[]{:S(2)}) async-start(bf16[8,256,256]{2,1,0:T(8,128)(2,1)} %copy-done.3), calls=%async_computation.1 | async-start | bytes 2097152 | tf_op jit(solution)/shard_map/all_to_all | solution.py:335
  82.1 1.4 copy-start.1
  99.6 23.6 %all-to-all-start.3 = ((bf16[16,24,512]{2,1,0:T(8,128)(2,1)}), bf16[16,24,512]{2,1,0:T(8,128)(2,1)}, u32[]{:S(2)}, u32[]{:S(2)}) async-start(bf16[16,24,512]{2,1,0:T(8,128)(2,1)} %bitcast.28), calls=%async_computation.3 | async-start | bytes 786432 | tf_op jit(solution)/shard_map/all_to_all | solution.py:346
  107.6 14.9 %collective-permute-start.9 = (bf16[384,512]{1,0:T(8,128)(2,1)S(1)}, bf16[384,512]{1,0:T(8,128)(2,1)S(1)}, u32[]{:S(2)}, u32[]{:S(2)}) collective-permute-start(bf16[384,512]{1,0:T(8,128)(2,1)S(1)} %student.1.output), channel_id=1, source_target_pairs={{0,8},{1,9},{2,10},{3,11},{4,12},{5,13},{6,14},{7,15},{8,0},{9,1},... | collective-permute-start | bytes 1179656 | tf_op jit(solution)/shard_map/ppermute | solution.py:341
  122.5 0.7 copy-start.5
  123.2 1.4 copy-start.2
  124.6 0.9 copy-start.4
  125.5 1.0 copy-start.6
  162.0 6.4 %collective-permute-start.10 = (f32[256,256]{1,0:T(8,128)S(1)}, f32[256,256]{1,0:T(8,128)}, u32[]{:S(2)}, u32[]{:S(2)}) collective-permute-start(f32[256,256]{1,0:T(8,128)S(1)} %convert_reduce_fusion), channel_id=1, source_target_pairs={{0,128},{1,129},{2,130},{3,131},{4,132},{5,133},{6,134},{7,135},{8... | collective-permute-start | bytes 786440 | tf_op jit(solution)/shard_map/ppermute | solution.py:367

commit v4 on v3

v4 whole, which is shorter than its diff:
```python
import functools

import jax
import jax.numpy as jnp
from jax import lax
from jax.experimental import pallas as pl
from jax.experimental.pallas import tpu as pltpu
from jax.sharding import PartitionSpec as P

HD = 128
ZN = 8
WINDOW = 9
PIECE = 272
LOW = -1e30


def partner_pairs(base):
    return [(base + i, base + (i + ZN) % (2 * ZN)) for i in range(2 * ZN)]


def attention_kernel(
    info, query, seg_query, mine, other, out, kept, seg_kept, stacked, scores, acc, top
):
    shard = info[0]
    core = info[1]
    tok = query.shape[0]
    heads = query.shape[1] // HD
    scale = (HD**-0.5) * 1.4426950408889634
    seg_q = seg_query[...]
    first_seg = seg_q[0:1, :][0, 0]

    upper = shard // ZN
    ring = lax.rem(shard, ZN)

    def keep_block(step, count):
        place = lax.rem(ring + 1 + step, ZN)
        place = jnp.where(step < ZN, place, step)
        block = jnp.where(place <= ring, upper * ZN + place, place)
        block = jnp.where(place == ZN, ring, block)
        block = jnp.where(place == ZN + 1, ring - 1, block)
        tail = mine[place, 256:272, :].astype(jnp.float32)
        last_seg = tail[1:2, HD - 1 : HD][0, 0]
        wanted = (block >= 0) & (block >= shard - WINDOW) & (block <= shard)
        wanted = wanted & (last_seg >= first_seg) & ((step < ZN) | (upper == 1))

        @pl.when(wanted)
        def _():
            first = mine[place, 0:256, :]
            second = other[place, 0:256, :]
            rows = pl.ds(pl.multiple_of(count * 256, 256), 256)
            kept[rows, 0:HD] = jnp.where(core == 0, first, second)
            kept[rows, HD : 2 * HD] = jnp.where(core == 0, second, first)
            seg_kept[count] = jnp.concatenate([tail[0:1, :], tail[1:2, :]], axis=1)

        return count + wanted.astype(jnp.int32)

    count = lax.fori_loop(ZN, ZN + 2, keep_block, jnp.int32(0))
    count = lax.fori_loop(0, ZN, keep_block, count)

    @pl.when(lax.rem(count, 2) == 1)
    def _():
        kept[pl.ds(pl.multiple_of(count * 256, 256), 256), :] = jnp.zeros(
            (256, 2 * HD), jnp.bfloat16
        )
        seg_kept[count] = jnp.full((1, 256), -1.0, jnp.float32)

    for head in range(heads):
        stacked[head * tok : (head + 1) * tok, :] = query[:, head * HD : (head + 1) * HD]
    top[...] = jnp.full_like(top, LOW)
    acc[...] = jnp.zeros_like(acc)
    causal = lax.broadcasted_iota(jnp.int32, (tok, 256), 1) <= lax.broadcasted_iota(
        jnp.int32, (tok, 256), 0
    )

    def score_pair(pair, carry):
        keys = kept[pl.ds(pl.multiple_of(pair * 512, 512), 512), 0:HD]
        found = lax.dot_general(
            stacked[...], keys, (((1,), (1,)), ((), ())), preferred_element_type=jnp.float32
        )
        for side in range(2):
            index = 2 * pair + side
            allowed = (seg_kept[index] == seg_q) & (causal | (index != count - 1))
            for head in range(heads):
                rows = slice(head * tok, (head + 1) * tok)
                part = jnp.where(allowed, found[rows, side * 256 : (side + 1) * 256], LOW)
                scores[index, rows, :] = part
                top[rows, :] = jnp.maximum(top[rows, :], jnp.maximum(part[:, :HD], part[:, HD:]))
        return carry

    pairs = (count + 1) // 2
    lax.fori_loop(0, pairs, score_pair, 0)
    top[...] = jnp.broadcast_to(jnp.max(top[...], axis=1, keepdims=True), top.shape)

    def mix_pair(pair, carry):
        values = kept[pl.ds(pl.multiple_of(pair * 512, 512), 512), HD : 2 * HD]
        values = jnp.concatenate([values, jnp.ones_like(values)], axis=1)
        best = jnp.concatenate([top[...], top[...]], axis=1)
        weights = jnp.concatenate(
            [
                jnp.exp2((scores[2 * pair + side] - best) * scale).astype(jnp.bfloat16)
                for side in range(2)
            ],
            axis=1,
        )
        acc[...] += jnp.dot(weights, values, preferred_element_type=jnp.float32)
        return carry

    lax.fori_loop(0, pairs, mix_pair, 0)
    for head in range(heads):
        mixed = acc[head * tok : (head + 1) * tok, :]
        out[:, head * HD : (head + 1) * HD] = (mixed[:, :HD] / mixed[:, HD:]).astype(jnp.bfloat16)


def attend(info, query, seg_query, mine, other):
    tok, width = query.shape
    heads = width // HD
    blocks = WINDOW + 1
    vmem = pl.BlockSpec(memory_space=pltpu.VMEM)
    return pl.pallas_call(
        attention_kernel,
        out_shape=jax.ShapeDtypeStruct((tok, width), jnp.bfloat16),
        in_specs=[pl.BlockSpec(memory_space=pltpu.SMEM)] + [pl.BlockSpec()] * 4,
        out_specs=vmem,
        scratch_shapes=[
            pltpu.VMEM((blocks * 256, 2 * HD), jnp.bfloat16),
            pltpu.VMEM((blocks, 1, 256), jnp.float32),
            pltpu.VMEM((heads * tok, HD), jnp.bfloat16),
            pltpu.VMEM((blocks, heads * tok, 256), jnp.float32),
            pltpu.VMEM((heads * tok, 2 * HD), jnp.float32),
            pltpu.VMEM((heads * tok, HD), jnp.float32),
        ],
        compiler_params=pltpu.CompilerParams(vmem_limit_bytes=24 * 1024 * 1024),
        cost_estimate=pl.CostEstimate(
            flops=8 * tok * width * 2560,
            bytes_accessed=4 << 20,
            transcendentals=tok * heads * 2560,
        ),
        name="attend",
    )(info, query, seg_query, mine, other)


def select_kernel(core, low, high, out):
    out[0] = jnp.concatenate([low[...], high[...]], axis=1)


def select_columns(core, projector, tensor_n):
    width = projector.shape[0]
    lanes = projector.shape[1] // (4 * tensor_n)
    return pl.pallas_call(
        select_kernel,
        out_shape=jax.ShapeDtypeStruct((tensor_n, width, 2 * lanes), projector.dtype),
        grid_spec=pltpu.PrefetchScalarGridSpec(
            num_scalar_prefetch=1,
            grid=(tensor_n,),
            in_specs=[
                pl.BlockSpec((width, lanes), lambda i, core: (0, 4 * i + core[0])),
                pl.BlockSpec((width, lanes), lambda i, core: (0, 4 * i + 2 + core[0])),
            ],
            out_specs=pl.BlockSpec((1, width, 2 * lanes), lambda i, core: (i, 0, 0)),
        ),
        compiler_params=pltpu.CompilerParams(vmem_limit_bytes=48 * 1024 * 1024),
        cost_estimate=pl.CostEstimate(
            flops=0, bytes_accessed=8 * width * lanes * tensor_n, transcendentals=0
        ),
        name="select_columns",
    )(core, projector, projector)


def project_kernel(context, weight, out):
    out[0] = jnp.dot(context[...], weight[0], preferred_element_type=jnp.float32).astype(
        jnp.bfloat16
    )


def project(context, weight):
    tok, width = context.shape
    blocks, _, feats = weight.shape
    return pl.pallas_call(
        project_kernel,
        out_shape=jax.ShapeDtypeStruct((blocks, tok, feats), jnp.bfloat16),
        grid=(blocks,),
        in_specs=[
            pl.BlockSpec((tok, width), lambda i: (0, 0)),
            pl.BlockSpec((1, width, feats), lambda i: (i, 0, 0)),
        ],
        out_specs=pl.BlockSpec((1, tok, feats), lambda i: (i, 0, 0)),
        compiler_params=pltpu.CompilerParams(vmem_limit_bytes=16 * 1024 * 1024),
        cost_estimate=pl.CostEstimate(
            flops=2 * tok * width * feats * blocks,
            bytes_accessed=2 * width * feats * blocks,
            transcendentals=0,
        ),
        name="project",
    )(context, weight)


def student_kernel(place, ours_low, ours_high, theirs_low, theirs_high, weight, kept, sent):
    core = place[1]
    middle = ours_low.shape[1]

    def product(low, high):
        return jnp.dot(
            low[...], weight[:middle, :], preferred_element_type=jnp.float32
        ) + jnp.dot(high[...], weight[middle:, :], preferred_element_type=jnp.float32)

    own = product(ours_low, ours_high)
    partner = product(theirs_low, theirs_high)
    lanes = own.shape[1] // 2
    first = jnp.concatenate([own[:, :lanes], partner[:, :lanes]], axis=1)
    second = jnp.concatenate([own[:, lanes:], partner[:, lanes:]], axis=1)
    kept[...] = jnp.where(core == 0, first, second)
    sent[...] = jnp.where(core == 0, second, first).astype(jnp.bfloat16)


def gradient_kernel(place, ours_low, ours_high, theirs_low, theirs_high, mine, other, out):
    core = place[1]
    lanes = mine.shape[1] // 2
    first = jnp.where(core == 0, mine[...], other[...])
    second = jnp.where(core == 0, other[...], mine[...])
    own = jnp.concatenate([first[:, :lanes], second[:, :lanes]], axis=1)
    partner = jnp.concatenate([first[:, lanes:], second[:, lanes:]], axis=1)
    over_rows = (((0,), (0,)), ((), ()))
    count, width = out.shape[0] // 2, out.shape[1]
    for side, (ours, theirs) in enumerate(((ours_low, theirs_low), (ours_high, theirs_high))):
        for index in range(count):
            columns = slice(index * width, (index + 1) * width)
            out[side * count + index] = (
                lax.dot_general(ours[:, columns], own, over_rows, preferred_element_type=jnp.float32)
                + lax.dot_general(
                    theirs[:, columns], partner, over_rows, preferred_element_type=jnp.float32
                )
            ).astype(jnp.bfloat16)


def on_core(kernel, name, out_shape, flops, place, *args):
    vmem = pl.BlockSpec(memory_space=pltpu.VMEM)
    return pl.pallas_call(
        kernel,
        out_shape=out_shape,
        in_specs=[pl.BlockSpec(memory_space=pltpu.SMEM)] + [vmem] * len(args),
        out_specs=jax.tree.map(lambda _: vmem, out_shape),
        compiler_params=pltpu.CompilerParams(vmem_limit_bytes=32 * 1024 * 1024),
        cost_estimate=pl.CostEstimate(flops=flops, bytes_accessed=6 << 20, transcendentals=0),
        name=name,
    )(place, *args)


def shards(
    teacher_query,
    teacher_keyval,
    segment_ids,
    projector,
    owner_table,
    student_context,
    student_out_weight,
):
    group = lax.axis_index("group")
    seq = lax.axis_index("seq")
    high = seq // ZN
    query = teacher_query[0]
    tok = query.shape[0]
    slots, model = student_context.shape
    owners_n = 2 * ZN
    capacity = slots // owners_n
    half = model // 2
    feats = student_out_weight.shape[1] // 2
    tensor_n = model // (2 * feats)
    z_groups = [[h * ZN + z for z in range(ZN)] for h in range(2)]

    core_swap = [(0, 1), (1, 0)]
    both = ("group", "seq")
    all_pairs = partner_pairs(0) + partner_pairs(owners_n)

    keyval = teacher_keyval[0]
    seg_rows = segment_ids.astype(jnp.bfloat16).reshape(2, HD)
    seg_rows = jnp.concatenate([seg_rows, jnp.zeros((14, HD), jnp.bfloat16)], axis=0)
    passed = lax.ppermute(keyval, "group", [(0, 1)])
    piece = jnp.where(group == 0, keyval[:, :HD], passed[:, HD:])
    piece = jnp.concatenate([piece, seg_rows], axis=0)
    piece, projector = lax.optimization_barrier((piece, projector))
    projector = select_columns(group[None].astype(jnp.int32), projector, tensor_n)
    crossing = lax.dynamic_slice_in_dim(student_out_weight, (1 - group) * feats, feats, axis=1)
    crossing = jnp.concatenate([crossing, jnp.zeros((16, feats), crossing.dtype)], axis=0)
    exchanged = lax.ppermute(jnp.concatenate([crossing, piece], axis=1), both, all_pairs)
    lower = exchanged[:, feats:]
    crossing = exchanged[:256, :feats]
    ring = seq % ZN
    later = (jnp.arange(ZN, dtype=jnp.int32) >= ring) | (high == 0)
    pieces = jnp.where(later[:, None, None], piece[None], lower[None])
    ours = [
        lax.dynamic_slice_in_dim(
            student_context, group * half + side * (half // 2), half // 2, axis=1
        )
        for side in range(2)
    ]
    pieces, query, ours, student_out_weight, owner_table, projector = lax.optimization_barrier(
        (pieces, query, ours, student_out_weight, owner_table, projector)
    )
    mine = lax.all_to_all(
        pieces, "seq", split_axis=0, concat_axis=0, tiled=True, axis_index_groups=z_groups
    )
    below = lax.ppermute(
        lower,
        both,
        [
            (g * 2 * ZN + ZN + z, g * 2 * ZN + ZN + z + 1)
            for g in range(2)
            for z in range(ZN - 1)
        ],
    )
    mine = jnp.concatenate([mine, lower[None], below[None]], axis=0)

    theirs = [lax.ppermute(part, both, all_pairs) for part in ours]

    width = query.shape[1] // 2
    other_query = lax.ppermute(query[:, width:], "group", [(0, 1)])
    query = jnp.where(group == 0, query[:, :width], other_query)
    seg_query = segment_ids.astype(jnp.float32)[:, None]
    info = jnp.stack([seq, group]).astype(jnp.int32)

    weight = lax.dynamic_slice_in_dim(student_out_weight, group * feats, feats, axis=1)
    weight = jnp.where(group == high, weight, crossing)
    weight = jnp.broadcast_to(weight[None], (ZN,) + weight.shape)

    owners_all = owner_table[:, 0]
    owners = lax.dynamic_slice_in_dim(owners_all, seq * tok, tok)
    index = jnp.arange(tok, dtype=jnp.int32)
    ranks = jnp.sum(
        ((owners[:, None] == owners[None, :]) & (index[None, :] < index[:, None])).astype(
            jnp.int32
        ),
        axis=1,
    )
    slot = owners * capacity + ranks
    route = (jnp.arange(slots, dtype=jnp.int32)[:, None] == slot[None, :]).astype(jnp.bfloat16)
    pair_owners = jnp.stack([seq, (seq + ZN) % owners_n])
    counts = jnp.sum(
        (owners_all.reshape(owners_n, tok, 1) == pair_owners[None, None, :]).astype(jnp.int32),
        axis=1,
    )
    live = jnp.arange(capacity, dtype=jnp.int32)[None, :, None] < counts[:, None, :]
    scale = live.reshape(slots, 2, 1).astype(jnp.float32) / tok
    scale = jnp.broadcast_to(scale, (slots, 2, feats // 2)).reshape(slots, feats)
    mine, query, seg_query, info, weight, route, scale, theirs[0] = (
        lax.optimization_barrier(
            (mine, query, seg_query, info, weight, route, scale, theirs[0])
        )
    )
    other = lax.ppermute(mine, "group", core_swap)
    weight = lax.all_to_all(
        weight, "seq", split_axis=0, concat_axis=0, tiled=True, axis_index_groups=z_groups
    ).reshape(half, feats)
    context = attend(info, query, seg_query, mine, other)
    place = info

    other_context = lax.ppermute(context, "group", core_swap)
    context = jnp.where(
        group == 0,
        jnp.concatenate([context, other_context], axis=1),
        jnp.concatenate([other_context, context], axis=1),
    )
    partial = project(context, projector)
    partial, theirs[1] = lax.optimization_barrier((partial, theirs[1]))
    partial = lax.all_to_all(partial, "tensor", split_axis=0, concat_axis=0, tiled=True)
    output, given = on_core(
        student_kernel,
        "student",
        [
            jax.ShapeDtypeStruct((slots, feats), jnp.float32),
            jax.ShapeDtypeStruct((slots, feats), jnp.bfloat16),
        ],
        4 * slots * half * feats,
        place,
        *ours,
        *theirs,
        weight,
    )
    output = output + lax.ppermute(given, "group", core_swap).astype(jnp.float32)
    partial, output = lax.optimization_barrier((partial, output))
    target = jnp.sum(partial.astype(jnp.float32), axis=0).astype(jnp.bfloat16)

    routed = jnp.dot(route, target, preferred_element_type=jnp.float32).astype(jnp.bfloat16)
    routed = routed.reshape(2, ZN, capacity, feats)
    lanes = feats // 2
    routed = jnp.stack(
        [
            jnp.concatenate([routed[0, :, :, :lanes], routed[1, :, :, :lanes]], axis=-1),
            jnp.concatenate([routed[1, :, :, lanes:], routed[0, :, :, lanes:]], axis=-1),
        ]
    ).reshape(owners_n, capacity, feats)
    routed = lax.all_to_all(
        routed, "seq", split_axis=0, concat_axis=0, tiled=True
    ).reshape(slots, feats)
    residual = ((output - routed.astype(jnp.float32)) * scale).astype(jnp.bfloat16)

    gradient = on_core(
        gradient_kernel,
        "gradient",
        jax.ShapeDtypeStruct((ZN, half // ZN, feats), jnp.bfloat16),
        4 * slots * half * feats,
        place,
        *ours,
        *theirs,
        residual,
        lax.ppermute(residual, "group", core_swap),
    )
    gradient = lax.all_to_all(
        gradient,
        "seq",
        split_axis=0,
        concat_axis=0,
        tiled=True,
        axis_index_groups=z_groups,
    )
    gradient = jnp.sum(gradient.astype(jnp.float32), axis=0).astype(jnp.bfloat16)

    straight = lax.ppermute(gradient, both, [(z, 2 * ZN + z) for z in range(ZN)])
    crossed = lax.ppermute(
        gradient,
        both,
        [(ZN + z, 2 * ZN + z) for z in range(ZN)] + [(2 * ZN + z, 3 * ZN + z) for z in range(ZN)],
    )
    whole = jnp.where(
        high == 0,
        jnp.concatenate([straight, crossed], axis=1),
        jnp.concatenate([crossed, gradient], axis=1),
    )
    return jnp.where(group == 1, whole.astype(jnp.float32), 0.0)[None]


def solution(mesh):
    placed = (
        P("group", "seq", "tensor"),
        P("group", "seq", "tensor"),
        P("seq"),
        P("tensor", None),
        P(),
        P("seq", None),
        P("seq", "tensor"),
    )
    return jax.shard_map(
        shards, mesh=mesh, in_specs=placed, out_specs=P("group", "seq", "tensor"), check_vma=False
    )
```

time: 171 us -> 164 us (0.959)
  waiting for transfers between devices: 53 us -> 37.5 us
  blocking collectives: 32.4 us -> 46 us
  starting transfers between devices: 44.3 us -> 38.1 us
  Pallas kernels: 12.1 us -> 15.7 us
    all_to_all x0 -> x1, blocking collectives: none -> 15.1 us  [shards(): lax.all_to_all(routed, 'seq', split_axis=0, concat_axis=0, tiled=True)]
    all_to_all x2 -> x1, starting transfers between devices: 17.6 us -> 6.67 us  [shards(): lax.all_to_all(pieces, 'seq', split_axis=0, concat_axis=0, tiled=True, ax...]
    ppermute x10 -> x11, waiting for transfers between devices: 26.2 us -> 17.9 us  [the longest x2 7.23 us: shards(): theirs = [lax.ppermute(part, both, all_pairs) for part in ours]]
    all_to_all x1, waiting for transfers between devices: 9.12 us -> 3.48 us  [shards(): lax.all_to_all(weight, 'seq', split_axis=0, concat_axis=0, tiled=True, ax...]
    ppermute x10 -> x11, starting transfers between devices: 17.4 us -> 22.4 us  [the longest x2 4.59 us: shards(): theirs = [lax.ppermute(part, both, all_pairs) for part in ours]]
    pallas_call x3 -> x4, Pallas kernels: 8.75 us -> 11.9 us  [the longest x1 4.8 us: select_columns(): pl.pallas_call(select_kernel, out_shape=jax.ShapeDtypeStruct((tensor_n, w...]
    all_to_all x1, waiting for transfers between devices: 9.35 us -> 6.94 us  [shards(): lax.all_to_all(partial, 'tensor', split_axis=0, concat_axis=0, tiled=True)]
    another operation x2, other arithmetic: 2.19 us -> 0.05 us  [shards(): jnp.stack([jnp.concatenate([routed[0, :, :, :lanes], routed[1, :, :, :lan...]
  transfers between devices with their start and end apart: 15 -> 15, of which waited for: 9 -> 11; matrix products, arithmetic and copies ran while one was open for 8% -> 8% of each run, Pallas kernels for 5% -> 8%
where the time goes in v4:
time: 164 us; the launch traced here: 163 us
  blocking collectives  46 us (28%)
  starting transfers between devices  38.1 us (23%)
  waiting for transfers between devices  37.5 us (23%)
  Pallas kernels  15.7 us (10%)
  local copies, waits for them, and re-layouts  12.3 us (8%)
  other arithmetic  12 us (7%)
    all_to_all x1, blocking collectives, shards(): lax.all_to_all(gradient, 'seq', split_axis=0, concat_axis=0, tiled=True,...  30.9 us
    all_to_all x1, blocking collectives, shards(): lax.all_to_all(routed, 'seq', split_axis=0, concat_axis=0, tiled=True)  15.1 us
    all_to_all x1, waiting for transfers between devices, shards(): lax.all_to_all(pieces, 'seq', split_axis=0, concat_axis=0, tiled=True, ax...  8.04 us
    ppermute x2, waiting for transfers between devices, shards(): theirs = [lax.ppermute(part, both, all_pairs) for part in ours]  7.23 us
    all_to_all x1, waiting for transfers between devices, shards(): lax.all_to_all(partial, 'tensor', split_axis=0, concat_axis=0, tiled=True)  6.94 us
    all_to_all x1, starting transfers between devices, shards(): lax.all_to_all(pieces, 'seq', split_axis=0, concat_axis=0, tiled=True, ax...  6.67 us
    unnamed x19, local copies, waits for them, and re-layouts  5.99 us
    ppermute x1, waiting for transfers between devices, shards(): lax.ppermute(gradient, both, [(ZN + z, 2 * ZN + z) for z in range(ZN)] +...  5.24 us
  transfers between devices with their start and end apart: 15, of which 11 were waited for; matrix products, arithmetic and copies ran while one was open for 8% of the time, Pallas kernels for 8%

profile of v4, /device:TPU:1, one launch (start us, length us, event | category | flops | bytes accessed | tf_op | source)
XLA Modules:
  0.0 163.0 jit_solution(16276735594935331996)
XLA Ops:
  0.0 1.3 collective-permute-start
  3.3 2.2 %collective-permute-done = bf16[256,256]{1,0:T(8,128)(2,1)S(1)} collective-permute-done((bf16[256,256]{1,0:T(8,128)(2,1)}, bf16[256,256]{1,0:T(8,128)(2,1)S(1)}, u32[]{:S(2)}, u32[]{:S(2)}) %collective-permute-start) | collective-permute-done | bytes 131104 | tf_op jit(solution)/shard_map/ppermute | solution.py:277
  6.5 1.7 %collective-permute-start.1 = (bf16[272,384]{1,0:T(8,128)(2,1)S(1)}, bf16[272,384]{1,0:T(8,128)(2,1)S(1)}, u32[]{:S(2)}, u32[]{:S(2)}) collective-permute-start(bf16[272,384]{1,0:T(8,128)(2,1)S(1)} %fusion.5), channel_id=1, source_target_pairs={{0,8},{1,9},{2,10},{3,11},{4,12},{5,13},{6,14},{7,15},{8,0},{9,1},... | collective-permute-start | bytes 626696 | tf_op jit(solution)/shard_map/ppermute | solution.py:284
  8.3 1.5 constant_dynamic-slice_fusion.1
  9.8 4.8 %select_columns.1.weight = bf16[8,1024,256]{2,1,0:T(8,128)(2,1)S(1)} custom-call(s32[1]{0:T(128)} %bitcast.3.core, bf16[1024,4096]{1,0:T(8,128)(2,1)} %high, bf16[1024,4096]{1,0:T(8,128)(2,1)} %high), custom_call_target="tpu_custom_call" | custom-call | bytes 8388608 | tf_op jit(solution)/shard_map/select_columns/pallas_call | solution.py:149
  14.6 1.9 %copy-done = bf16[8,1024,256]{2,1,0:T(8,128)(2,1)} copy-done((bf16[8,1024,256]{2,1,0:T(8,128)(2,1)}, bf16[8,1024,256]{2,1,0:T(8,128)(2,1)S(1)}, u32[]{:S(2)}) %copy-start) | copy-done | bytes 4194328
  19.6 3.0 %collective-permute-start.4 = (bf16[384,1024]{1,0:T(8,128)(2,1)S(1)}, bf16[384,1024]{1,0:T(8,128)(2,1)S(1)}, u32[]{:S(2)}, u32[]{:S(2)}) collective-permute-start(bf16[384,1024]{1,0:T(8,128)(2,1)S(1)} %get-tuple-element.34.ours_low), channel_id=1, source_target_pairs={{0,8},{1,9},{2,10},{3,11},{4,12},{5,13},{6,14},{7,15},{8,0},{9,1},... | collective-permute-start | bytes 2359304 | tf_op jit(solution)/shard_map/ppermute | solution.py:313
  22.7 6.7 %all-to-all-start = ((bf16[8,272,128]{2,1,0:T(8,128)(2,1)}), bf16[8,272,128]{2,1,0:T(8,128)(2,1)S(1)}, u32[]{:S(2)}, u32[]{:S(2)}) async-start(bf16[8,272,128]{2,1,0:T(8,128)(2,1)} %broadcast_select_fusion), calls=%async_computation | async-start | bytes 1114112 | tf_op jit(solution)/shard_map/all_to_all | solution.py:299
  30.8 1.3 collective-permute-start.3
  36.0 1.7 %slice_select_fusion.query = bf16[256,512]{1,0:T(8,128)(2,1)} fusion(bf16[256,512]{1,0:T(8,128)(2,1)S(1)} %collective-permute-done.3, bf16[256,1024]{1,0:T(8,128)(2,1)} %bitcast.50, pred[]{:T(512)S(6)} %eq.61), kind=kLoop, calls=%fused_computation.17 | loop fusion | flops 131072 | bytes 786433 | tf_op jit(solution)/shard_map/jit(_where)/select_n | solution.py:317
  37.7 8.0 %all-to-all-done = bf16[8,272,128]{2,1,0:T(8,128)(2,1)S(1)} async-done(((bf16[8,272,128]{2,1,0:T(8,128)(2,1)}), bf16[8,272,128]{2,1,0:T(8,128)(2,1)S(1)}, u32[]{:S(2)}, u32[]{:S(2)}) %all-to-all-start) | async-done | bytes 557088 | tf_op jit(solution)/shard_map/all_to_all | solution.py:299
  45.7 1.9 %pad_maximum_fusion.mine = bf16[10,272,128]{2,1,0:T(8,128)(2,1)} fusion(bf16[1,272,128]{2,1,0:T(8,128)(2,1)} %bitcast.5, bf16[1,272,128]{2,1,0:T(8,128)(2,1)} %get-tuple-element.53, bf16[8,272,128]{2,1,0:T(8,128)(2,1)S(1)} %all-to-all-done), kind=kLoop, calls=%fused_computation.1 | loop fusion | flops 696320 | bytes 1392640 | tf_op jit(solution)/shard_map/concatenate | solution.py:311
  48.6 3.6 %all-to-all-start.2 = ((bf16[8,256,256]{2,1,0:T(8,128)(2,1)}), bf16[8,256,256]{2,1,0:T(8,128)(2,1)S(1)}, u32[]{:S(2)}, u32[]{:S(2)}) async-start(bf16[8,256,256]{2,1,0:T(8,128)(2,1)} %broadcast_in_dim.76), calls=%async_computation.2 | async-start | bytes 2097152 | tf_op jit(solution)/shard_map/all_to_all | solution.py:350
  52.2 2.9 %collective-permute-start.5 = (bf16[10,272,128]{2,1,0:T(8,128)(2,1)}, bf16[10,272,128]{2,1,0:T(8,128)(2,1)}, u32[]{:S(2)}, u32[]{:S(2)}) collective-permute-start(bf16[10,272,128]{2,1,0:T(8,128)(2,1)} %pad_maximum_fusion.mine), channel_id=1, source_target_pairs={{0,128},{128,0},{1,129},{129,1},{2,130},{130,2},{3,131},{131,3},{4... | collective-permute-start | bytes 2088968 | tf_op jit(solution)/shard_map/ppermute | solution.py:349
  55.0 1.6 collective-permute-start.7
  57.2 1.3 copy-done.3
  59.4 3.8 %attend.1 = bf16[256,512]{1,0:T(8,128)(2,1)S(1)} custom-call(s32[2]{0:T(128)S(1)} %pad_add_fusion.info.place, bf16[256,512]{1,0:T(8,128)(2,1)S(1)} %copy-done.4, f32[256,1]{1,0:T(8,128)S(1)} %copy.10.seg_query, bf16[10,272,128]{2,1,0:T(8,128)(2,1)S(1)} %copy-done.3, bf16[10,272,128]{2,1,0:T(8,128)(2,1)} %collective-permute-done.5.other), custom_call_target="tpu_custom_call" | custom-call | flops 2684354560 | bytes 4194304 | tf_op jit(solution)/shard_map/attend/pallas_call | solution.py:119
  65.0 2.5 %project.1 = bf16[8,256,256]{2,1,0:T(8,128)(2,1)S(1)} custom-call(bf16[256,1024]{1,0:T(8,128)(2,1)S(1)} %maximum_select_fusion.context, bf16[8,1024,256]{2,1,0:T(8,128)(2,1)S(1)} %copy-done.1), custom_call_target="tpu_custom_call" | custom-call | flops 1073741824 | bytes 4194304 | tf_op jit(solution)/shard_map/project/pallas_call | solution.py:178
  68.5 7.2 %collective-permute-done.7.theirs_high = bf16[384,1024]{1,0:T(8,128)(2,1)} collective-permute-done((bf16[384,1024]{1,0:T(8,128)(2,1)S(1)}, bf16[384,1024]{1,0:T(8,128)(2,1)}, u32[]{:S(2)}, u32[]{:S(2)}) %collective-permute-start.7) | collective-permute-done | bytes 786464 | tf_op jit(solution)/shard_map/ppermute | solution.py:313
  75.7 3.5 %all-to-all-done.2 = bf16[8,256,256]{2,1,0:T(8,128)(2,1)S(1)} async-done(((bf16[8,256,256]{2,1,0:T(8,128)(2,1)}), bf16[8,256,256]{2,1,0:T(8,128)(2,1)S(1)}, u32[]{:S(2)}, u32[]{:S(2)}) %all-to-all-start.2) | async-done | bytes 1048608 | tf_op jit(solution)/shard_map/all_to_all | solution.py:350
  79.2 5.0 %all-to-all-start.1 = ((bf16[8,256,256]{2,1,0:T(8,128)(2,1)}), bf16[8,256,256]{2,1,0:T(8,128)(2,1)}, u32[]{:S(2)}, u32[]{:S(2)}) async-start(bf16[8,256,256]{2,1,0:T(8,128)(2,1)} %copy-done.2), calls=%async_computation.1 | async-start | bytes 2097152 | tf_op jit(solution)/shard_map/all_to_all | solution.py:364
  84.3 2.1 %student.1 = (f32[384,256]{1,0:T(8,128)S(1)}, bf16[384,256]{1,0:T(8,128)(2,1)S(1)}) custom-call(s32[2]{0:T(128)S(1)} %pad_add_fusion.info.place, bf16[384,1024]{1,0:T(8,128)(2,1)S(1)} %get-tuple-element.34.ours_low, bf16[384,1024]{1,0:T(8,128)(2,1)S(1)} %get-tuple-element.36.ours_high, bf16[384,1024]{1,0:T(8,128)(2,1)S(1)} %collective-permute-done.4.theirs_low, ...), custom_call_target="tpu_custom_call" | custom-call | flops 805306368 | bytes 6291456 | tf_op jit(solution)/shard_map/student/pallas_call | solution.py:237
  86.4 2.9 %collective-permute-start.8 = (bf16[384,256]{1,0:T(8,128)(2,1)S(1)}, bf16[384,256]{1,0:T(8,128)(2,1)S(1)}, u32[]{:S(2)}, u32[]{:S(2)}) collective-permute-start(bf16[384,256]{1,0:T(8,128)(2,1)S(1)} %get-tuple-element.46), channel_id=1, source_target_pairs={{0,128},{128,0},{1,129},{129,1},{2,130},{130,2},{3,131},{131,3},{4... | collective-permute-start | bytes 589832 | tf_op jit(solution)/shard_map/ppermute | solution.py:378
  90.4 6.9 %all-to-all-done.1 = bf16[8,256,256]{2,1,0:T(8,128)(2,1)} async-done(((bf16[8,256,256]{2,1,0:T(8,128)(2,1)}), bf16[8,256,256]{2,1,0:T(8,128)(2,1)}, u32[]{:S(2)}, u32[]{:S(2)}) %all-to-all-start.1) | async-done | bytes 1048608 | tf_op jit(solution)/shard_map/all_to_all | solution.py:364
  97.4 1.4 reduce_sum.44
  100.0 15.1 %all_to_all.25 = bf16[16,24,256]{2,1,0:T(8,128)(2,1)S(1)} all-to-all(bf16[16,24,256]{2,1,0:T(8,128)(2,1)S(1)} %bitcast.47), channel_id=1, replica_groups=mesh['group'=2,'tensor'=8,'seq'=16] {'seq'}, dimensions={0} | all-to-all | bytes 393216 | tf_op jit(solution)/shard_map/all_to_all | solution.py:391
  115.2 3.3 %collective-permute-start.9 = (bf16[384,256]{1,0:T(8,128)(2,1)S(1)}, bf16[384,256]{1,0:T(8,128)(2,1)S(1)}, u32[]{:S(2)}, u32[]{:S(2)}) collective-permute-start(bf16[384,256]{1,0:T(8,128)(2,1)S(1)} %fusion.2.mine), channel_id=1, source_target_pairs={{0,128},{128,0},{1,129},{129,1},{2,130},{130,2},{3,131},{131,3},{4... | collective-permute-start | bytes 589832 | tf_op jit(solution)/shard_map/ppermute | solution.py:405
  119.6 2.5 %gradient.1 = bf16[8,256,256]{2,1,0:T(8,128)(2,1)S(1)} custom-call(s32[2]{0:T(128)S(1)} %pad_add_fusion.info.place, bf16[384,1024]{1,0:T(8,128)(2,1)S(1)} %get-tuple-element.34.ours_low, bf16[384,1024]{1,0:T(8,128)(2,1)S(1)} %get-tuple-element.36.ours_high, bf16[384,1024]{1,0:T(8,128)(2,1)S(1)} %collective-permute-done.4.theirs_low, ...), custom_call_target="tpu_custom_call" | custom-call | flops 805306368 | bytes 6291456 | tf_op jit(solution)/shard_map/gradient/pallas_call | solution.py:237
  122.0 30.9 %all_to_all.26 = bf16[8,256,256]{2,1,0:T(8,128)(2,1)S(1)} all-to-all(bf16[8,256,256]{2,1,0:T(8,128)(2,1)S(1)} %gradient.1), channel_id=1, replica_groups={{0,1,2,3,4,5,6,7},{8,9,10,11,12,13,14,15},{16,17,18,19,20,21,22,23},{24..., dimensions={0} | all-to-all | bytes 2097152 | tf_op jit(solution)/shard_map/all_to_all | solution.py:407
  153.1 1.3 collective-permute-start.10
  154.4 1.9 %collective-permute-start.11 = (bf16[256,256]{1,0:T(8,128)(2,1)S(1)}, bf16[256,256]{1,0:T(8,128)(2,1)S(1)}, u32[]{:S(2)}, u32[]{:S(2)}) collective-permute-start(bf16[256,256]{1,0:T(8,128)(2,1)S(1)} %reduce_sum.45), channel_id=1, source_target_pairs={{8,128},{9,129},{10,130},{11,131},{12,132},{13,133},{14,134},{15,1... | collective-permute-start | bytes 393224 | tf_op jit(solution)/shard_map/ppermute | solution.py:418
  156.9 5.2 %collective-permute-done.11 = bf16[256,256]{1,0:T(8,128)(2,1)S(1)} collective-permute-done((bf16[256,256]{1,0:T(8,128)(2,1)S(1)}, bf16[256,256]{1,0:T(8,128)(2,1)S(1)}, u32[]{:S(2)}, u32[]{:S(2)}) %collective-permute-start.11) | collective-permute-done | bytes 131104 | tf_op jit(solution)/shard_map/ppermute | solution.py:418
  (66 shorter events, 21.8 us)
Async XLA Ops:
  0.0 5.6 %collective-permute-start = (bf16[256,256]{1,0:T(8,128)(2,1)}, bf16[256,256]{1,0:T(8,128)(2,1)S(1)}, u32[]{:S(2)}, u32[]{:S(2)}) collective-permute-start(bf16[256,256]{1,0:T(8,128)(2,1)} %bitcast.54), channel_id=1, source_target_pairs={{0,128},{1,129},{2,130},{3,131},{4,132},{5,133},{6,134},{7,135},{8... | collective-permute-start | bytes 393224 | tf_op jit(solution)/shard_map/ppermute | solution.py:277
  6.5 10.0 %collective-permute-start.1 = (bf16[272,384]{1,0:T(8,128)(2,1)S(1)}, bf16[272,384]{1,0:T(8,128)(2,1)S(1)}, u32[]{:S(2)}, u32[]{:S(2)}) collective-permute-start(bf16[272,384]{1,0:T(8,128)(2,1)S(1)} %fusion.5), channel_id=1, source_target_pairs={{0,8},{1,9},{2,10},{3,11},{4,12},{5,13},{6,14},{7,15},{8,0},{9,1},... | collective-permute-start | bytes 626696 | tf_op jit(solution)/shard_map/ppermute | solution.py:284
  9.8 9.7 %copy-start.8 = (s32[4096,1]{0,1:T(1,128)S(1)}, s32[4096,1]{0,1:T(1,128)}, u32[]{:S(2)}) copy-start(s32[4096,1]{0,1:T(1,128)} %param.11) | copy-start | bytes 49156
  9.8 20.3 %copy-start.6 = (bf16[1,256,1024]{2,1,0:T(8,128)(2,1)S(1)}, bf16[1,256,1024]{2,1,0:T(8,128)(2,1)}, u32[]{:S(2)}) copy-start(bf16[1,256,1024]{2,1,0:T(8,128)(2,1)} %param.7) | copy-start | bytes 1572868
  14.6 2.0 %copy-start = (bf16[8,1024,256]{2,1,0:T(8,128)(2,1)}, bf16[8,1024,256]{2,1,0:T(8,128)(2,1)S(1)}, u32[]{:S(2)}) copy-start(bf16[8,1024,256]{2,1,0:T(8,128)(2,1)S(1)} %select_columns.1.weight) | copy-start | bytes 12582916
  16.6 2.9 %copy-start.7 = (bf16[272,384]{1,0:T(8,128)(2,1)}, bf16[272,384]{1,0:T(8,128)(2,1)S(1)}, u32[]{:S(2)}) copy-start(bf16[272,384]{1,0:T(8,128)(2,1)S(1)} %collective-permute-done.1) | copy-start | bytes 626692
  17.2 20.4 %collective-permute-start.2 = (bf16[272,128]{1,0:T(8,128)(2,1)S(1)}, bf16[272,128]{1,0:T(8,128)(2,1)}, u32[]{:S(2)}, u32[]{:S(2)}) collective-permute-start(bf16[272,128]{1,0:T(8,128)(2,1)S(1)} %get-tuple-element.54), channel_id=1, source_target_pairs={{8,9},{9,10},{10,11},{11,12},{12,13},{13,14},{14,15},{136,137},{13... | collective-permute-start | bytes 208904 | tf_op jit(solution)/shard_map/ppermute | solution.py:302
  19.6 27.9 %collective-permute-start.4 = (bf16[384,1024]{1,0:T(8,128)(2,1)S(1)}, bf16[384,1024]{1,0:T(8,128)(2,1)S(1)}, u32[]{:S(2)}, u32[]{:S(2)}) collective-permute-start(bf16[384,1024]{1,0:T(8,128)(2,1)S(1)} %get-tuple-element.34.ours_low), channel_id=1, source_target_pairs={{0,8},{1,9},{2,10},{3,11},{4,12},{5,13},{6,14},{7,15},{8,0},{9,1},... | collective-permute-start | bytes 2359304 | tf_op jit(solution)/shard_map/ppermute | solution.py:313
  22.7 23.0 %all-to-all-start = ((bf16[8,272,128]{2,1,0:T(8,128)(2,1)}), bf16[8,272,128]{2,1,0:T(8,128)(2,1)S(1)}, u32[]{:S(2)}, u32[]{:S(2)}) async-start(bf16[8,272,128]{2,1,0:T(8,128)(2,1)} %broadcast_select_fusion), calls=%async_computation | async-start | bytes 1114112 | tf_op jit(solution)/shard_map/all_to_all | solution.py:299
  30.8 5.2 %collective-permute-start.3 = (bf16[256,512]{1,0:T(8,128)(2,1)}, bf16[256,512]{1,0:T(8,128)(2,1)S(1)}, u32[]{:S(2)}, u32[]{:S(2)}) collective-permute-start(bf16[256,512]{1,0:T(8,128)(2,1)} %slice.34), channel_id=1, source_target_pairs={{0,128},{1,129},{2,130},{3,131},{4,132},{5,133},{6,134},{7,135},{8... | collective-permute-start | bytes 786440 | tf_op jit(solution)/shard_map/ppermute | solution.py:316
  48.6 30.6 %all-to-all-start.2 = ((bf16[8,256,256]{2,1,0:T(8,128)(2,1)}), bf16[8,256,256]{2,1,0:T(8,128)(2,1)S(1)}, u32[]{:S(2)}, u32[]{:S(2)}) async-start(bf16[8,256,256]{2,1,0:T(8,128)(2,1)} %broadcast_in_dim.76), calls=%async_computation.2 | async-start | bytes 2097152 | tf_op jit(solution)/shard_map/all_to_all | solution.py:350
  52.2 5.0 %collective-permute-start.5 = (bf16[10,272,128]{2,1,0:T(8,128)(2,1)}, bf16[10,272,128]{2,1,0:T(8,128)(2,1)}, u32[]{:S(2)}, u32[]{:S(2)}) collective-permute-start(bf16[10,272,128]{2,1,0:T(8,128)(2,1)} %pad_maximum_fusion.mine), channel_id=1, source_target_pairs={{0,128},{128,0},{1,129},{129,1},{2,130},{130,2},{3,131},{131,3},{4... | collective-permute-start | bytes 2088968 | tf_op jit(solution)/shard_map/ppermute | solution.py:349
  55.0 20.7 %collective-permute-start.7 = (bf16[384,1024]{1,0:T(8,128)(2,1)S(1)}, bf16[384,1024]{1,0:T(8,128)(2,1)}, u32[]{:S(2)}, u32[]{:S(2)}) collective-permute-start(bf16[384,1024]{1,0:T(8,128)(2,1)S(1)} %get-tuple-element.36.ours_high), channel_id=1, source_target_pairs={{0,8},{1,9},{2,10},{3,11},{4,12},{5,13},{6,14},{7,15},{8,0},{9,1},... | collective-permute-start | bytes 2359304 | tf_op jit(solution)/shard_map/ppermute | solution.py:313
  56.7 8.3 %copy-start.1 = (bf16[8,1024,256]{2,1,0:T(8,128)(2,1)S(1)}, bf16[8,1024,256]{2,1,0:T(8,128)(2,1)}, u32[]{:S(2)}) copy-start(bf16[8,1024,256]{2,1,0:T(8,128)(2,1)} %copy-done) | copy-start | bytes 12582916
  57.2 1.3 copy-start.3
  58.5 0.9 copy-start.4
  63.2 1.6 collective-permute-start.6
  67.5 1.0 copy-start.2
  79.2 18.1 %all-to-all-start.1 = ((bf16[8,256,256]{2,1,0:T(8,128)(2,1)}), bf16[8,256,256]{2,1,0:T(8,128)(2,1)}, u32[]{:S(2)}, u32[]{:S(2)}) async-start(bf16[8,256,256]{2,1,0:T(8,128)(2,1)} %copy-done.2), calls=%async_computation.1 | async-start | bytes 2097152 | tf_op jit(solution)/shard_map/all_to_all | solution.py:364
  86.4 28.7 %copy-start.5 = (f32[48,8,2,128]{3,1,2,0:T(8,128)S(1)}, f32[48,8,2,128]{3,1,2,0:T(8,128)}, u32[]{:S(2)}) copy-start(f32[48,8,2,128]{3,1,2,0:T(8,128)} %copy.13) | copy-start | bytes 1179652
  86.4 4.0 %collective-permute-start.8 = (bf16[384,256]{1,0:T(8,128)(2,1)S(1)}, bf16[384,256]{1,0:T(8,128)(2,1)S(1)}, u32[]{:S(2)}, u32[]{:S(2)}) collective-permute-start(bf16[384,256]{1,0:T(8,128)(2,1)S(1)} %get-tuple-element.46), channel_id=1, source_target_pairs={{0,128},{128,0},{1,129},{129,1},{2,130},{130,2},{3,131},{131,3},{4... | collective-permute-start | bytes 589832 | tf_op jit(solution)/shard_map/ppermute | solution.py:378
  115.2 4.4 %collective-permute-start.9 = (bf16[384,256]{1,0:T(8,128)(2,1)S(1)}, bf16[384,256]{1,0:T(8,128)(2,1)S(1)}, u32[]{:S(2)}, u32[]{:S(2)}) collective-permute-start(bf16[384,256]{1,0:T(8,128)(2,1)S(1)} %fusion.2.mine), channel_id=1, source_target_pairs={{0,128},{128,0},{1,129},{129,1},{2,130},{130,2},{3,131},{131,3},{4... | collective-permute-start | bytes 589832 | tf_op jit(solution)/shard_map/ppermute | solution.py:405
  153.1 3.9 %collective-permute-start.10 = (bf16[256,256]{1,0:T(8,128)(2,1)S(1)}, bf16[256,256]{1,0:T(8,128)(2,1)S(1)}, u32[]{:S(2)}, u32[]{:S(2)}) collective-permute-start(bf16[256,256]{1,0:T(8,128)(2,1)S(1)} %reduce_sum.45), channel_id=1, source_target_pairs={{0,128},{1,129},{2,130},{3,131},{4,132},{5,133},{6,134},{7,135},{1... | collective-permute-start | bytes 393224 | tf_op jit(solution)/shard_map/ppermute | solution.py:417
  154.4 7.8 %collective-permute-start.11 = (bf16[256,256]{1,0:T(8,128)(2,1)S(1)}, bf16[256,256]{1,0:T(8,128)(2,1)S(1)}, u32[]{:S(2)}, u32[]{:S(2)}) collective-permute-start(bf16[256,256]{1,0:T(8,128)(2,1)S(1)} %reduce_sum.45), channel_id=1, source_target_pairs={{8,128},{9,129},{10,130},{11,131},{12,132},{13,133},{14,134},{15,1... | collective-permute-start | bytes 393224 | tf_op jit(solution)/shard_map/ppermute | solution.py:418

commit v5 on v4

--- a/solution.py
+++ b/solution.py
@@ -139,59 +139,35 @@
     )(info, query, seg_query, mine, other)
 
 
-def select_kernel(core, low, high, out):
-    out[0] = jnp.concatenate([low[...], high[...]], axis=1)
-
-
-def select_columns(core, projector, tensor_n):
-    width = projector.shape[0]
-    lanes = projector.shape[1] // (4 * tensor_n)
+def project_kernel(core, context, low, high, out):
+    weight = jnp.concatenate([low[...], high[...]], axis=1)
+    out[0] = jnp.dot(context[...], weight, preferred_element_type=jnp.float32).astype(jnp.bfloat16)
+
+
+def project(core, context, projector, tensor_n):
+    tok, width = context.shape
+    feats = projector.shape[1] // (4 * tensor_n)
     return pl.pallas_call(
-        select_kernel,
-        out_shape=jax.ShapeDtypeStruct((tensor_n, width, 2 * lanes), projector.dtype),
+        project_kernel,
+        out_shape=jax.ShapeDtypeStruct((tensor_n, tok, 2 * feats), jnp.bfloat16),
         grid_spec=pltpu.PrefetchScalarGridSpec(
             num_scalar_prefetch=1,
             grid=(tensor_n,),
             in_specs=[
-                pl.BlockSpec((width, lanes), lambda i, core: (0, 4 * i + core[0])),
-                pl.BlockSpec((width, lanes), lambda i, core: (0, 4 * i + 2 + core[0])),
+                pl.BlockSpec((tok, width), lambda i, core: (0, 0)),
+                pl.BlockSpec((width, feats), lambda i, core: (0, 4 * i + core[0])),
+                pl.BlockSpec((width, feats), lambda i, core: (0, 4 * i + 2 + core[0])),
             ],
-            out_specs=pl.BlockSpec((1, width, 2 * lanes), lambda i, core: (i, 0, 0)),
+            out_specs=pl.BlockSpec((1, tok, 2 * feats), lambda i, core: (i, 0, 0)),
         ),
-        compiler_params=pltpu.CompilerParams(vmem_limit_bytes=48 * 1024 * 1024),
-        cost_estimate=pl.CostEstimate(
-            flops=0, bytes_accessed=8 * width * lanes * tensor_n, transcendentals=0
-        ),
-        name="select_columns",
-    )(core, projector, projector)
-
-
-def project_kernel(context, weight, out):
-    out[0] = jnp.dot(context[...], weight[0], preferred_element_type=jnp.float32).astype(
-        jnp.bfloat16
-    )
-
-
-def project(context, weight):
-    tok, width = context.shape
-    blocks, _, feats = weight.shape
-    return pl.pallas_call(
-        project_kernel,
-        out_shape=jax.ShapeDtypeStruct((blocks, tok, feats), jnp.bfloat16),
-        grid=(blocks,),
-        in_specs=[
-            pl.BlockSpec((tok, width), lambda i: (0, 0)),
-            pl.BlockSpec((1, width, feats), lambda i: (i, 0, 0)),
-        ],
-        out_specs=pl.BlockSpec((1, tok, feats), lambda i: (i, 0, 0)),
         compiler_params=pltpu.CompilerParams(vmem_limit_bytes=16 * 1024 * 1024),
         cost_estimate=pl.CostEstimate(
-            flops=2 * tok * width * feats * blocks,
-            bytes_accessed=2 * width * feats * blocks,
+            flops=4 * tok * width * feats * tensor_n,
+            bytes_accessed=4 * width * feats * tensor_n,
             transcendentals=0,
         ),
         name="project",
-    )(context, weight)
+    )(core, context, projector, projector)
 
 
 def student_kernel(place, ours_low, ours_high, theirs_low, theirs_high, weight, kept, sent):
@@ -277,8 +253,6 @@
     passed = lax.ppermute(keyval, "group", [(0, 1)])
     piece = jnp.where(group == 0, keyval[:, :HD], passed[:, HD:])
     piece = jnp.concatenate([piece, seg_rows], axis=0)
-    piece, projector = lax.optimization_barrier((piece, projector))
-    projector = select_columns(group[None].astype(jnp.int32), projector, tensor_n)
     crossing = lax.dynamic_slice_in_dim(student_out_weight, (1 - group) * feats, feats, axis=1)
     crossing = jnp.concatenate([crossing, jnp.zeros((16, feats), crossing.dtype)], axis=0)
     exchanged = lax.ppermute(jnp.concatenate([crossing, piece], axis=1), both, all_pairs)
@@ -293,12 +267,18 @@
         )
         for side in range(2)
     ]
-    pieces, query, ours, student_out_weight, owner_table, projector = lax.optimization_barrier(
-        (pieces, query, ours, student_out_weight, owner_table, projector)
+    pieces, query, ours, student_out_weight, owner_table = lax.optimization_barrier(
+        (pieces, query, ours, student_out_weight, owner_table)
     )
     mine = lax.all_to_all(
         pieces, "seq", split_axis=0, concat_axis=0, tiled=True, axis_index_groups=z_groups
     )
+
+    theirs = [lax.ppermute(part, both, all_pairs) for part in ours]
+
+    width = query.shape[1] // 2
+    other_query = lax.ppermute(query[:, width:], "group", [(0, 1)])
+    other_query, lower = lax.optimization_barrier((other_query, lower))
     below = lax.ppermute(
         lower,
         both,
@@ -309,11 +289,6 @@
         ],
     )
     mine = jnp.concatenate([mine, lower[None], below[None]], axis=0)
-
-    theirs = [lax.ppermute(part, both, all_pairs) for part in ours]
-
-    width = query.shape[1] // 2
-    other_query = lax.ppermute(query[:, width:], "group", [(0, 1)])
     query = jnp.where(group == 0, query[:, :width], other_query)
     seg_query = segment_ids.astype(jnp.float32)[:, None]
     info = jnp.stack([seq, group]).astype(jnp.int32)
@@ -359,7 +334,7 @@
         jnp.concatenate([context, other_context], axis=1),
         jnp.concatenate([other_context, context], axis=1),
     )
-    partial = project(context, projector)
+    partial = project(group[None].astype(jnp.int32), context, projector, tensor_n)
     partial, theirs[1] = lax.optimization_barrier((partial, theirs[1]))
     partial = lax.all_to_all(partial, "tensor", split_axis=0, concat_axis=0, tiled=True)
     output, given = on_core(

time: 164 us -> 162 us (0.988)
  waiting for transfers between devices: 37.5 us -> 24.5 us
  starting transfers between devices: 38.1 us -> 47.6 us
  blocking collectives: 46 us -> 52.6 us
  Pallas kernels: 15.7 us -> 12.1 us
    all_to_all x1, blocking collectives: 15.1 us -> 21.8 us  [shards(): lax.all_to_all(routed, 'seq', split_axis=0, concat_axis=0, tiled=True)]
    all_to_all x1, waiting for transfers between devices: 8.04 us -> 3.1 us  [shards(): lax.all_to_all(pieces, 'seq', split_axis=0, concat_axis=0, tiled=True, ax...]
    ppermute x2, waiting for transfers between devices: 7.23 us -> 2.99 us  [shards(): theirs = [lax.ppermute(part, both, all_pairs) for part in ours]]
    pallas_call x2 -> x1, Pallas kernels: 7.32 us -> 3.73 us  [project(): pl.pallas_call(project_kernel, out_shape=jax.ShapeDtypeStruct((tensor_n,...]
    ppermute x1, waiting for transfers between devices: 0.01 us -> 3.47 us  [shards(): lax.ppermute(jnp.concatenate([crossing, piece], axis=1), both, all_pairs)]
    all_to_all x1, starting transfers between devices: 3.56 us -> 6.37 us  [shards(): lax.all_to_all(weight, 'seq', split_axis=0, concat_axis=0, tiled=True, ax...]
    all_to_all x1, waiting for transfers between devices: 6.94 us -> 4.59 us  [shards(): lax.all_to_all(partial, 'tensor', split_axis=0, concat_axis=0, tiled=True)]
    all_to_all x1, starting transfers between devices: 6.67 us -> 8.83 us  [shards(): lax.all_to_all(pieces, 'seq', split_axis=0, concat_axis=0, tiled=True, ax...]
  transfers between devices with their start and end apart: 15 -> 15, of which waited for: 11 -> 12; matrix products, arithmetic and copies ran while one was open for 8% -> 7% of each run, Pallas kernels for 8% -> 6%
where the time goes in v5:
time: 162 us; the launch traced here: 161 us
  blocking collectives  52.6 us (32%)
  starting transfers between devices  47.6 us (29%)
  waiting for transfers between devices  24.5 us (15%)
  Pallas kernels  12.1 us (7%)
  local copies, waits for them, and re-layouts  11.9 us (7%)
  other arithmetic  11.3 us (7%)
    all_to_all x1, blocking collectives, shards(): lax.all_to_all(gradient, 'seq', split_axis=0, concat_axis=0, tiled=True,...  30.7 us
    all_to_all x1, blocking collectives, shards(): lax.all_to_all(routed, 'seq', split_axis=0, concat_axis=0, tiled=True)  21.8 us
    all_to_all x1, starting transfers between devices, shards(): lax.all_to_all(pieces, 'seq', split_axis=0, concat_axis=0, tiled=True, ax...  8.83 us
    unnamed x21, local copies, waits for them, and re-layouts  7.19 us
    all_to_all x1, starting transfers between devices, shards(): lax.all_to_all(weight, 'seq', split_axis=0, concat_axis=0, tiled=True, ax...  6.37 us
    ppermute x2, starting transfers between devices, shards(): theirs = [lax.ppermute(part, both, all_pairs) for part in ours]  5.84 us
    all_to_all x1, starting transfers between devices, shards(): lax.all_to_all(partial, 'tensor', split_axis=0, concat_axis=0, tiled=True)  5.03 us
    all_to_all x1, waiting for transfers between devices, shards(): lax.all_to_all(partial, 'tensor', split_axis=0, concat_axis=0, tiled=True)  4.59 us
  transfers between devices with their start and end apart: 15, of which 12 were waited for; matrix products, arithmetic and copies ran while one was open for 7% of the time, Pallas kernels for 6%

profile of v5, /device:TPU:1, one launch (start us, length us, event | category | flops | bytes accessed | tf_op | source)
XLA Modules:
  0.0 161.4 jit_solution(11913382930445038673)
XLA Ops:
  0.0 1.4 collective-permute-start
  2.8 1.6 constant_dynamic-slice_fusion.1
  4.6 1.1 collective-permute-done
  5.8 2.8 %collective-permute-start.1 = (bf16[272,384]{1,0:T(8,128)(2,1)S(1)}, bf16[272,384]{1,0:T(8,128)(2,1)S(1)}, u32[]{:S(2)}, u32[]{:S(2)}) collective-permute-start(bf16[272,384]{1,0:T(8,128)(2,1)S(1)} %fusion.5), channel_id=1, source_target_pairs={{0,8},{1,9},{2,10},{3,11},{4,12},{5,13},{6,14},{7,15},{8,0},{9,1},... | collective-permute-start | bytes 626696 | tf_op jit(solution)/shard_map/ppermute | solution.py:258
  8.5 3.5 %collective-permute-done.1 = bf16[272,384]{1,0:T(8,128)(2,1)S(1)} collective-permute-done((bf16[272,384]{1,0:T(8,128)(2,1)S(1)}, bf16[272,384]{1,0:T(8,128)(2,1)S(1)}, u32[]{:S(2)}, u32[]{:S(2)}) %collective-permute-start.1) | collective-permute-done | bytes 208928 | tf_op jit(solution)/shard_map/ppermute | solution.py:258
  13.1 8.8 %all-to-all-start = ((bf16[8,272,128]{2,1,0:T(8,128)(2,1)}), bf16[8,272,128]{2,1,0:T(8,128)(2,1)S(1)}, u32[]{:S(2)}, u32[]{:S(2)}) async-start(bf16[8,272,128]{2,1,0:T(8,128)(2,1)} %broadcast_select_fusion), calls=%async_computation | async-start | bytes 1114112 | tf_op jit(solution)/shard_map/all_to_all | solution.py:273
  21.9 2.9 %collective-permute-start.4 = (bf16[384,1024]{1,0:T(8,128)(2,1)S(1)}, bf16[384,1024]{1,0:T(8,128)(2,1)S(1)}, u32[]{:S(2)}, u32[]{:S(2)}) collective-permute-start(bf16[384,1024]{1,0:T(8,128)(2,1)S(1)} %get-tuple-element.33.ours_low), channel_id=1, source_target_pairs={{0,8},{1,9},{2,10},{3,11},{4,12},{5,13},{6,14},{7,15},{8,0},{9,1},... | collective-permute-start | bytes 2359304 | tf_op jit(solution)/shard_map/ppermute | solution.py:277
  27.6 1.3 collective-permute-start.2
  33.3 1.7 %slice_select_fusion.query = bf16[256,512]{1,0:T(8,128)(2,1)} fusion(bf16[256,512]{1,0:T(8,128)(2,1)S(1)} %collective-permute-done.2, bf16[256,1024]{1,0:T(8,128)(2,1)} %bitcast.50, pred[]{:T(512)S(6)} %eq.61), kind=kLoop, calls=%fused_computation.17 | loop fusion | flops 131072 | bytes 786433 | tf_op jit(solution)/shard_map/jit(_where)/select_n | solution.py:292
  35.0 3.1 %all-to-all-done = bf16[8,272,128]{2,1,0:T(8,128)(2,1)S(1)} async-done(((bf16[8,272,128]{2,1,0:T(8,128)(2,1)}), bf16[8,272,128]{2,1,0:T(8,128)(2,1)S(1)}, u32[]{:S(2)}, u32[]{:S(2)}) %all-to-all-start) | async-done | bytes 557088 | tf_op jit(solution)/shard_map/all_to_all | solution.py:273
  41.2 6.4 %all-to-all-start.2 = ((bf16[8,256,256]{2,1,0:T(8,128)(2,1)}), bf16[8,256,256]{2,1,0:T(8,128)(2,1)S(1)}, u32[]{:S(2)}, u32[]{:S(2)}) async-start(bf16[8,256,256]{2,1,0:T(8,128)(2,1)} %broadcast_in_dim.73), calls=%async_computation.2 | async-start | bytes 2097152 | tf_op jit(solution)/shard_map/all_to_all | solution.py:325
  47.6 3.8 %collective-permute-start.5 = (bf16[10,272,128]{2,1,0:T(8,128)(2,1)}, bf16[10,272,128]{2,1,0:T(8,128)(2,1)}, u32[]{:S(2)}, u32[]{:S(2)}) collective-permute-start(bf16[10,272,128]{2,1,0:T(8,128)(2,1)} %pad_maximum_fusion.mine), channel_id=1, source_target_pairs={{0,128},{128,0},{1,129},{129,1},{2,130},{130,2},{3,131},{131,3},{4... | collective-permute-start | bytes 2088968 | tf_op jit(solution)/shard_map/ppermute | solution.py:324
  51.4 2.9 %collective-permute-start.7 = (bf16[384,1024]{1,0:T(8,128)(2,1)S(1)}, bf16[384,1024]{1,0:T(8,128)(2,1)}, u32[]{:S(2)}, u32[]{:S(2)}) collective-permute-start(bf16[384,1024]{1,0:T(8,128)(2,1)S(1)} %get-tuple-element.35.ours_high), channel_id=1, source_target_pairs={{0,8},{1,9},{2,10},{3,11},{4,12},{5,13},{6,14},{7,15},{8,0},{9,1},... | collective-permute-start | bytes 2359304 | tf_op jit(solution)/shard_map/ppermute | solution.py:277
  56.5 3.8 %attend.1 = bf16[256,512]{1,0:T(8,128)(2,1)S(1)} custom-call(s32[2]{0:T(128)S(1)} %pad_add_fusion.info.place, bf16[256,512]{1,0:T(8,128)(2,1)S(1)} %copy-done.3, f32[256,1]{1,0:T(8,128)S(1)} %copy.10.seg_query, bf16[10,272,128]{2,1,0:T(8,128)(2,1)S(1)} %copy-done.2, bf16[10,272,128]{2,1,0:T(8,128)(2,1)} %collective-permute-done.5.other), custom_call_target="tpu_custom_call" | custom-call | flops 2684354560 | bytes 4194304 | tf_op jit(solution)/shard_map/attend/pallas_call | solution.py:119
  60.8 1.2 collective-permute-done.6
  62.1 3.4 %copy-done = bf16[1024,4096]{1,0:T(8,128)(2,1)S(1)} copy-done((bf16[1024,4096]{1,0:T(8,128)(2,1)S(1)}, bf16[1024,4096]{1,0:T(8,128)(2,1)}, u32[]{:S(2)}) %copy-start) | copy-done | bytes 8388632
  65.5 3.7 %project.1 = bf16[8,256,256]{2,1,0:T(8,128)(2,1)S(1)} custom-call(s32[1]{0:T(128)} %bitcast.7.core, bf16[256,1024]{1,0:T(8,128)(2,1)S(1)} %maximum_select_fusion.context, bf16[1024,4096]{1,0:T(8,128)(2,1)S(1)} %copy-done, bf16[1024,4096]{1,0:T(8,128)(2,1)S(1)} %copy-done), custom_call_target="tpu_custom_call" | custom-call | flops 1073741824 | bytes 4194304 | tf_op jit(solution)/shard_map/project/pallas_call | solution.py:150
  70.2 1.9 %collective-permute-done.7.theirs_high = bf16[384,1024]{1,0:T(8,128)(2,1)} collective-permute-done((bf16[384,1024]{1,0:T(8,128)(2,1)S(1)}, bf16[384,1024]{1,0:T(8,128)(2,1)}, u32[]{:S(2)}, u32[]{:S(2)}) %collective-permute-start.7) | collective-permute-done | bytes 786464 | tf_op jit(solution)/shard_map/ppermute | solution.py:277
  72.1 1.4 all-to-all-done.2
  73.5 5.0 %all-to-all-start.1 = ((bf16[8,256,256]{2,1,0:T(8,128)(2,1)}), bf16[8,256,256]{2,1,0:T(8,128)(2,1)}, u32[]{:S(2)}, u32[]{:S(2)}) async-start(bf16[8,256,256]{2,1,0:T(8,128)(2,1)} %copy-done.1), calls=%async_computation.1 | async-start | bytes 2097152 | tf_op jit(solution)/shard_map/all_to_all | solution.py:339
  78.5 2.1 %student.1 = (f32[384,256]{1,0:T(8,128)S(1)}, bf16[384,256]{1,0:T(8,128)(2,1)S(1)}) custom-call(s32[2]{0:T(128)S(1)} %pad_add_fusion.info.place, bf16[384,1024]{1,0:T(8,128)(2,1)S(1)} %get-tuple-element.33.ours_low, bf16[384,1024]{1,0:T(8,128)(2,1)S(1)} %get-tuple-element.35.ours_high, bf16[384,1024]{1,0:T(8,128)(2,1)S(1)} %collective-permute-done.4.theirs_low, ...), custom_call_target="tpu_custom_call" | custom-call | flops 805306368 | bytes 6291456 | tf_op jit(solution)/shard_map/student/pallas_call | solution.py:213
  80.6 4.2 %collective-permute-start.8 = (bf16[384,256]{1,0:T(8,128)(2,1)S(1)}, bf16[384,256]{1,0:T(8,128)(2,1)S(1)}, u32[]{:S(2)}, u32[]{:S(2)}) collective-permute-start(bf16[384,256]{1,0:T(8,128)(2,1)S(1)} %get-tuple-element.44), channel_id=1, source_target_pairs={{0,128},{128,0},{1,129},{129,1},{2,130},{130,2},{3,131},{131,3},{4... | collective-permute-start | bytes 589832 | tf_op jit(solution)/shard_map/ppermute | solution.py:353
  86.0 4.6 %all-to-all-done.1 = bf16[8,256,256]{2,1,0:T(8,128)(2,1)} async-done(((bf16[8,256,256]{2,1,0:T(8,128)(2,1)}), bf16[8,256,256]{2,1,0:T(8,128)(2,1)}, u32[]{:S(2)}, u32[]{:S(2)}) %all-to-all-start.1) | async-done | bytes 1048608 | tf_op jit(solution)/shard_map/all_to_all | solution.py:339
  90.6 1.4 reduce_sum.44
  91.9 1.1 convolution_convert_fusion
  93.2 21.8 %all_to_all.25 = bf16[16,24,256]{2,1,0:T(8,128)(2,1)S(1)} all-to-all(bf16[16,24,256]{2,1,0:T(8,128)(2,1)S(1)} %bitcast.46), channel_id=1, replica_groups=mesh['group'=2,'tensor'=8,'seq'=16] {'seq'}, dimensions={0} | all-to-all | bytes 393216 | tf_op jit(solution)/shard_map/all_to_all | solution.py:366
  115.1 3.2 %collective-permute-start.9 = (bf16[384,256]{1,0:T(8,128)(2,1)S(1)}, bf16[384,256]{1,0:T(8,128)(2,1)S(1)}, u32[]{:S(2)}, u32[]{:S(2)}) collective-permute-start(bf16[384,256]{1,0:T(8,128)(2,1)S(1)} %fusion.2.mine), channel_id=1, source_target_pairs={{0,128},{128,0},{1,129},{129,1},{2,130},{130,2},{3,131},{131,3},{4... | collective-permute-start | bytes 589832 | tf_op jit(solution)/shard_map/ppermute | solution.py:380
  119.4 2.4 %gradient.1 = bf16[8,256,256]{2,1,0:T(8,128)(2,1)S(1)} custom-call(s32[2]{0:T(128)S(1)} %pad_add_fusion.info.place, bf16[384,1024]{1,0:T(8,128)(2,1)S(1)} %get-tuple-element.33.ours_low, bf16[384,1024]{1,0:T(8,128)(2,1)S(1)} %get-tuple-element.35.ours_high, bf16[384,1024]{1,0:T(8,128)(2,1)S(1)} %collective-permute-done.4.theirs_low, ...), custom_call_target="tpu_custom_call" | custom-call | flops 805306368 | bytes 6291456 | tf_op jit(solution)/shard_map/gradient/pallas_call | solution.py:213
  121.8 30.7 %all_to_all.26 = bf16[8,256,256]{2,1,0:T(8,128)(2,1)S(1)} all-to-all(bf16[8,256,256]{2,1,0:T(8,128)(2,1)S(1)} %gradient.1), channel_id=1, replica_groups={{0,1,2,3,4,5,6,7},{8,9,10,11,12,13,14,15},{16,17,18,19,20,21,22,23},{24..., dimensions={0} | all-to-all | bytes 2097152 | tf_op jit(solution)/shard_map/all_to_all | solution.py:382
  152.7 2.5 %collective-permute-start.11 = (bf16[256,256]{1,0:T(8,128)(2,1)S(1)}, bf16[256,256]{1,0:T(8,128)(2,1)S(1)}, u32[]{:S(2)}, u32[]{:S(2)}) collective-permute-start(bf16[256,256]{1,0:T(8,128)(2,1)S(1)} %reduce_sum.45), channel_id=1, source_target_pairs={{8,128},{9,129},{10,130},{11,131},{12,132},{13,133},{14,134},{15,1... | collective-permute-start | bytes 393224 | tf_op jit(solution)/shard_map/ppermute | solution.py:393
  155.2 1.3 collective-permute-start.10
  156.5 4.0 %collective-permute-done.11 = bf16[256,256]{1,0:T(8,128)(2,1)S(1)} collective-permute-done((bf16[256,256]{1,0:T(8,128)(2,1)S(1)}, bf16[256,256]{1,0:T(8,128)(2,1)S(1)}, u32[]{:S(2)}, u32[]{:S(2)}) %collective-permute-start.11) | collective-permute-done | bytes 131104 | tf_op jit(solution)/shard_map/ppermute | solution.py:393
  (66 shorter events, 20.1 us)
Async XLA Ops:
  0.0 5.7 %copy-start.8 = (bf16[1,256,256]{2,1,0:T(8,128)(2,1)S(1)}, bf16[1,256,256]{2,1,0:T(8,128)(2,1)}, u32[]{:S(2)}) copy-start(bf16[1,256,256]{2,1,0:T(8,128)(2,1)} %param.8) | copy-start | bytes 393220
  0.0 4.6 %copy-start.6 = (bf16[256,512]{1,0:T(8,128)(2,1)S(1)}, bf16[256,512]{1,0:T(8,128)(2,1)}, u32[]{:S(2)}) copy-start(bf16[256,512]{1,0:T(8,128)(2,1)} %param.13) | copy-start | bytes 786436
  0.0 12.9 %copy-start.9 = (s32[4096,1]{0,1:T(1,128)S(1)}, s32[4096,1]{0,1:T(1,128)}, u32[]{:S(2)}) copy-start(s32[4096,1]{0,1:T(1,128)} %param.11) | copy-start | bytes 49156
  0.0 5.7 %collective-permute-start = (bf16[256,256]{1,0:T(8,128)(2,1)}, bf16[256,256]{1,0:T(8,128)(2,1)S(1)}, u32[]{:S(2)}, u32[]{:S(2)}) collective-permute-start(bf16[256,256]{1,0:T(8,128)(2,1)} %bitcast.55), channel_id=1, source_target_pairs={{0,128},{1,129},{2,130},{3,131},{4,132},{5,133},{6,134},{7,135},{8... | collective-permute-start | bytes 393224 | tf_op jit(solution)/shard_map/ppermute | solution.py:253
  2.8 24.0 %copy-start.5 = (bf16[1,256,1024]{2,1,0:T(8,128)(2,1)S(1)}, bf16[1,256,1024]{2,1,0:T(8,128)(2,1)}, u32[]{:S(2)}) copy-start(bf16[1,256,1024]{2,1,0:T(8,128)(2,1)} %param.7) | copy-start | bytes 1572868
  5.8 6.2 %collective-permute-start.1 = (bf16[272,384]{1,0:T(8,128)(2,1)S(1)}, bf16[272,384]{1,0:T(8,128)(2,1)S(1)}, u32[]{:S(2)}, u32[]{:S(2)}) collective-permute-start(bf16[272,384]{1,0:T(8,128)(2,1)S(1)} %fusion.5), channel_id=1, source_target_pairs={{0,8},{1,9},{2,10},{3,11},{4,12},{5,13},{6,14},{7,15},{8,0},{9,1},... | collective-permute-start | bytes 626696 | tf_op jit(solution)/shard_map/ppermute | solution.py:258
  12.0 1.1 copy-start.7
  13.1 25.0 %all-to-all-start = ((bf16[8,272,128]{2,1,0:T(8,128)(2,1)}), bf16[8,272,128]{2,1,0:T(8,128)(2,1)S(1)}, u32[]{:S(2)}, u32[]{:S(2)}) async-start(bf16[8,272,128]{2,1,0:T(8,128)(2,1)} %broadcast_select_fusion), calls=%async_computation | async-start | bytes 1114112 | tf_op jit(solution)/shard_map/all_to_all | solution.py:273
  21.9 18.2 %collective-permute-start.4 = (bf16[384,1024]{1,0:T(8,128)(2,1)S(1)}, bf16[384,1024]{1,0:T(8,128)(2,1)S(1)}, u32[]{:S(2)}, u32[]{:S(2)}) collective-permute-start(bf16[384,1024]{1,0:T(8,128)(2,1)S(1)} %get-tuple-element.33.ours_low), channel_id=1, source_target_pairs={{0,8},{1,9},{2,10},{3,11},{4,12},{5,13},{6,14},{7,15},{8,0},{9,1},... | collective-permute-start | bytes 2359304 | tf_op jit(solution)/shard_map/ppermute | solution.py:277
  27.6 5.1 %collective-permute-start.2 = (bf16[256,512]{1,0:T(8,128)(2,1)}, bf16[256,512]{1,0:T(8,128)(2,1)S(1)}, u32[]{:S(2)}, u32[]{:S(2)}) collective-permute-start(bf16[256,512]{1,0:T(8,128)(2,1)} %slice.33), channel_id=1, source_target_pairs={{0,128},{1,129},{2,130},{3,131},{4,132},{5,133},{6,134},{7,135},{8... | collective-permute-start | bytes 786440 | tf_op jit(solution)/shard_map/ppermute | solution.py:280
  32.7 2.4 %collective-permute-start.3 = (bf16[272,128]{1,0:T(8,128)(2,1)S(1)}, bf16[272,128]{1,0:T(8,128)(2,1)S(1)}, u32[]{:S(2)}, u32[]{:S(2)}) collective-permute-start(bf16[272,128]{1,0:T(8,128)(2,1)S(1)} %slice.42), channel_id=1, source_target_pairs={{8,9},{9,10},{10,11},{11,12},{12,13},{13,14},{14,15},{136,137},{13... | collective-permute-start | bytes 208904 | tf_op jit(solution)/shard_map/ppermute | solution.py:282
  41.2 32.2 %all-to-all-start.2 = ((bf16[8,256,256]{2,1,0:T(8,128)(2,1)}), bf16[8,256,256]{2,1,0:T(8,128)(2,1)S(1)}, u32[]{:S(2)}, u32[]{:S(2)}) async-start(bf16[8,256,256]{2,1,0:T(8,128)(2,1)} %broadcast_in_dim.73), calls=%async_computation.2 | async-start | bytes 2097152 | tf_op jit(solution)/shard_map/all_to_all | solution.py:325
  47.6 6.9 %collective-permute-start.5 = (bf16[10,272,128]{2,1,0:T(8,128)(2,1)}, bf16[10,272,128]{2,1,0:T(8,128)(2,1)}, u32[]{:S(2)}, u32[]{:S(2)}) collective-permute-start(bf16[10,272,128]{2,1,0:T(8,128)(2,1)} %pad_maximum_fusion.mine), channel_id=1, source_target_pairs={{0,128},{128,0},{1,129},{129,1},{2,130},{130,2},{3,131},{131,3},{4... | collective-permute-start | bytes 2088968 | tf_op jit(solution)/shard_map/ppermute | solution.py:324
  51.4 20.7 %collective-permute-start.7 = (bf16[384,1024]{1,0:T(8,128)(2,1)S(1)}, bf16[384,1024]{1,0:T(8,128)(2,1)}, u32[]{:S(2)}, u32[]{:S(2)}) collective-permute-start(bf16[384,1024]{1,0:T(8,128)(2,1)S(1)} %get-tuple-element.35.ours_high), channel_id=1, source_target_pairs={{0,8},{1,9},{2,10},{3,11},{4,12},{5,13},{6,14},{7,15},{8,0},{9,1},... | collective-permute-start | bytes 2359304 | tf_op jit(solution)/shard_map/ppermute | solution.py:277
  54.5 1.1 copy-start.2
  55.6 0.9 copy-start.3
  60.4 1.6 %collective-permute-start.6 = (bf16[256,512]{1,0:T(8,128)(2,1)S(1)}, bf16[256,512]{1,0:T(8,128)(2,1)S(1)}, u32[]{:S(2)}, u32[]{:S(2)}) collective-permute-start(bf16[256,512]{1,0:T(8,128)(2,1)S(1)} %attend.1), channel_id=1, source_target_pairs={{0,128},{128,0},{1,129},{129,1},{2,130},{130,2},{3,131},{131,3},{4... | collective-permute-start | bytes 786440 | tf_op jit(solution)/shard_map/ppermute | solution.py:331
  62.1 3.4 %copy-start = (bf16[1024,4096]{1,0:T(8,128)(2,1)S(1)}, bf16[1024,4096]{1,0:T(8,128)(2,1)}, u32[]{:S(2)}) copy-start(bf16[1024,4096]{1,0:T(8,128)(2,1)} %high.1) | copy-start | bytes 25165828
  69.2 1.0 copy-start.1
  73.5 17.1 %all-to-all-start.1 = ((bf16[8,256,256]{2,1,0:T(8,128)(2,1)}), bf16[8,256,256]{2,1,0:T(8,128)(2,1)}, u32[]{:S(2)}, u32[]{:S(2)}) async-start(bf16[8,256,256]{2,1,0:T(8,128)(2,1)} %copy-done.1), calls=%async_computation.1 | async-start | bytes 2097152 | tf_op jit(solution)/shard_map/all_to_all | solution.py:339
  80.6 34.4 %copy-start.4 = (f32[48,8,2,128]{3,1,2,0:T(8,128)S(1)}, f32[48,8,2,128]{3,1,2,0:T(8,128)}, u32[]{:S(2)}) copy-start(f32[48,8,2,128]{3,1,2,0:T(8,128)} %copy.13) | copy-start | bytes 1179652
  80.6 5.3 %collective-permute-start.8 = (bf16[384,256]{1,0:T(8,128)(2,1)S(1)}, bf16[384,256]{1,0:T(8,128)(2,1)S(1)}, u32[]{:S(2)}, u32[]{:S(2)}) collective-permute-start(bf16[384,256]{1,0:T(8,128)(2,1)S(1)} %get-tuple-element.44), channel_id=1, source_target_pairs={{0,128},{128,0},{1,129},{129,1},{2,130},{130,2},{3,131},{131,3},{4... | collective-permute-start | bytes 589832 | tf_op jit(solution)/shard_map/ppermute | solution.py:353
  115.1 4.2 %collective-permute-start.9 = (bf16[384,256]{1,0:T(8,128)(2,1)S(1)}, bf16[384,256]{1,0:T(8,128)(2,1)S(1)}, u32[]{:S(2)}, u32[]{:S(2)}) collective-permute-start(bf16[384,256]{1,0:T(8,128)(2,1)S(1)} %fusion.2.mine), channel_id=1, source_target_pairs={{0,128},{128,0},{1,129},{129,1},{2,130},{130,2},{3,131},{131,3},{4... | collective-permute-start | bytes 589832 | tf_op jit(solution)/shard_map/ppermute | solution.py:380
  152.7 7.8 %collective-permute-start.11 = (bf16[256,256]{1,0:T(8,128)(2,1)S(1)}, bf16[256,256]{1,0:T(8,128)(2,1)S(1)}, u32[]{:S(2)}, u32[]{:S(2)}) collective-permute-start(bf16[256,256]{1,0:T(8,128)(2,1)S(1)} %reduce_sum.45), channel_id=1, source_target_pairs={{8,128},{9,129},{10,130},{11,131},{12,132},{13,133},{14,134},{15,1... | collective-permute-start | bytes 393224 | tf_op jit(solution)/shard_map/ppermute | solution.py:393
  155.2 5.3 %collective-permute-start.10 = (bf16[256,256]{1,0:T(8,128)(2,1)S(1)}, bf16[256,256]{1,0:T(8,128)(2,1)S(1)}, u32[]{:S(2)}, u32[]{:S(2)}) collective-permute-start(bf16[256,256]{1,0:T(8,128)(2,1)S(1)} %reduce_sum.45), channel_id=1, source_target_pairs={{0,128},{1,129},{2,130},{3,131},{4,132},{5,133},{6,134},{7,135},{1... | collective-permute-start | bytes 393224 | tf_op jit(solution)/shard_map/ppermute | solution.py:392

commit v6 on v5

--- a/solution.py
+++ b/solution.py
@@ -253,7 +253,8 @@
     passed = lax.ppermute(keyval, "group", [(0, 1)])
     piece = jnp.where(group == 0, keyval[:, :HD], passed[:, HD:])
     piece = jnp.concatenate([piece, seg_rows], axis=0)
-    crossing = lax.dynamic_slice_in_dim(student_out_weight, (1 - group) * feats, feats, axis=1)
+    column_half = jnp.where(group == 1, high, 1 - high)
+    crossing = lax.dynamic_slice_in_dim(student_out_weight, (1 - high) * feats, feats, axis=1)
     crossing = jnp.concatenate([crossing, jnp.zeros((16, feats), crossing.dtype)], axis=0)
     exchanged = lax.ppermute(jnp.concatenate([crossing, piece], axis=1), both, all_pairs)
     lower = exchanged[:, feats:]
@@ -261,24 +262,30 @@
     ring = seq % ZN
     later = (jnp.arange(ZN, dtype=jnp.int32) >= ring) | (high == 0)
     pieces = jnp.where(later[:, None, None], piece[None], lower[None])
-    ours = [
-        lax.dynamic_slice_in_dim(
-            student_context, group * half + side * (half // 2), half // 2, axis=1
+    def column_parts(rows, place):
+        return [
+            lax.dynamic_slice_in_dim(rows, place * half + side * (half // 2), half // 2, axis=1)
+            for side in range(2)
+        ]
+
+    sent = column_parts(student_context, 1 - column_half)
+    pieces, query, sent, student_context, student_out_weight, owner_table = (
+        lax.optimization_barrier(
+            (pieces, query, sent, student_context, student_out_weight, owner_table)
         )
-        for side in range(2)
-    ]
-    pieces, query, ours, student_out_weight, owner_table = lax.optimization_barrier(
-        (pieces, query, ours, student_out_weight, owner_table)
     )
     mine = lax.all_to_all(
         pieces, "seq", split_axis=0, concat_axis=0, tiled=True, axis_index_groups=z_groups
     )
 
-    theirs = [lax.ppermute(part, both, all_pairs) for part in ours]
+    theirs = [lax.ppermute(part, both, all_pairs) for part in sent]
 
     width = query.shape[1] // 2
     other_query = lax.ppermute(query[:, width:], "group", [(0, 1)])
-    other_query, lower = lax.optimization_barrier((other_query, lower))
+    weight = lax.dynamic_slice_in_dim(student_out_weight, high * feats, feats, axis=1)
+    weight = jnp.where(group == 1, weight, crossing)
+    weight = jnp.broadcast_to(weight[None], (ZN,) + weight.shape)
+    other_query, lower, weight = lax.optimization_barrier((other_query, lower, weight))
     below = lax.ppermute(
         lower,
         both,
@@ -288,14 +295,9 @@
             for z in range(ZN - 1)
         ],
     )
-    mine = jnp.concatenate([mine, lower[None], below[None]], axis=0)
     query = jnp.where(group == 0, query[:, :width], other_query)
     seg_query = segment_ids.astype(jnp.float32)[:, None]
     info = jnp.stack([seq, group]).astype(jnp.int32)
-
-    weight = lax.dynamic_slice_in_dim(student_out_weight, group * feats, feats, axis=1)
-    weight = jnp.where(group == high, weight, crossing)
-    weight = jnp.broadcast_to(weight[None], (ZN,) + weight.shape)
 
     owners_all = owner_table[:, 0]
     owners = lax.dynamic_slice_in_dim(owners_all, seq * tok, tok)
@@ -316,17 +318,18 @@
     live = jnp.arange(capacity, dtype=jnp.int32)[None, :, None] < counts[:, None, :]
     scale = live.reshape(slots, 2, 1).astype(jnp.float32) / tok
     scale = jnp.broadcast_to(scale, (slots, 2, feats // 2)).reshape(slots, feats)
-    mine, query, seg_query, info, weight, route, scale, theirs[0] = (
-        lax.optimization_barrier(
-            (mine, query, seg_query, info, weight, route, scale, theirs[0])
-        )
-    )
-    other = lax.ppermute(mine, "group", core_swap)
+    mine, weight, below, query, seg_query, info, route, scale = lax.optimization_barrier(
+        (mine, weight, below, query, seg_query, info, route, scale)
+    )
     weight = lax.all_to_all(
         weight, "seq", split_axis=0, concat_axis=0, tiled=True, axis_index_groups=z_groups
     ).reshape(half, feats)
+    mine = jnp.concatenate([mine, lower[None], below[None]], axis=0)
+    mine, theirs[0] = lax.optimization_barrier((mine, theirs[0]))
+    other = lax.ppermute(mine, "group", core_swap)
     context = attend(info, query, seg_query, mine, other)
     place = info
+    ours = column_parts(student_context, column_half)
 
     other_context = lax.ppermute(context, "group", core_swap)
     context = jnp.where(
@@ -389,16 +392,15 @@
     )
     gradient = jnp.sum(gradient.astype(jnp.float32), axis=0).astype(jnp.bfloat16)
 
-    straight = lax.ppermute(gradient, both, [(z, 2 * ZN + z) for z in range(ZN)])
-    crossed = lax.ppermute(
+    passed = lax.ppermute(
         gradient,
         both,
-        [(ZN + z, 2 * ZN + z) for z in range(ZN)] + [(2 * ZN + z, 3 * ZN + z) for z in range(ZN)],
+        [(h * ZN + z, (3 - h) * ZN + z) for h in range(2) for z in range(ZN)],
     )
     whole = jnp.where(
         high == 0,
-        jnp.concatenate([straight, crossed], axis=1),
-        jnp.concatenate([crossed, gradient], axis=1),
+        jnp.concatenate([gradient, passed], axis=1),
+        jnp.concatenate([passed, gradient], axis=1),
     )
     return jnp.where(group == 1, whole.astype(jnp.float32), 0.0)[None]
 

time: 162 us -> 158 us (0.975)
  starting transfers between devices: 47.6 us -> 41.4 us
  waiting for transfers between devices: 24.5 us -> 30.4 us
  other arithmetic: 11.3 us -> 9.24 us
  blocking collectives: 52.6 us -> 50.7 us
    ppermute x4 -> x3, waiting for transfers between devices: 6.97 us -> 12.3 us  [the longest x1 6.49 us: shards(): lax.ppermute(gradient, both, [(h * ZN + z, (3 - h) * ZN + z) for h in ran...]
    all_to_all x1, starting transfers between devices: 6.37 us -> 3.56 us  [shards(): lax.all_to_all(weight, 'seq', split_axis=0, concat_axis=0, tiled=True, ax...]
    dynamic_slice x2 -> x3, local copies, waits for them, and re-layouts: 1.57 us -> 4.28 us  [the longest x2 4.27 us: column_parts(): lax.dynamic_slice_in_dim(rows, place * half + side * (half // 2), half //...]
    all_to_all x1, waiting for transfers between devices: 3.1 us -> 5.72 us  [shards(): lax.all_to_all(pieces, 'seq', split_axis=0, concat_axis=0, tiled=True, ax...]
    ppermute x4 -> x3, starting transfers between devices: 9.63 us -> 7.21 us  [the longest x2 5.92 us: shards(): theirs = [lax.ppermute(part, both, all_pairs) for part in sent]]
    unnamed x21 -> x19, local copies, waits for them, and re-layouts: 7.19 us -> 5.15 us
    all_to_all x1, blocking collectives: 21.8 us -> 19.9 us  [shards(): lax.all_to_all(routed, 'seq', split_axis=0, concat_axis=0, tiled=True)]
  transfers between devices with their start and end apart: 15 -> 14, of which waited for: 12 -> 10; matrix products, arithmetic and copies ran while one was open for 7% -> 8% of each run, Pallas kernels for 6% -> 6%
where the time goes in v6:
time: 158 us; the launch traced here: 157 us
  blocking collectives  50.7 us (32%)
  starting transfers between devices  41.4 us (26%)
  waiting for transfers between devices  30.4 us (19%)
  Pallas kernels  12.1 us (8%)
  local copies, waits for them, and re-layouts  11.8 us (7%)
  other arithmetic  9.24 us (6%)
    all_to_all x1, blocking collectives, shards(): lax.all_to_all(gradient, 'seq', split_axis=0, concat_axis=0, tiled=True,...  30.9 us
    all_to_all x1, blocking collectives, shards(): lax.all_to_all(routed, 'seq', split_axis=0, concat_axis=0, tiled=True)  19.9 us
    all_to_all x1, starting transfers between devices, shards(): lax.all_to_all(pieces, 'seq', split_axis=0, concat_axis=0, tiled=True, ax...  8.99 us
    ppermute x1, waiting for transfers between devices, shards(): lax.ppermute(gradient, both, [(h * ZN + z, (3 - h) * ZN + z) for h in ran...  6.49 us
    ppermute x2, starting transfers between devices, shards(): theirs = [lax.ppermute(part, both, all_pairs) for part in sent]  5.92 us
    ppermute x2, waiting for transfers between devices, shards(): theirs = [lax.ppermute(part, both, all_pairs) for part in sent]  5.85 us
    all_to_all x1, waiting for transfers between devices, shards(): lax.all_to_all(pieces, 'seq', split_axis=0, concat_axis=0, tiled=True, ax...  5.72 us
    all_to_all x1, waiting for transfers between devices, shards(): lax.all_to_all(partial, 'tensor', split_axis=0, concat_axis=0, tiled=True)  5.16 us
  transfers between devices with their start and end apart: 14, of which 10 were waited for; matrix products, arithmetic and copies ran while one was open for 8% of the time, Pallas kernels for 6%

profile of v6, /device:TPU:1, one launch (start us, length us, event | category | flops | bytes accessed | tf_op | source)
XLA Modules:
  0.0 157.2 jit_solution(6060436737866266305)
XLA Ops:
  0.0 1.4 collective-permute-start
  2.3 2.7 %constant_dynamic-slice_fusion.3 = (bf16[384,1024]{1,0:T(8,128)(2,1)}, bf16[384,1024]{1,0:T(8,128)(2,1)}) fusion(bf16[384,4096]{1,0:T(8,128)(2,1)} %param.12, s32[]{:T(128)S(6)} %select_n.113, s32[]{:T(128)S(6)} %select_n.112), kind=kLoop, calls=%fused_computation.37 | loop fusion | bytes 3145736 | tf_op jit(solution)/shard_map/dynamic_slice | solution.py:267
  5.8 3.4 %collective-permute-start.1 = (bf16[272,384]{1,0:T(8,128)(2,1)S(1)}, bf16[272,384]{1,0:T(8,128)(2,1)S(1)}, u32[]{:S(2)}, u32[]{:S(2)}) collective-permute-start(bf16[272,384]{1,0:T(8,128)(2,1)S(1)} %fusion.5), channel_id=1, source_target_pairs={{0,8},{1,9},{2,10},{3,11},{4,12},{5,13},{6,14},{7,15},{8,0},{9,1},... | collective-permute-start | bytes 626696 | tf_op jit(solution)/shard_map/ppermute | solution.py:259
  9.2 3.3 %collective-permute-done.1 = bf16[272,384]{1,0:T(8,128)(2,1)S(1)} collective-permute-done((bf16[272,384]{1,0:T(8,128)(2,1)S(1)}, bf16[272,384]{1,0:T(8,128)(2,1)S(1)}, u32[]{:S(2)}, u32[]{:S(2)}) %collective-permute-start.1) | collective-permute-done | bytes 208928 | tf_op jit(solution)/shard_map/ppermute | solution.py:259
  13.6 9.0 %all-to-all-start = ((bf16[8,272,128]{2,1,0:T(8,128)(2,1)}), bf16[8,272,128]{2,1,0:T(8,128)(2,1)S(1)}, u32[]{:S(2)}, u32[]{:S(2)}) async-start(bf16[8,272,128]{2,1,0:T(8,128)(2,1)} %broadcast_select_fusion), calls=%async_computation | async-start | bytes 1114112 | tf_op jit(solution)/shard_map/all_to_all | solution.py:277
  25.4 1.3 collective-permute-start.2
  26.7 3.0 %collective-permute-start.4 = (bf16[384,1024]{1,0:T(8,128)(2,1)}, bf16[384,1024]{1,0:T(8,128)(2,1)S(1)}, u32[]{:S(2)}, u32[]{:S(2)}) collective-permute-start(bf16[384,1024]{1,0:T(8,128)(2,1)} %get-tuple-element.42), channel_id=1, source_target_pairs={{0,8},{1,9},{2,10},{3,11},{4,12},{5,13},{6,14},{7,15},{8,0},{9,1},... | collective-permute-start | bytes 2359304 | tf_op jit(solution)/shard_map/ppermute | solution.py:281
  33.0 5.7 %all-to-all-done = bf16[8,272,128]{2,1,0:T(8,128)(2,1)S(1)} async-done(((bf16[8,272,128]{2,1,0:T(8,128)(2,1)}), bf16[8,272,128]{2,1,0:T(8,128)(2,1)S(1)}, u32[]{:S(2)}, u32[]{:S(2)}) %all-to-all-start) | async-done | bytes 557088 | tf_op jit(solution)/shard_map/all_to_all | solution.py:277
  38.7 3.6 %all-to-all-start.2 = ((bf16[8,256,256]{2,1,0:T(8,128)(2,1)}), bf16[8,256,256]{2,1,0:T(8,128)(2,1)S(1)}, u32[]{:S(2)}, u32[]{:S(2)}) async-start(bf16[8,256,256]{2,1,0:T(8,128)(2,1)} %broadcast_in_dim.43), calls=%async_computation.2 | async-start | bytes 2097152 | tf_op jit(solution)/shard_map/all_to_all | solution.py:324
  42.4 2.8 %collective-permute-done.4.theirs_low = bf16[384,1024]{1,0:T(8,128)(2,1)S(1)} collective-permute-done((bf16[384,1024]{1,0:T(8,128)(2,1)}, bf16[384,1024]{1,0:T(8,128)(2,1)S(1)}, u32[]{:S(2)}, u32[]{:S(2)}) %collective-permute-start.4) | collective-permute-done | bytes 786464 | tf_op jit(solution)/shard_map/ppermute | solution.py:281
  45.2 3.3 %collective-permute-start.5 = (bf16[10,272,128]{2,1,0:T(8,128)(2,1)S(1)}, bf16[10,272,128]{2,1,0:T(8,128)(2,1)}, u32[]{:S(2)}, u32[]{:S(2)}) collective-permute-start(bf16[10,272,128]{2,1,0:T(8,128)(2,1)S(1)} %pad_maximum_fusion.mine), channel_id=1, source_target_pairs={{0,128},{128,0},{1,129},{129,1},{2,130},{130,2},{3,131},{131,3},{4... | collective-permute-start | bytes 2088968 | tf_op jit(solution)/shard_map/ppermute | solution.py:329
  48.5 2.9 %collective-permute-start.7 = (bf16[384,1024]{1,0:T(8,128)(2,1)}, bf16[384,1024]{1,0:T(8,128)(2,1)S(1)}, u32[]{:S(2)}, u32[]{:S(2)}) collective-permute-start(bf16[384,1024]{1,0:T(8,128)(2,1)} %get-tuple-element.47), channel_id=1, source_target_pairs={{0,8},{1,9},{2,10},{3,11},{4,12},{5,13},{6,14},{7,15},{8,0},{9,1},... | collective-permute-start | bytes 2359304 | tf_op jit(solution)/shard_map/ppermute | solution.py:281
  52.5 3.8 %attend.1 = bf16[256,512]{1,0:T(8,128)(2,1)S(1)} custom-call(s32[2]{0:T(128)S(1)} %pad_add_fusion.info.place, bf16[256,512]{1,0:T(8,128)(2,1)S(1)} %copy-done.4, f32[256,1]{1,0:T(8,128)S(1)} %copy.10.seg_query, bf16[10,272,128]{2,1,0:T(8,128)(2,1)S(1)} %pad_maximum_fusion.mine, bf16[10,272,128]{2,1,0:T(8,128)(2,1)} %collective-permute-done.5.other), custom_call_target="tpu_custom_call" | custom-call | flops 2684354560 | bytes 4194304 | tf_op jit(solution)/shard_map/attend/pallas_call | solution.py:119
  56.7 1.3 collective-permute-done.6
  58.1 3.4 %copy-done = bf16[1024,4096]{1,0:T(8,128)(2,1)S(1)} copy-done((bf16[1024,4096]{1,0:T(8,128)(2,1)S(1)}, bf16[1024,4096]{1,0:T(8,128)(2,1)}, u32[]{:S(2)}) %copy-start) | copy-done | bytes 8388632
  61.4 4.9 %project.1 = bf16[8,256,256]{2,1,0:T(8,128)(2,1)} custom-call(s32[1]{0:T(128)} %bitcast.5.core, bf16[256,1024]{1,0:T(8,128)(2,1)S(1)} %maximum_select_fusion.context, bf16[1024,4096]{1,0:T(8,128)(2,1)S(1)} %copy-done, bf16[1024,4096]{1,0:T(8,128)(2,1)S(1)} %copy-done), custom_call_target="tpu_custom_call" | custom-call | flops 1073741824 | bytes 4194304 | tf_op jit(solution)/shard_map/project/pallas_call | solution.py:150
  66.4 3.0 %collective-permute-done.7.theirs_high = bf16[384,1024]{1,0:T(8,128)(2,1)S(1)} collective-permute-done((bf16[384,1024]{1,0:T(8,128)(2,1)}, bf16[384,1024]{1,0:T(8,128)(2,1)S(1)}, u32[]{:S(2)}, u32[]{:S(2)}) %collective-permute-start.7) | collective-permute-done | bytes 786464 | tf_op jit(solution)/shard_map/ppermute | solution.py:281
  69.4 5.0 %all-to-all-start.1 = ((bf16[8,256,256]{2,1,0:T(8,128)(2,1)}), bf16[8,256,256]{2,1,0:T(8,128)(2,1)}, u32[]{:S(2)}, u32[]{:S(2)}) async-start(bf16[8,256,256]{2,1,0:T(8,128)(2,1)} %project.1), calls=%async_computation.1 | async-start | bytes 2097152 | tf_op jit(solution)/shard_map/all_to_all | solution.py:342
  74.4 1.6 constant_dynamic-slice_fusion
  76.0 1.5 student.1
  77.6 2.9 %collective-permute-start.8 = (bf16[384,256]{1,0:T(8,128)(2,1)S(1)}, bf16[384,256]{1,0:T(8,128)(2,1)S(1)}, u32[]{:S(2)}, u32[]{:S(2)}) collective-permute-start(bf16[384,256]{1,0:T(8,128)(2,1)S(1)} %get-tuple-element.52), channel_id=1, source_target_pairs={{0,128},{128,0},{1,129},{129,1},{2,130},{130,2},{3,131},{131,3},{4... | collective-permute-start | bytes 589832 | tf_op jit(solution)/shard_map/ppermute | solution.py:356
  82.3 5.2 %all-to-all-done.1 = bf16[8,256,256]{2,1,0:T(8,128)(2,1)} async-done(((bf16[8,256,256]{2,1,0:T(8,128)(2,1)}), bf16[8,256,256]{2,1,0:T(8,128)(2,1)}, u32[]{:S(2)}, u32[]{:S(2)}) %all-to-all-start.1) | async-done | bytes 1048608 | tf_op jit(solution)/shard_map/all_to_all | solution.py:342
  87.5 1.4 reduce_sum.44
  88.9 1.1 convolution_convert_fusion
  90.1 19.9 %all_to_all.25 = bf16[16,24,256]{2,1,0:T(8,128)(2,1)S(1)} all-to-all(bf16[16,24,256]{2,1,0:T(8,128)(2,1)S(1)} %bitcast.45), channel_id=1, replica_groups=mesh['group'=2,'tensor'=8,'seq'=16] {'seq'}, dimensions={0} | all-to-all | bytes 393216 | tf_op jit(solution)/shard_map/all_to_all | solution.py:369
  110.0 1.2 fusion.2.mine
  111.2 3.3 %collective-permute-start.9 = (bf16[384,256]{1,0:T(8,128)(2,1)S(1)}, bf16[384,256]{1,0:T(8,128)(2,1)S(1)}, u32[]{:S(2)}, u32[]{:S(2)}) collective-permute-start(bf16[384,256]{1,0:T(8,128)(2,1)S(1)} %fusion.2.mine), channel_id=1, source_target_pairs={{0,128},{128,0},{1,129},{129,1},{2,130},{130,2},{3,131},{131,3},{4... | collective-permute-start | bytes 589832 | tf_op jit(solution)/shard_map/ppermute | solution.py:383
  114.5 1.1 collective-permute-done.9.other
  115.6 1.9 %gradient.1 = bf16[8,256,256]{2,1,0:T(8,128)(2,1)S(1)} custom-call(s32[2]{0:T(128)S(1)} %pad_add_fusion.info.place, bf16[384,1024]{1,0:T(8,128)(2,1)S(1)} %get-tuple-element.58.ours_low, bf16[384,1024]{1,0:T(8,128)(2,1)S(1)} %get-tuple-element.57.ours_high, bf16[384,1024]{1,0:T(8,128)(2,1)S(1)} %collective-permute-done.4.theirs_low, ...), custom_call_target="tpu_custom_call" | custom-call | flops 805306368 | bytes 6291456 | tf_op jit(solution)/shard_map/gradient/pallas_call | solution.py:213
  117.5 30.9 %all_to_all.26 = bf16[8,256,256]{2,1,0:T(8,128)(2,1)S(1)} all-to-all(bf16[8,256,256]{2,1,0:T(8,128)(2,1)S(1)} %gradient.1), channel_id=1, replica_groups={{0,1,2,3,4,5,6,7},{8,9,10,11,12,13,14,15},{16,17,18,19,20,21,22,23},{24..., dimensions={0} | all-to-all | bytes 2097152 | tf_op jit(solution)/shard_map/all_to_all | solution.py:385
  148.5 1.3 collective-permute-start.10
  149.8 6.5 %collective-permute-done.10 = bf16[256,256]{1,0:T(8,128)(2,1)S(1)} collective-permute-done((bf16[256,256]{1,0:T(8,128)(2,1)S(1)}, bf16[256,256]{1,0:T(8,128)(2,1)S(1)}, u32[]{:S(2)}, u32[]{:S(2)}) %collective-permute-start.10) | collective-permute-done | bytes 131104 | tf_op jit(solution)/shard_map/ppermute | solution.py:395
  (63 shorter events, 13.5 us)
Async XLA Ops:
  0.0 5.7 %copy-start.7 = (bf16[1,256,256]{2,1,0:T(8,128)(2,1)S(1)}, bf16[1,256,256]{2,1,0:T(8,128)(2,1)}, u32[]{:S(2)}) copy-start(bf16[1,256,256]{2,1,0:T(8,128)(2,1)} %param.8) | copy-start | bytes 393220
  0.0 5.2 %copy-start.6 = (bf16[256,512]{1,0:T(8,128)(2,1)S(1)}, bf16[256,512]{1,0:T(8,128)(2,1)}, u32[]{:S(2)}) copy-start(bf16[256,512]{1,0:T(8,128)(2,1)} %param.13) | copy-start | bytes 786436
  0.0 13.4 %copy-start.8 = (s32[4096,1]{0,1:T(1,128)S(1)}, s32[4096,1]{0,1:T(1,128)}, u32[]{:S(2)}) copy-start(s32[4096,1]{0,1:T(1,128)} %param.11) | copy-start | bytes 49156
  0.0 5.7 %collective-permute-start = (bf16[256,256]{1,0:T(8,128)(2,1)}, bf16[256,256]{1,0:T(8,128)(2,1)S(1)}, u32[]{:S(2)}, u32[]{:S(2)}) collective-permute-start(bf16[256,256]{1,0:T(8,128)(2,1)} %bitcast.53), channel_id=1, source_target_pairs={{0,128},{1,129},{2,130},{3,131},{4,132},{5,133},{6,134},{7,135},{8... | collective-permute-start | bytes 393224 | tf_op jit(solution)/shard_map/ppermute | solution.py:253
  5.0 20.4 %copy-start.5 = (bf16[1,256,1024]{2,1,0:T(8,128)(2,1)S(1)}, bf16[1,256,1024]{2,1,0:T(8,128)(2,1)}, u32[]{:S(2)}) copy-start(bf16[1,256,1024]{2,1,0:T(8,128)(2,1)} %param.7) | copy-start | bytes 1572868
  5.8 6.7 %collective-permute-start.1 = (bf16[272,384]{1,0:T(8,128)(2,1)S(1)}, bf16[272,384]{1,0:T(8,128)(2,1)S(1)}, u32[]{:S(2)}, u32[]{:S(2)}) collective-permute-start(bf16[272,384]{1,0:T(8,128)(2,1)S(1)} %fusion.5), channel_id=1, source_target_pairs={{0,8},{1,9},{2,10},{3,11},{4,12},{5,13},{6,14},{7,15},{8,0},{9,1},... | collective-permute-start | bytes 626696 | tf_op jit(solution)/shard_map/ppermute | solution.py:259
  13.6 25.2 %all-to-all-start = ((bf16[8,272,128]{2,1,0:T(8,128)(2,1)}), bf16[8,272,128]{2,1,0:T(8,128)(2,1)S(1)}, u32[]{:S(2)}, u32[]{:S(2)}) async-start(bf16[8,272,128]{2,1,0:T(8,128)(2,1)} %broadcast_select_fusion), calls=%async_computation | async-start | bytes 1114112 | tf_op jit(solution)/shard_map/all_to_all | solution.py:277
  25.4 5.1 %collective-permute-start.2 = (bf16[256,512]{1,0:T(8,128)(2,1)S(1)}, bf16[256,512]{1,0:T(8,128)(2,1)S(1)}, u32[]{:S(2)}, u32[]{:S(2)}) collective-permute-start(bf16[256,512]{1,0:T(8,128)(2,1)S(1)} %slice.33), channel_id=1, source_target_pairs={{0,128},{1,129},{2,130},{3,131},{4,132},{5,133},{6,134},{7,135},{8... | collective-permute-start | bytes 786440 | tf_op jit(solution)/shard_map/ppermute | solution.py:284
  26.7 18.5 %collective-permute-start.4 = (bf16[384,1024]{1,0:T(8,128)(2,1)}, bf16[384,1024]{1,0:T(8,128)(2,1)S(1)}, u32[]{:S(2)}, u32[]{:S(2)}) collective-permute-start(bf16[384,1024]{1,0:T(8,128)(2,1)} %get-tuple-element.42), channel_id=1, source_target_pairs={{0,8},{1,9},{2,10},{3,11},{4,12},{5,13},{6,14},{7,15},{8,0},{9,1},... | collective-permute-start | bytes 2359304 | tf_op jit(solution)/shard_map/ppermute | solution.py:281
  31.6 1.4 collective-permute-start.3
  38.7 30.7 %all-to-all-start.2 = ((bf16[8,256,256]{2,1,0:T(8,128)(2,1)}), bf16[8,256,256]{2,1,0:T(8,128)(2,1)S(1)}, u32[]{:S(2)}, u32[]{:S(2)}) async-start(bf16[8,256,256]{2,1,0:T(8,128)(2,1)} %broadcast_in_dim.43), calls=%async_computation.2 | async-start | bytes 2097152 | tf_op jit(solution)/shard_map/all_to_all | solution.py:324
  45.2 6.3 %collective-permute-start.5 = (bf16[10,272,128]{2,1,0:T(8,128)(2,1)S(1)}, bf16[10,272,128]{2,1,0:T(8,128)(2,1)}, u32[]{:S(2)}, u32[]{:S(2)}) collective-permute-start(bf16[10,272,128]{2,1,0:T(8,128)(2,1)S(1)} %pad_maximum_fusion.mine), channel_id=1, source_target_pairs={{0,128},{128,0},{1,129},{129,1},{2,130},{130,2},{3,131},{131,3},{4... | collective-permute-start | bytes 2088968 | tf_op jit(solution)/shard_map/ppermute | solution.py:329
  48.5 20.9 %collective-permute-start.7 = (bf16[384,1024]{1,0:T(8,128)(2,1)}, bf16[384,1024]{1,0:T(8,128)(2,1)S(1)}, u32[]{:S(2)}, u32[]{:S(2)}) collective-permute-start(bf16[384,1024]{1,0:T(8,128)(2,1)} %get-tuple-element.47), channel_id=1, source_target_pairs={{0,8},{1,9},{2,10},{3,11},{4,12},{5,13},{6,14},{7,15},{8,0},{9,1},... | collective-permute-start | bytes 2359304 | tf_op jit(solution)/shard_map/ppermute | solution.py:281
  51.6 1.0 copy-start.4
  56.3 1.6 %collective-permute-start.6 = (bf16[256,512]{1,0:T(8,128)(2,1)S(1)}, bf16[256,512]{1,0:T(8,128)(2,1)S(1)}, u32[]{:S(2)}, u32[]{:S(2)}) collective-permute-start(bf16[256,512]{1,0:T(8,128)(2,1)S(1)} %attend.1), channel_id=1, source_target_pairs={{0,128},{128,0},{1,129},{129,1},{2,130},{130,2},{3,131},{131,3},{4... | collective-permute-start | bytes 786440 | tf_op jit(solution)/shard_map/ppermute | solution.py:334
  58.1 3.4 %copy-start = (bf16[1024,4096]{1,0:T(8,128)(2,1)S(1)}, bf16[1024,4096]{1,0:T(8,128)(2,1)}, u32[]{:S(2)}) copy-start(bf16[1024,4096]{1,0:T(8,128)(2,1)} %high.1) | copy-start | bytes 25165828
  69.4 5.0 %copy-start.1 = (bf16[384,1024]{1,0:T(8,128)(2,1)}, bf16[384,1024]{1,0:T(8,128)(2,1)S(1)}, u32[]{:S(2)}) copy-start(bf16[384,1024]{1,0:T(8,128)(2,1)S(1)} %collective-permute-done.7.theirs_high) | copy-start | bytes 2359300
  69.4 18.1 %all-to-all-start.1 = ((bf16[8,256,256]{2,1,0:T(8,128)(2,1)}), bf16[8,256,256]{2,1,0:T(8,128)(2,1)}, u32[]{:S(2)}, u32[]{:S(2)}) async-start(bf16[8,256,256]{2,1,0:T(8,128)(2,1)} %project.1), calls=%async_computation.1 | async-start | bytes 2097152 | tf_op jit(solution)/shard_map/all_to_all | solution.py:342
  74.4 1.6 %copy-start.2 = (bf16[384,1024]{1,0:T(8,128)(2,1)S(1)}, bf16[384,1024]{1,0:T(8,128)(2,1)}, u32[]{:S(2)}) copy-start(bf16[384,1024]{1,0:T(8,128)(2,1)} %copy-done.1) | copy-start | bytes 2359300
  77.6 38.0 %copy-start.3 = (bf16[384,1024]{1,0:T(8,128)(2,1)S(1)}, bf16[384,1024]{1,0:T(8,128)(2,1)}, u32[]{:S(2)}) copy-start(bf16[384,1024]{1,0:T(8,128)(2,1)} %copy-done.1) | copy-start | bytes 2359300
  77.6 4.0 %collective-permute-start.8 = (bf16[384,256]{1,0:T(8,128)(2,1)S(1)}, bf16[384,256]{1,0:T(8,128)(2,1)S(1)}, u32[]{:S(2)}, u32[]{:S(2)}) collective-permute-start(bf16[384,256]{1,0:T(8,128)(2,1)S(1)} %get-tuple-element.52), channel_id=1, source_target_pairs={{0,128},{128,0},{1,129},{129,1},{2,130},{130,2},{3,131},{131,3},{4... | collective-permute-start | bytes 589832 | tf_op jit(solution)/shard_map/ppermute | solution.py:356
  111.2 4.4 %collective-permute-start.9 = (bf16[384,256]{1,0:T(8,128)(2,1)S(1)}, bf16[384,256]{1,0:T(8,128)(2,1)S(1)}, u32[]{:S(2)}, u32[]{:S(2)}) collective-permute-start(bf16[384,256]{1,0:T(8,128)(2,1)S(1)} %fusion.2.mine), channel_id=1, source_target_pairs={{0,128},{128,0},{1,129},{129,1},{2,130},{130,2},{3,131},{131,3},{4... | collective-permute-start | bytes 589832 | tf_op jit(solution)/shard_map/ppermute | solution.py:383
  148.5 7.8 %collective-permute-start.10 = (bf16[256,256]{1,0:T(8,128)(2,1)S(1)}, bf16[256,256]{1,0:T(8,128)(2,1)S(1)}, u32[]{:S(2)}, u32[]{:S(2)}) collective-permute-start(bf16[256,256]{1,0:T(8,128)(2,1)S(1)} %reduce_sum.45), channel_id=1, source_target_pairs={{0,136},{1,137},{2,138},{3,139},{4,140},{5,141},{6,142},{7,143},{8... | collective-permute-start | bytes 393224 | tf_op jit(solution)/shard_map/ppermute | solution.py:395

commit v7 on v6

--- a/solution.py
+++ b/solution.py
@@ -170,6 +170,19 @@
     )(core, context, projector, projector)
 
 
+def route_kernel(route, partial, out):
+    target = partial[0].astype(jnp.float32)
+    for index in range(1, partial.shape[0]):
+        target = target + partial[index].astype(jnp.float32)
+    routed = jnp.dot(
+        route[...], target.astype(jnp.bfloat16), preferred_element_type=jnp.float32
+    ).astype(jnp.bfloat16)
+    rows, lanes = out.shape[1], out.shape[2] // 2
+    low, high = routed[:rows], routed[rows:]
+    out[0] = jnp.concatenate([low[:, :lanes], high[:, :lanes]], axis=1)
+    out[1] = jnp.concatenate([high[:, lanes:], low[:, lanes:]], axis=1)
+
+
 def student_kernel(place, ours_low, ours_high, theirs_low, theirs_high, weight, kept, sent):
     core = place[1]
     middle = ours_low.shape[1]
@@ -355,17 +368,16 @@
     )
     output = output + lax.ppermute(given, "group", core_swap).astype(jnp.float32)
     partial, output = lax.optimization_barrier((partial, output))
-    target = jnp.sum(partial.astype(jnp.float32), axis=0).astype(jnp.bfloat16)
-
-    routed = jnp.dot(route, target, preferred_element_type=jnp.float32).astype(jnp.bfloat16)
-    routed = routed.reshape(2, ZN, capacity, feats)
-    lanes = feats // 2
-    routed = jnp.stack(
-        [
-            jnp.concatenate([routed[0, :, :, :lanes], routed[1, :, :, :lanes]], axis=-1),
-            jnp.concatenate([routed[1, :, :, lanes:], routed[0, :, :, lanes:]], axis=-1),
-        ]
-    ).reshape(owners_n, capacity, feats)
+
+    routed = pl.pallas_call(
+        route_kernel,
+        out_shape=jax.ShapeDtypeStruct((2, slots // 2, feats), jnp.bfloat16),
+        compiler_params=pltpu.CompilerParams(vmem_limit_bytes=16 * 1024 * 1024),
+        cost_estimate=pl.CostEstimate(
+            flops=2 * slots * tok * feats, bytes_accessed=2 << 20, transcendentals=0
+        ),
+        name="route",
+    )(route, partial).reshape(owners_n, capacity, feats)
     routed = lax.all_to_all(
         routed, "seq", split_axis=0, concat_axis=0, tiled=True
     ).reshape(slots, feats)

time: 158 us -> 158 us (level)
    unnamed x19 -> x21, local copies, waits for them, and re-layouts: 5.15 us -> 6.08 us
  transfers between devices with their start and end apart: 14 -> 14, of which waited for: 10 -> 10; matrix products, arithmetic and copies ran while one was open for 8% -> 8% of each run, Pallas kernels for 6% -> 7%
where the time goes in v7:
time: 158 us; the launch traced here: 157 us
  blocking collectives  50.8 us (32%)
  starting transfers between devices  41.4 us (26%)
  waiting for transfers between devices  30.4 us (19%)
  Pallas kernels  13.6 us (9%)
  local copies, waits for them, and re-layouts  12.7 us (8%)
  other arithmetic  7.81 us (5%)
    all_to_all x1, blocking collectives, shards(): lax.all_to_all(gradient, 'seq', split_axis=0, concat_axis=0, tiled=True,...  30.9 us
    all_to_all x1, blocking collectives, shards(): lax.all_to_all(routed, 'seq', split_axis=0, concat_axis=0, tiled=True)  19.9 us
    all_to_all x1, starting transfers between devices, shards(): lax.all_to_all(pieces, 'seq', split_axis=0, concat_axis=0, tiled=True, ax...  8.99 us
    ppermute x1, waiting for transfers between devices, shards(): lax.ppermute(gradient, both, [(h * ZN + z, (3 - h) * ZN + z) for h in ran...  6.49 us
    unnamed x21, local copies, waits for them, and re-layouts  6.08 us
    ppermute x2, starting transfers between devices, shards(): theirs = [lax.ppermute(part, both, all_pairs) for part in sent]  5.92 us
    ppermute x2, waiting for transfers between devices, shards(): theirs = [lax.ppermute(part, both, all_pairs) for part in sent]  5.84 us
    all_to_all x1, waiting for transfers between devices, shards(): lax.all_to_all(pieces, 'seq', split_axis=0, concat_axis=0, tiled=True, ax...  5.75 us
  transfers between devices with their start and end apart: 14, of which 10 were waited for; matrix products, arithmetic and copies ran while one was open for 8% of the time, Pallas kernels for 7%

profile of v7, /device:TPU:1, one launch (start us, length us, event | category | flops | bytes accessed | tf_op | source)
XLA Modules:
  0.0 157.0 jit_solution(15399537721967412563)
XLA Ops:
  0.0 1.4 collective-permute-start
  2.3 2.7 %constant_dynamic-slice_fusion.3 = (bf16[384,1024]{1,0:T(8,128)(2,1)}, bf16[384,1024]{1,0:T(8,128)(2,1)}) fusion(bf16[384,4096]{1,0:T(8,128)(2,1)} %param.12, s32[]{:T(128)S(6)} %select_n.113, s32[]{:T(128)S(6)} %select_n.112), kind=kLoop, calls=%fused_computation.29 | loop fusion | bytes 3145736 | tf_op jit(solution)/shard_map/dynamic_slice | solution.py:280
  5.8 3.4 %collective-permute-start.1 = (bf16[272,384]{1,0:T(8,128)(2,1)S(1)}, bf16[272,384]{1,0:T(8,128)(2,1)S(1)}, u32[]{:S(2)}, u32[]{:S(2)}) collective-permute-start(bf16[272,384]{1,0:T(8,128)(2,1)S(1)} %fusion.5), channel_id=1, source_target_pairs={{0,8},{1,9},{2,10},{3,11},{4,12},{5,13},{6,14},{7,15},{8,0},{9,1},... | collective-permute-start | bytes 626696 | tf_op jit(solution)/shard_map/ppermute | solution.py:272
  9.1 3.3 %collective-permute-done.1 = bf16[272,384]{1,0:T(8,128)(2,1)S(1)} collective-permute-done((bf16[272,384]{1,0:T(8,128)(2,1)S(1)}, bf16[272,384]{1,0:T(8,128)(2,1)S(1)}, u32[]{:S(2)}, u32[]{:S(2)}) %collective-permute-start.1) | collective-permute-done | bytes 208928 | tf_op jit(solution)/shard_map/ppermute | solution.py:272
  13.5 9.0 %all-to-all-start = ((bf16[8,272,128]{2,1,0:T(8,128)(2,1)}), bf16[8,272,128]{2,1,0:T(8,128)(2,1)S(1)}, u32[]{:S(2)}, u32[]{:S(2)}) async-start(bf16[8,272,128]{2,1,0:T(8,128)(2,1)} %broadcast_select_fusion), calls=%async_computation | async-start | bytes 1114112 | tf_op jit(solution)/shard_map/all_to_all | solution.py:290
  25.4 1.3 collective-permute-start.2
  26.7 3.0 %collective-permute-start.4 = (bf16[384,1024]{1,0:T(8,128)(2,1)}, bf16[384,1024]{1,0:T(8,128)(2,1)S(1)}, u32[]{:S(2)}, u32[]{:S(2)}) collective-permute-start(bf16[384,1024]{1,0:T(8,128)(2,1)} %get-tuple-element.42), channel_id=1, source_target_pairs={{0,8},{1,9},{2,10},{3,11},{4,12},{5,13},{6,14},{7,15},{8,0},{9,1},... | collective-permute-start | bytes 2359304 | tf_op jit(solution)/shard_map/ppermute | solution.py:294
  33.0 5.7 %all-to-all-done = bf16[8,272,128]{2,1,0:T(8,128)(2,1)S(1)} async-done(((bf16[8,272,128]{2,1,0:T(8,128)(2,1)}), bf16[8,272,128]{2,1,0:T(8,128)(2,1)S(1)}, u32[]{:S(2)}, u32[]{:S(2)}) %all-to-all-start) | async-done | bytes 557088 | tf_op jit(solution)/shard_map/all_to_all | solution.py:290
  38.7 3.6 %all-to-all-start.2 = ((bf16[8,256,256]{2,1,0:T(8,128)(2,1)}), bf16[8,256,256]{2,1,0:T(8,128)(2,1)S(1)}, u32[]{:S(2)}, u32[]{:S(2)}) async-start(bf16[8,256,256]{2,1,0:T(8,128)(2,1)} %broadcast_in_dim.43), calls=%async_computation.2 | async-start | bytes 2097152 | tf_op jit(solution)/shard_map/all_to_all | solution.py:337
  42.4 2.8 %collective-permute-done.4.theirs_low = bf16[384,1024]{1,0:T(8,128)(2,1)S(1)} collective-permute-done((bf16[384,1024]{1,0:T(8,128)(2,1)}, bf16[384,1024]{1,0:T(8,128)(2,1)S(1)}, u32[]{:S(2)}, u32[]{:S(2)}) %collective-permute-start.4) | collective-permute-done | bytes 786464 | tf_op jit(solution)/shard_map/ppermute | solution.py:294
  45.2 3.3 %collective-permute-start.5 = (bf16[10,272,128]{2,1,0:T(8,128)(2,1)S(1)}, bf16[10,272,128]{2,1,0:T(8,128)(2,1)}, u32[]{:S(2)}, u32[]{:S(2)}) collective-permute-start(bf16[10,272,128]{2,1,0:T(8,128)(2,1)S(1)} %pad_maximum_fusion.mine), channel_id=1, source_target_pairs={{0,128},{128,0},{1,129},{129,1},{2,130},{130,2},{3,131},{131,3},{4... | collective-permute-start | bytes 2088968 | tf_op jit(solution)/shard_map/ppermute | solution.py:342
  48.5 2.9 %collective-permute-start.7 = (bf16[384,1024]{1,0:T(8,128)(2,1)}, bf16[384,1024]{1,0:T(8,128)(2,1)S(1)}, u32[]{:S(2)}, u32[]{:S(2)}) collective-permute-start(bf16[384,1024]{1,0:T(8,128)(2,1)} %get-tuple-element.47), channel_id=1, source_target_pairs={{0,8},{1,9},{2,10},{3,11},{4,12},{5,13},{6,14},{7,15},{8,0},{9,1},... | collective-permute-start | bytes 2359304 | tf_op jit(solution)/shard_map/ppermute | solution.py:294
  52.5 3.8 %attend.1 = bf16[256,512]{1,0:T(8,128)(2,1)S(1)} custom-call(s32[2]{0:T(128)S(1)} %pad_add_fusion.info.place, bf16[256,512]{1,0:T(8,128)(2,1)S(1)} %copy-done.5, f32[256,1]{1,0:T(8,128)S(1)} %copy.10.seg_query, bf16[10,272,128]{2,1,0:T(8,128)(2,1)S(1)} %pad_maximum_fusion.mine, bf16[10,272,128]{2,1,0:T(8,128)(2,1)} %collective-permute-done.5.other), custom_call_target="tpu_custom_call" | custom-call | flops 2684354560 | bytes 4194304 | tf_op jit(solution)/shard_map/attend/pallas_call | solution.py:119
  56.7 1.3 collective-permute-done.6
  58.1 3.4 %copy-done = bf16[1024,4096]{1,0:T(8,128)(2,1)S(1)} copy-done((bf16[1024,4096]{1,0:T(8,128)(2,1)S(1)}, bf16[1024,4096]{1,0:T(8,128)(2,1)}, u32[]{:S(2)}) %copy-start) | copy-done | bytes 8388632
  61.4 4.9 %project.1 = bf16[8,256,256]{2,1,0:T(8,128)(2,1)} custom-call(s32[1]{0:T(128)} %bitcast.5.core, bf16[256,1024]{1,0:T(8,128)(2,1)S(1)} %maximum_select_fusion.context, bf16[1024,4096]{1,0:T(8,128)(2,1)S(1)} %copy-done, bf16[1024,4096]{1,0:T(8,128)(2,1)S(1)} %copy-done), custom_call_target="tpu_custom_call" | custom-call | flops 1073741824 | bytes 4194304 | tf_op jit(solution)/shard_map/project/pallas_call | solution.py:150
  66.4 3.0 %collective-permute-done.7.theirs_high = bf16[384,1024]{1,0:T(8,128)(2,1)S(1)} collective-permute-done((bf16[384,1024]{1,0:T(8,128)(2,1)}, bf16[384,1024]{1,0:T(8,128)(2,1)S(1)}, u32[]{:S(2)}, u32[]{:S(2)}) %collective-permute-start.7) | collective-permute-done | bytes 786464 | tf_op jit(solution)/shard_map/ppermute | solution.py:294
  69.4 5.0 %all-to-all-start.1 = ((bf16[8,256,256]{2,1,0:T(8,128)(2,1)}), bf16[8,256,256]{2,1,0:T(8,128)(2,1)}, u32[]{:S(2)}, u32[]{:S(2)}) async-start(bf16[8,256,256]{2,1,0:T(8,128)(2,1)} %project.1), calls=%async_computation.1 | async-start | bytes 2097152 | tf_op jit(solution)/shard_map/all_to_all | solution.py:355
  74.4 1.6 constant_dynamic-slice_fusion
  76.0 1.5 student.1
  77.6 2.9 %collective-permute-start.8 = (bf16[384,256]{1,0:T(8,128)(2,1)S(1)}, bf16[384,256]{1,0:T(8,128)(2,1)S(1)}, u32[]{:S(2)}, u32[]{:S(2)}) collective-permute-start(bf16[384,256]{1,0:T(8,128)(2,1)S(1)} %get-tuple-element.52), channel_id=1, source_target_pairs={{0,128},{128,0},{1,129},{129,1},{2,130},{130,2},{3,131},{131,3},{4... | collective-permute-start | bytes 589832 | tf_op jit(solution)/shard_map/ppermute | solution.py:369
  80.5 1.1 collective-permute-done.8
  82.3 5.2 %all-to-all-done.1.partial = bf16[8,256,256]{2,1,0:T(8,128)(2,1)} async-done(((bf16[8,256,256]{2,1,0:T(8,128)(2,1)}), bf16[8,256,256]{2,1,0:T(8,128)(2,1)}, u32[]{:S(2)}, u32[]{:S(2)}) %all-to-all-start.1) | async-done | bytes 1048608 | tf_op jit(solution)/shard_map/all_to_all | solution.py:355
  88.4 1.5 route.1
  90.0 19.9 %all_to_all.25 = bf16[16,24,256]{2,1,0:T(8,128)(2,1)S(1)} all-to-all(bf16[16,24,256]{2,1,0:T(8,128)(2,1)S(1)} %bitcast.28), channel_id=1, replica_groups=mesh['group'=2,'tensor'=8,'seq'=16] {'seq'}, dimensions={0} | all-to-all | bytes 393216 | tf_op jit(solution)/shard_map/all_to_all | solution.py:381
  109.8 1.2 fusion.2.mine
  111.0 3.3 %collective-permute-start.9 = (bf16[384,256]{1,0:T(8,128)(2,1)S(1)}, bf16[384,256]{1,0:T(8,128)(2,1)S(1)}, u32[]{:S(2)}, u32[]{:S(2)}) collective-permute-start(bf16[384,256]{1,0:T(8,128)(2,1)S(1)} %fusion.2.mine), channel_id=1, source_target_pairs={{0,128},{128,0},{1,129},{129,1},{2,130},{130,2},{3,131},{131,3},{4... | collective-permute-start | bytes 589832 | tf_op jit(solution)/shard_map/ppermute | solution.py:395
  114.4 1.1 collective-permute-done.9.other
  115.4 1.9 %gradient.1 = bf16[8,256,256]{2,1,0:T(8,128)(2,1)S(1)} custom-call(s32[2]{0:T(128)S(1)} %pad_add_fusion.info.place, bf16[384,1024]{1,0:T(8,128)(2,1)S(1)} %get-tuple-element.58.ours_low, bf16[384,1024]{1,0:T(8,128)(2,1)S(1)} %get-tuple-element.57.ours_high, bf16[384,1024]{1,0:T(8,128)(2,1)S(1)} %collective-permute-done.4.theirs_low, ...), custom_call_target="tpu_custom_call" | custom-call | flops 805306368 | bytes 6291456 | tf_op jit(solution)/shard_map/gradient/pallas_call | solution.py:226
  117.3 30.9 %all_to_all.26 = bf16[8,256,256]{2,1,0:T(8,128)(2,1)S(1)} all-to-all(bf16[8,256,256]{2,1,0:T(8,128)(2,1)S(1)} %gradient.1), channel_id=1, replica_groups={{0,1,2,3,4,5,6,7},{8,9,10,11,12,13,14,15},{16,17,18,19,20,21,22,23},{24..., dimensions={0} | all-to-all | bytes 2097152 | tf_op jit(solution)/shard_map/all_to_all | solution.py:397
  148.3 1.3 collective-permute-start.10
  149.6 6.5 %collective-permute-done.10 = bf16[256,256]{1,0:T(8,128)(2,1)S(1)} collective-permute-done((bf16[256,256]{1,0:T(8,128)(2,1)S(1)}, bf16[256,256]{1,0:T(8,128)(2,1)S(1)}, u32[]{:S(2)}, u32[]{:S(2)}) %collective-permute-start.10) | collective-permute-done | bytes 131104 | tf_op jit(solution)/shard_map/ppermute | solution.py:407
  (61 shorter events, 13.2 us)
Async XLA Ops:
  0.0 5.7 %copy-start.8 = (bf16[1,256,256]{2,1,0:T(8,128)(2,1)S(1)}, bf16[1,256,256]{2,1,0:T(8,128)(2,1)}, u32[]{:S(2)}) copy-start(bf16[1,256,256]{2,1,0:T(8,128)(2,1)} %param.8) | copy-start | bytes 393220
  0.0 5.2 %copy-start.7 = (bf16[256,512]{1,0:T(8,128)(2,1)S(1)}, bf16[256,512]{1,0:T(8,128)(2,1)}, u32[]{:S(2)}) copy-start(bf16[256,512]{1,0:T(8,128)(2,1)} %param.13) | copy-start | bytes 786436
  0.0 13.4 %copy-start.9 = (s32[4096,1]{0,1:T(1,128)S(1)}, s32[4096,1]{0,1:T(1,128)}, u32[]{:S(2)}) copy-start(s32[4096,1]{0,1:T(1,128)} %param.11) | copy-start | bytes 49156
  0.0 5.7 %collective-permute-start = (bf16[256,256]{1,0:T(8,128)(2,1)}, bf16[256,256]{1,0:T(8,128)(2,1)S(1)}, u32[]{:S(2)}, u32[]{:S(2)}) collective-permute-start(bf16[256,256]{1,0:T(8,128)(2,1)} %bitcast.37), channel_id=1, source_target_pairs={{0,128},{1,129},{2,130},{3,131},{4,132},{5,133},{6,134},{7,135},{8... | collective-permute-start | bytes 393224 | tf_op jit(solution)/shard_map/ppermute | solution.py:266
  5.0 20.4 %copy-start.6 = (bf16[1,256,1024]{2,1,0:T(8,128)(2,1)S(1)}, bf16[1,256,1024]{2,1,0:T(8,128)(2,1)}, u32[]{:S(2)}) copy-start(bf16[1,256,1024]{2,1,0:T(8,128)(2,1)} %param.7) | copy-start | bytes 1572868
  5.8 6.7 %collective-permute-start.1 = (bf16[272,384]{1,0:T(8,128)(2,1)S(1)}, bf16[272,384]{1,0:T(8,128)(2,1)S(1)}, u32[]{:S(2)}, u32[]{:S(2)}) collective-permute-start(bf16[272,384]{1,0:T(8,128)(2,1)S(1)} %fusion.5), channel_id=1, source_target_pairs={{0,8},{1,9},{2,10},{3,11},{4,12},{5,13},{6,14},{7,15},{8,0},{9,1},... | collective-permute-start | bytes 626696 | tf_op jit(solution)/shard_map/ppermute | solution.py:272
  13.5 25.2 %all-to-all-start = ((bf16[8,272,128]{2,1,0:T(8,128)(2,1)}), bf16[8,272,128]{2,1,0:T(8,128)(2,1)S(1)}, u32[]{:S(2)}, u32[]{:S(2)}) async-start(bf16[8,272,128]{2,1,0:T(8,128)(2,1)} %broadcast_select_fusion), calls=%async_computation | async-start | bytes 1114112 | tf_op jit(solution)/shard_map/all_to_all | solution.py:290
  25.4 5.1 %collective-permute-start.2 = (bf16[256,512]{1,0:T(8,128)(2,1)S(1)}, bf16[256,512]{1,0:T(8,128)(2,1)S(1)}, u32[]{:S(2)}, u32[]{:S(2)}) collective-permute-start(bf16[256,512]{1,0:T(8,128)(2,1)S(1)} %slice.21), channel_id=1, source_target_pairs={{0,128},{1,129},{2,130},{3,131},{4,132},{5,133},{6,134},{7,135},{8... | collective-permute-start | bytes 786440 | tf_op jit(solution)/shard_map/ppermute | solution.py:297
  26.7 18.5 %collective-permute-start.4 = (bf16[384,1024]{1,0:T(8,128)(2,1)}, bf16[384,1024]{1,0:T(8,128)(2,1)S(1)}, u32[]{:S(2)}, u32[]{:S(2)}) collective-permute-start(bf16[384,1024]{1,0:T(8,128)(2,1)} %get-tuple-element.42), channel_id=1, source_target_pairs={{0,8},{1,9},{2,10},{3,11},{4,12},{5,13},{6,14},{7,15},{8,0},{9,1},... | collective-permute-start | bytes 2359304 | tf_op jit(solution)/shard_map/ppermute | solution.py:294
  31.5 1.4 collective-permute-start.3
  38.7 30.7 %all-to-all-start.2 = ((bf16[8,256,256]{2,1,0:T(8,128)(2,1)}), bf16[8,256,256]{2,1,0:T(8,128)(2,1)S(1)}, u32[]{:S(2)}, u32[]{:S(2)}) async-start(bf16[8,256,256]{2,1,0:T(8,128)(2,1)} %broadcast_in_dim.43), calls=%async_computation.2 | async-start | bytes 2097152 | tf_op jit(solution)/shard_map/all_to_all | solution.py:337
  45.2 6.3 %collective-permute-start.5 = (bf16[10,272,128]{2,1,0:T(8,128)(2,1)S(1)}, bf16[10,272,128]{2,1,0:T(8,128)(2,1)}, u32[]{:S(2)}, u32[]{:S(2)}) collective-permute-start(bf16[10,272,128]{2,1,0:T(8,128)(2,1)S(1)} %pad_maximum_fusion.mine), channel_id=1, source_target_pairs={{0,128},{128,0},{1,129},{129,1},{2,130},{130,2},{3,131},{131,3},{4... | collective-permute-start | bytes 2088968 | tf_op jit(solution)/shard_map/ppermute | solution.py:342
  48.5 20.9 %collective-permute-start.7 = (bf16[384,1024]{1,0:T(8,128)(2,1)}, bf16[384,1024]{1,0:T(8,128)(2,1)S(1)}, u32[]{:S(2)}, u32[]{:S(2)}) collective-permute-start(bf16[384,1024]{1,0:T(8,128)(2,1)} %get-tuple-element.47), channel_id=1, source_target_pairs={{0,8},{1,9},{2,10},{3,11},{4,12},{5,13},{6,14},{7,15},{8,0},{9,1},... | collective-permute-start | bytes 2359304 | tf_op jit(solution)/shard_map/ppermute | solution.py:294
  51.5 1.0 copy-start.5
  56.3 1.6 %collective-permute-start.6 = (bf16[256,512]{1,0:T(8,128)(2,1)S(1)}, bf16[256,512]{1,0:T(8,128)(2,1)S(1)}, u32[]{:S(2)}, u32[]{:S(2)}) collective-permute-start(bf16[256,512]{1,0:T(8,128)(2,1)S(1)} %attend.1), channel_id=1, source_target_pairs={{0,128},{128,0},{1,129},{129,1},{2,130},{130,2},{3,131},{131,3},{4... | collective-permute-start | bytes 786440 | tf_op jit(solution)/shard_map/ppermute | solution.py:347
  58.0 3.4 %copy-start = (bf16[1024,4096]{1,0:T(8,128)(2,1)S(1)}, bf16[1024,4096]{1,0:T(8,128)(2,1)}, u32[]{:S(2)}) copy-start(bf16[1024,4096]{1,0:T(8,128)(2,1)} %high.1) | copy-start | bytes 25165828
  69.4 5.0 %copy-start.1 = (bf16[384,1024]{1,0:T(8,128)(2,1)}, bf16[384,1024]{1,0:T(8,128)(2,1)S(1)}, u32[]{:S(2)}) copy-start(bf16[384,1024]{1,0:T(8,128)(2,1)S(1)} %collective-permute-done.7.theirs_high) | copy-start | bytes 2359300
  69.4 18.1 %all-to-all-start.1 = ((bf16[8,256,256]{2,1,0:T(8,128)(2,1)}), bf16[8,256,256]{2,1,0:T(8,128)(2,1)}, u32[]{:S(2)}, u32[]{:S(2)}) async-start(bf16[8,256,256]{2,1,0:T(8,128)(2,1)} %project.1), calls=%async_computation.1 | async-start | bytes 2097152 | tf_op jit(solution)/shard_map/all_to_all | solution.py:355
  74.4 1.6 %copy-start.2 = (bf16[384,1024]{1,0:T(8,128)(2,1)S(1)}, bf16[384,1024]{1,0:T(8,128)(2,1)}, u32[]{:S(2)}) copy-start(bf16[384,1024]{1,0:T(8,128)(2,1)} %copy-done.1) | copy-start | bytes 2359300
  77.5 37.9 %copy-start.3 = (bf16[384,1024]{1,0:T(8,128)(2,1)S(1)}, bf16[384,1024]{1,0:T(8,128)(2,1)}, u32[]{:S(2)}) copy-start(bf16[384,1024]{1,0:T(8,128)(2,1)} %copy-done.1) | copy-start | bytes 2359300
  77.6 4.0 %collective-permute-start.8 = (bf16[384,256]{1,0:T(8,128)(2,1)S(1)}, bf16[384,256]{1,0:T(8,128)(2,1)S(1)}, u32[]{:S(2)}, u32[]{:S(2)}) collective-permute-start(bf16[384,256]{1,0:T(8,128)(2,1)S(1)} %get-tuple-element.52), channel_id=1, source_target_pairs={{0,128},{128,0},{1,129},{129,1},{2,130},{130,2},{3,131},{131,3},{4... | collective-permute-start | bytes 589832 | tf_op jit(solution)/shard_map/ppermute | solution.py:369
  87.5 0.9 copy-start.4
  111.0 4.4 %collective-permute-start.9 = (bf16[384,256]{1,0:T(8,128)(2,1)S(1)}, bf16[384,256]{1,0:T(8,128)(2,1)S(1)}, u32[]{:S(2)}, u32[]{:S(2)}) collective-permute-start(bf16[384,256]{1,0:T(8,128)(2,1)S(1)} %fusion.2.mine), channel_id=1, source_target_pairs={{0,128},{128,0},{1,129},{129,1},{2,130},{130,2},{3,131},{131,3},{4... | collective-permute-start | bytes 589832 | tf_op jit(solution)/shard_map/ppermute | solution.py:395
  148.3 7.8 %collective-permute-start.10 = (bf16[256,256]{1,0:T(8,128)(2,1)S(1)}, bf16[256,256]{1,0:T(8,128)(2,1)S(1)}, u32[]{:S(2)}, u32[]{:S(2)}) collective-permute-start(bf16[256,256]{1,0:T(8,128)(2,1)S(1)} %reduce_sum.32), channel_id=1, source_target_pairs={{0,136},{1,137},{2,138},{3,139},{4,140},{5,141},{6,142},{7,143},{8... | collective-permute-start | bytes 393224 | tf_op jit(solution)/shard_map/ppermute | solution.py:407

commit v8 on v7

--- a/solution.py
+++ b/solution.py
@@ -266,6 +266,7 @@
     passed = lax.ppermute(keyval, "group", [(0, 1)])
     piece = jnp.where(group == 0, keyval[:, :HD], passed[:, HD:])
     piece = jnp.concatenate([piece, seg_rows], axis=0)
+    piece, student_context = lax.optimization_barrier((piece, student_context))
     column_half = jnp.where(group == 1, high, 1 - high)
     crossing = lax.dynamic_slice_in_dim(student_out_weight, (1 - high) * feats, feats, axis=1)
     crossing = jnp.concatenate([crossing, jnp.zeros((16, feats), crossing.dtype)], axis=0)

time: 158 us -> 157 us (level)
  starting transfers between devices: 41.4 us -> 37.7 us
    all_to_all x1, starting transfers between devices: 8.99 us -> 6.91 us  [shards(): lax.all_to_all(pieces, 'seq', split_axis=0, concat_axis=0, tiled=True, ax...]
    ppermute x1, waiting for transfers between devices: 0.49 us -> 2.22 us  [shards(): passed = lax.ppermute(keyval, 'group', [(0, 1)])]
    ppermute x1, starting transfers between devices: 3.36 us -> 1.71 us  [shards(): lax.ppermute(jnp.concatenate([crossing, piece], axis=1), both, all_pairs)]
    unnamed x21 -> x19, local copies, waits for them, and re-layouts: 6.08 us -> 6.08 us
where the time goes in v8:
time: 157 us; the launch traced here: 156 us
  blocking collectives  50.8 us (32%)
  starting transfers between devices  37.7 us (24%)
  waiting for transfers between devices  31.5 us (20%)
  local copies, waits for them, and re-layouts  13.8 us (9%)
  Pallas kernels  13.6 us (9%)
  other arithmetic  8.72 us (6%)
    all_to_all x1, blocking collectives, shards(): lax.all_to_all(gradient, 'seq', split_axis=0, concat_axis=0, tiled=True,...  30.9 us
    all_to_all x1, blocking collectives, shards(): lax.all_to_all(routed, 'seq', split_axis=0, concat_axis=0, tiled=True)  20 us
    all_to_all x1, starting transfers between devices, shards(): lax.all_to_all(pieces, 'seq', split_axis=0, concat_axis=0, tiled=True, ax...  6.91 us
    ppermute x1, waiting for transfers between devices, shards(): lax.ppermute(gradient, both, [(h * ZN + z, (3 - h) * ZN + z) for h in ran...  6.49 us
    unnamed x19, local copies, waits for them, and re-layouts  6.08 us
    ppermute x2, starting transfers between devices, shards(): theirs = [lax.ppermute(part, both, all_pairs) for part in sent]  5.92 us
    all_to_all x1, waiting for transfers between devices, shards(): lax.all_to_all(pieces, 'seq', split_axis=0, concat_axis=0, tiled=True, ax...  5.83 us
    ppermute x2, waiting for transfers between devices, shards(): theirs = [lax.ppermute(part, both, all_pairs) for part in sent]  5.83 us
  transfers between devices with their start and end apart: 14, of which 10 were waited for; matrix products, arithmetic and copies ran while one was open for 8% of the time, Pallas kernels for 7%

profile of v8, /device:TPU:1, one launch (start us, length us, event | category | flops | bytes accessed | tf_op | source)
XLA Modules:
  0.0 156.4 jit_solution(16076372781298085405)
XLA Ops:
  0.0 1.4 collective-permute-start
  3.5 2.2 %collective-permute-done = bf16[256,256]{1,0:T(8,128)(2,1)S(1)} collective-permute-done((bf16[256,256]{1,0:T(8,128)(2,1)}, bf16[256,256]{1,0:T(8,128)(2,1)S(1)}, u32[]{:S(2)}, u32[]{:S(2)}) %collective-permute-start) | collective-permute-done | bytes 131104 | tf_op jit(solution)/shard_map/ppermute | solution.py:266
  6.7 1.7 %collective-permute-start.1 = (bf16[272,384]{1,0:T(8,128)(2,1)S(1)}, bf16[272,384]{1,0:T(8,128)(2,1)S(1)}, u32[]{:S(2)}, u32[]{:S(2)}) collective-permute-start(bf16[272,384]{1,0:T(8,128)(2,1)S(1)} %fusion.5), channel_id=1, source_target_pairs={{0,8},{1,9},{2,10},{3,11},{4,12},{5,13},{6,14},{7,15},{8,0},{9,1},... | collective-permute-start | bytes 626696 | tf_op jit(solution)/shard_map/ppermute | solution.py:273
  8.4 2.8 %constant_dynamic-slice_fusion.3 = (bf16[384,1024]{1,0:T(8,128)(2,1)}, bf16[384,1024]{1,0:T(8,128)(2,1)}) fusion(bf16[384,4096]{1,0:T(8,128)(2,1)} %param.12, s32[]{:T(128)S(6)} %select_n.113, s32[]{:T(128)S(6)} %select_n.112), kind=kLoop, calls=%fused_computation.29 | loop fusion | bytes 3145736 | tf_op jit(solution)/shard_map/dynamic_slice | solution.py:281
  11.2 2.7 %collective-permute-done.1 = bf16[272,384]{1,0:T(8,128)(2,1)S(1)} collective-permute-done((bf16[272,384]{1,0:T(8,128)(2,1)S(1)}, bf16[272,384]{1,0:T(8,128)(2,1)S(1)}, u32[]{:S(2)}, u32[]{:S(2)}) %collective-permute-start.1) | collective-permute-done | bytes 208928 | tf_op jit(solution)/shard_map/ppermute | solution.py:273
  15.0 6.9 %all-to-all-start = ((bf16[8,272,128]{2,1,0:T(8,128)(2,1)}), bf16[8,272,128]{2,1,0:T(8,128)(2,1)S(1)}, u32[]{:S(2)}, u32[]{:S(2)}) async-start(bf16[8,272,128]{2,1,0:T(8,128)(2,1)} %broadcast_select_fusion), calls=%async_computation | async-start | bytes 1114112 | tf_op jit(solution)/shard_map/all_to_all | solution.py:291
  24.8 1.3 collective-permute-start.2
  26.1 3.0 %collective-permute-start.4 = (bf16[384,1024]{1,0:T(8,128)(2,1)}, bf16[384,1024]{1,0:T(8,128)(2,1)S(1)}, u32[]{:S(2)}, u32[]{:S(2)}) collective-permute-start(bf16[384,1024]{1,0:T(8,128)(2,1)} %get-tuple-element.46), channel_id=1, source_target_pairs={{0,8},{1,9},{2,10},{3,11},{4,12},{5,13},{6,14},{7,15},{8,0},{9,1},... | collective-permute-start | bytes 2359304 | tf_op jit(solution)/shard_map/ppermute | solution.py:295
  32.3 5.8 %all-to-all-done = bf16[8,272,128]{2,1,0:T(8,128)(2,1)S(1)} async-done(((bf16[8,272,128]{2,1,0:T(8,128)(2,1)}), bf16[8,272,128]{2,1,0:T(8,128)(2,1)S(1)}, u32[]{:S(2)}, u32[]{:S(2)}) %all-to-all-start) | async-done | bytes 557088 | tf_op jit(solution)/shard_map/all_to_all | solution.py:291
  38.2 3.6 %all-to-all-start.2 = ((bf16[8,256,256]{2,1,0:T(8,128)(2,1)}), bf16[8,256,256]{2,1,0:T(8,128)(2,1)S(1)}, u32[]{:S(2)}, u32[]{:S(2)}) async-start(bf16[8,256,256]{2,1,0:T(8,128)(2,1)} %broadcast_in_dim.43), calls=%async_computation.2 | async-start | bytes 2097152 | tf_op jit(solution)/shard_map/all_to_all | solution.py:338
  41.8 2.8 %collective-permute-done.4.theirs_low = bf16[384,1024]{1,0:T(8,128)(2,1)S(1)} collective-permute-done((bf16[384,1024]{1,0:T(8,128)(2,1)}, bf16[384,1024]{1,0:T(8,128)(2,1)S(1)}, u32[]{:S(2)}, u32[]{:S(2)}) %collective-permute-start.4) | collective-permute-done | bytes 786464 | tf_op jit(solution)/shard_map/ppermute | solution.py:295
  44.7 3.2 %collective-permute-start.5 = (bf16[10,272,128]{2,1,0:T(8,128)(2,1)S(1)}, bf16[10,272,128]{2,1,0:T(8,128)(2,1)}, u32[]{:S(2)}, u32[]{:S(2)}) collective-permute-start(bf16[10,272,128]{2,1,0:T(8,128)(2,1)S(1)} %pad_maximum_fusion.mine), channel_id=1, source_target_pairs={{0,128},{128,0},{1,129},{129,1},{2,130},{130,2},{3,131},{131,3},{4... | collective-permute-start | bytes 2088968 | tf_op jit(solution)/shard_map/ppermute | solution.py:343
  47.8 2.9 %collective-permute-start.7 = (bf16[384,1024]{1,0:T(8,128)(2,1)}, bf16[384,1024]{1,0:T(8,128)(2,1)S(1)}, u32[]{:S(2)}, u32[]{:S(2)}) collective-permute-start(bf16[384,1024]{1,0:T(8,128)(2,1)} %get-tuple-element.51), channel_id=1, source_target_pairs={{0,8},{1,9},{2,10},{3,11},{4,12},{5,13},{6,14},{7,15},{8,0},{9,1},... | collective-permute-start | bytes 2359304 | tf_op jit(solution)/shard_map/ppermute | solution.py:295
  51.9 3.8 %attend.1 = bf16[256,512]{1,0:T(8,128)(2,1)S(1)} custom-call(s32[2]{0:T(128)S(1)} %pad_add_fusion.info.place, bf16[256,512]{1,0:T(8,128)(2,1)S(1)} %copy-done.5, f32[256,1]{1,0:T(8,128)S(1)} %copy.10.seg_query, bf16[10,272,128]{2,1,0:T(8,128)(2,1)S(1)} %pad_maximum_fusion.mine, bf16[10,272,128]{2,1,0:T(8,128)(2,1)} %collective-permute-done.5.other), custom_call_target="tpu_custom_call" | custom-call | flops 2684354560 | bytes 4194304 | tf_op jit(solution)/shard_map/attend/pallas_call | solution.py:119
  56.0 1.2 collective-permute-done.6
  57.4 3.4 %copy-done = bf16[1024,4096]{1,0:T(8,128)(2,1)S(1)} copy-done((bf16[1024,4096]{1,0:T(8,128)(2,1)S(1)}, bf16[1024,4096]{1,0:T(8,128)(2,1)}, u32[]{:S(2)}) %copy-start) | copy-done | bytes 8388632
  60.8 4.9 %project.1 = bf16[8,256,256]{2,1,0:T(8,128)(2,1)} custom-call(s32[1]{0:T(128)} %bitcast.5.core, bf16[256,1024]{1,0:T(8,128)(2,1)S(1)} %maximum_select_fusion.context, bf16[1024,4096]{1,0:T(8,128)(2,1)S(1)} %copy-done, bf16[1024,4096]{1,0:T(8,128)(2,1)S(1)} %copy-done), custom_call_target="tpu_custom_call" | custom-call | flops 1073741824 | bytes 4194304 | tf_op jit(solution)/shard_map/project/pallas_call | solution.py:150
  65.7 3.0 %collective-permute-done.7.theirs_high = bf16[384,1024]{1,0:T(8,128)(2,1)S(1)} collective-permute-done((bf16[384,1024]{1,0:T(8,128)(2,1)}, bf16[384,1024]{1,0:T(8,128)(2,1)S(1)}, u32[]{:S(2)}, u32[]{:S(2)}) %collective-permute-start.7) | collective-permute-done | bytes 786464 | tf_op jit(solution)/shard_map/ppermute | solution.py:295
  68.7 5.0 %all-to-all-start.1 = ((bf16[8,256,256]{2,1,0:T(8,128)(2,1)}), bf16[8,256,256]{2,1,0:T(8,128)(2,1)}, u32[]{:S(2)}, u32[]{:S(2)}) async-start(bf16[8,256,256]{2,1,0:T(8,128)(2,1)} %project.1), calls=%async_computation.1 | async-start | bytes 2097152 | tf_op jit(solution)/shard_map/all_to_all | solution.py:356
  73.8 1.6 %constant_dynamic-slice_fusion = (bf16[384,1024]{1,0:T(8,128)(2,1)S(1)}, bf16[384,1024]{1,0:T(8,128)(2,1)S(1)}) fusion(bf16[384,4096]{1,0:T(8,128)(2,1)} %param.12, s32[]{:T(128)S(6)} %select_n.122, s32[]{:T(128)S(6)} %select_n.121), kind=kLoop, calls=%fused_computation.26 | loop fusion | bytes 3145736 | tf_op jit(solution)/shard_map/dynamic_slice | solution.py:281
  75.4 1.5 student.1
  76.9 3.0 %collective-permute-start.8 = (bf16[384,256]{1,0:T(8,128)(2,1)S(1)}, bf16[384,256]{1,0:T(8,128)(2,1)S(1)}, u32[]{:S(2)}, u32[]{:S(2)}) collective-permute-start(bf16[384,256]{1,0:T(8,128)(2,1)S(1)} %get-tuple-element.56), channel_id=1, source_target_pairs={{0,128},{128,0},{1,129},{129,1},{2,130},{130,2},{3,131},{131,3},{4... | collective-permute-start | bytes 589832 | tf_op jit(solution)/shard_map/ppermute | solution.py:370
  79.9 1.1 collective-permute-done.8
  81.8 5.0 %all-to-all-done.1.partial = bf16[8,256,256]{2,1,0:T(8,128)(2,1)} async-done(((bf16[8,256,256]{2,1,0:T(8,128)(2,1)}), bf16[8,256,256]{2,1,0:T(8,128)(2,1)}, u32[]{:S(2)}, u32[]{:S(2)}) %all-to-all-start.1) | async-done | bytes 1048608 | tf_op jit(solution)/shard_map/all_to_all | solution.py:356
  87.7 1.5 route.1
  89.2 20.0 %all_to_all.25 = bf16[16,24,256]{2,1,0:T(8,128)(2,1)S(1)} all-to-all(bf16[16,24,256]{2,1,0:T(8,128)(2,1)S(1)} %bitcast.28), channel_id=1, replica_groups=mesh['group'=2,'tensor'=8,'seq'=16] {'seq'}, dimensions={0} | all-to-all | bytes 393216 | tf_op jit(solution)/shard_map/all_to_all | solution.py:382
  109.2 1.2 fusion.2.mine
  110.4 3.3 %collective-permute-start.9 = (bf16[384,256]{1,0:T(8,128)(2,1)S(1)}, bf16[384,256]{1,0:T(8,128)(2,1)S(1)}, u32[]{:S(2)}, u32[]{:S(2)}) collective-permute-start(bf16[384,256]{1,0:T(8,128)(2,1)S(1)} %fusion.2.mine), channel_id=1, source_target_pairs={{0,128},{128,0},{1,129},{129,1},{2,130},{130,2},{3,131},{131,3},{4... | collective-permute-start | bytes 589832 | tf_op jit(solution)/shard_map/ppermute | solution.py:396
  114.8 1.9 %gradient.1 = bf16[8,256,256]{2,1,0:T(8,128)(2,1)S(1)} custom-call(s32[2]{0:T(128)S(1)} %pad_add_fusion.info.place, bf16[384,1024]{1,0:T(8,128)(2,1)S(1)} %get-tuple-element.62.ours_low, bf16[384,1024]{1,0:T(8,128)(2,1)S(1)} %get-tuple-element.61.ours_high, bf16[384,1024]{1,0:T(8,128)(2,1)S(1)} %collective-permute-done.4.theirs_low, ...), custom_call_target="tpu_custom_call" | custom-call | flops 805306368 | bytes 6291456 | tf_op jit(solution)/shard_map/gradient/pallas_call | solution.py:226
  116.7 30.9 %all_to_all.26 = bf16[8,256,256]{2,1,0:T(8,128)(2,1)S(1)} all-to-all(bf16[8,256,256]{2,1,0:T(8,128)(2,1)S(1)} %gradient.1), channel_id=1, replica_groups={{0,1,2,3,4,5,6,7},{8,9,10,11,12,13,14,15},{16,17,18,19,20,21,22,23},{24..., dimensions={0} | all-to-all | bytes 2097152 | tf_op jit(solution)/shard_map/all_to_all | solution.py:398
  147.7 1.3 collective-permute-start.10
  149.0 6.5 %collective-permute-done.10 = bf16[256,256]{1,0:T(8,128)(2,1)S(1)} collective-permute-done((bf16[256,256]{1,0:T(8,128)(2,1)S(1)}, bf16[256,256]{1,0:T(8,128)(2,1)S(1)}, u32[]{:S(2)}, u32[]{:S(2)}) %collective-permute-start.10) | collective-permute-done | bytes 131104 | tf_op jit(solution)/shard_map/ppermute | solution.py:408
  (60 shorter events, 15.7 us)
Async XLA Ops:
  0.0 14.8 %copy-start.8 = (s32[4096,1]{0,1:T(1,128)S(1)}, s32[4096,1]{0,1:T(1,128)}, u32[]{:S(2)}) copy-start(s32[4096,1]{0,1:T(1,128)} %param.11) | copy-start | bytes 49156
  0.0 5.7 %collective-permute-start = (bf16[256,256]{1,0:T(8,128)(2,1)}, bf16[256,256]{1,0:T(8,128)(2,1)S(1)}, u32[]{:S(2)}, u32[]{:S(2)}) collective-permute-start(bf16[256,256]{1,0:T(8,128)(2,1)} %bitcast.37), channel_id=1, source_target_pairs={{0,128},{1,129},{2,130},{3,131},{4,132},{5,133},{6,134},{7,135},{8... | collective-permute-start | bytes 393224 | tf_op jit(solution)/shard_map/ppermute | solution.py:266
  6.7 7.2 %collective-permute-start.1 = (bf16[272,384]{1,0:T(8,128)(2,1)S(1)}, bf16[272,384]{1,0:T(8,128)(2,1)S(1)}, u32[]{:S(2)}, u32[]{:S(2)}) collective-permute-start(bf16[272,384]{1,0:T(8,128)(2,1)S(1)} %fusion.5), channel_id=1, source_target_pairs={{0,8},{1,9},{2,10},{3,11},{4,12},{5,13},{6,14},{7,15},{8,0},{9,1},... | collective-permute-start | bytes 626696 | tf_op jit(solution)/shard_map/ppermute | solution.py:273
  8.4 16.3 %copy-start.6 = (bf16[1,256,1024]{2,1,0:T(8,128)(2,1)S(1)}, bf16[1,256,1024]{2,1,0:T(8,128)(2,1)}, u32[]{:S(2)}) copy-start(bf16[1,256,1024]{2,1,0:T(8,128)(2,1)} %param.7) | copy-start | bytes 1572868
  8.4 20.7 %copy-start.7 = (bf16[256,512]{1,0:T(8,128)(2,1)S(1)}, bf16[256,512]{1,0:T(8,128)(2,1)}, u32[]{:S(2)}) copy-start(bf16[256,512]{1,0:T(8,128)(2,1)} %param.13) | copy-start | bytes 786436
  15.0 23.2 %all-to-all-start = ((bf16[8,272,128]{2,1,0:T(8,128)(2,1)}), bf16[8,272,128]{2,1,0:T(8,128)(2,1)S(1)}, u32[]{:S(2)}, u32[]{:S(2)}) async-start(bf16[8,272,128]{2,1,0:T(8,128)(2,1)} %broadcast_select_fusion), calls=%async_computation | async-start | bytes 1114112 | tf_op jit(solution)/shard_map/all_to_all | solution.py:291
  24.8 5.1 %collective-permute-start.2 = (bf16[256,512]{1,0:T(8,128)(2,1)S(1)}, bf16[256,512]{1,0:T(8,128)(2,1)S(1)}, u32[]{:S(2)}, u32[]{:S(2)}) collective-permute-start(bf16[256,512]{1,0:T(8,128)(2,1)S(1)} %slice.21), channel_id=1, source_target_pairs={{0,128},{1,129},{2,130},{3,131},{4,132},{5,133},{6,134},{7,135},{8... | collective-permute-start | bytes 786440 | tf_op jit(solution)/shard_map/ppermute | solution.py:298
  26.1 18.6 %collective-permute-start.4 = (bf16[384,1024]{1,0:T(8,128)(2,1)}, bf16[384,1024]{1,0:T(8,128)(2,1)S(1)}, u32[]{:S(2)}, u32[]{:S(2)}) collective-permute-start(bf16[384,1024]{1,0:T(8,128)(2,1)} %get-tuple-element.46), channel_id=1, source_target_pairs={{0,8},{1,9},{2,10},{3,11},{4,12},{5,13},{6,14},{7,15},{8,0},{9,1},... | collective-permute-start | bytes 2359304 | tf_op jit(solution)/shard_map/ppermute | solution.py:295
  30.9 1.4 collective-permute-start.3
  38.2 30.6 %all-to-all-start.2 = ((bf16[8,256,256]{2,1,0:T(8,128)(2,1)}), bf16[8,256,256]{2,1,0:T(8,128)(2,1)S(1)}, u32[]{:S(2)}, u32[]{:S(2)}) async-start(bf16[8,256,256]{2,1,0:T(8,128)(2,1)} %broadcast_in_dim.43), calls=%async_computation.2 | async-start | bytes 2097152 | tf_op jit(solution)/shard_map/all_to_all | solution.py:338
  44.7 6.2 %collective-permute-start.5 = (bf16[10,272,128]{2,1,0:T(8,128)(2,1)S(1)}, bf16[10,272,128]{2,1,0:T(8,128)(2,1)}, u32[]{:S(2)}, u32[]{:S(2)}) collective-permute-start(bf16[10,272,128]{2,1,0:T(8,128)(2,1)S(1)} %pad_maximum_fusion.mine), channel_id=1, source_target_pairs={{0,128},{128,0},{1,129},{129,1},{2,130},{130,2},{3,131},{131,3},{4... | collective-permute-start | bytes 2088968 | tf_op jit(solution)/shard_map/ppermute | solution.py:343
  47.8 20.9 %collective-permute-start.7 = (bf16[384,1024]{1,0:T(8,128)(2,1)}, bf16[384,1024]{1,0:T(8,128)(2,1)S(1)}, u32[]{:S(2)}, u32[]{:S(2)}) collective-permute-start(bf16[384,1024]{1,0:T(8,128)(2,1)} %get-tuple-element.51), channel_id=1, source_target_pairs={{0,8},{1,9},{2,10},{3,11},{4,12},{5,13},{6,14},{7,15},{8,0},{9,1},... | collective-permute-start | bytes 2359304 | tf_op jit(solution)/shard_map/ppermute | solution.py:295
  50.9 1.0 copy-start.5
  55.6 1.6 %collective-permute-start.6 = (bf16[256,512]{1,0:T(8,128)(2,1)S(1)}, bf16[256,512]{1,0:T(8,128)(2,1)S(1)}, u32[]{:S(2)}, u32[]{:S(2)}) collective-permute-start(bf16[256,512]{1,0:T(8,128)(2,1)S(1)} %attend.1), channel_id=1, source_target_pairs={{0,128},{128,0},{1,129},{129,1},{2,130},{130,2},{3,131},{131,3},{4... | collective-permute-start | bytes 786440 | tf_op jit(solution)/shard_map/ppermute | solution.py:348
  57.4 3.4 %copy-start = (bf16[1024,4096]{1,0:T(8,128)(2,1)S(1)}, bf16[1024,4096]{1,0:T(8,128)(2,1)}, u32[]{:S(2)}) copy-start(bf16[1024,4096]{1,0:T(8,128)(2,1)} %high.1) | copy-start | bytes 25165828
  68.7 5.0 %copy-start.1 = (bf16[384,1024]{1,0:T(8,128)(2,1)}, bf16[384,1024]{1,0:T(8,128)(2,1)S(1)}, u32[]{:S(2)}) copy-start(bf16[384,1024]{1,0:T(8,128)(2,1)S(1)} %collective-permute-done.7.theirs_high) | copy-start | bytes 2359300
  68.7 18.0 %all-to-all-start.1 = ((bf16[8,256,256]{2,1,0:T(8,128)(2,1)}), bf16[8,256,256]{2,1,0:T(8,128)(2,1)}, u32[]{:S(2)}, u32[]{:S(2)}) async-start(bf16[8,256,256]{2,1,0:T(8,128)(2,1)} %project.1), calls=%async_computation.1 | async-start | bytes 2097152 | tf_op jit(solution)/shard_map/all_to_all | solution.py:356
  73.8 1.6 %copy-start.2 = (bf16[384,1024]{1,0:T(8,128)(2,1)S(1)}, bf16[384,1024]{1,0:T(8,128)(2,1)}, u32[]{:S(2)}) copy-start(bf16[384,1024]{1,0:T(8,128)(2,1)} %copy-done.1) | copy-start | bytes 2359300
  76.9 37.9 %copy-start.3 = (bf16[384,1024]{1,0:T(8,128)(2,1)S(1)}, bf16[384,1024]{1,0:T(8,128)(2,1)}, u32[]{:S(2)}) copy-start(bf16[384,1024]{1,0:T(8,128)(2,1)} %copy-done.1) | copy-start | bytes 2359300
  76.9 4.1 %collective-permute-start.8 = (bf16[384,256]{1,0:T(8,128)(2,1)S(1)}, bf16[384,256]{1,0:T(8,128)(2,1)S(1)}, u32[]{:S(2)}, u32[]{:S(2)}) collective-permute-start(bf16[384,256]{1,0:T(8,128)(2,1)S(1)} %get-tuple-element.56), channel_id=1, source_target_pairs={{0,128},{128,0},{1,129},{129,1},{2,130},{130,2},{3,131},{131,3},{4... | collective-permute-start | bytes 589832 | tf_op jit(solution)/shard_map/ppermute | solution.py:370
  86.8 0.9 copy-start.4
  110.4 4.4 %collective-permute-start.9 = (bf16[384,256]{1,0:T(8,128)(2,1)S(1)}, bf16[384,256]{1,0:T(8,128)(2,1)S(1)}, u32[]{:S(2)}, u32[]{:S(2)}) collective-permute-start(bf16[384,256]{1,0:T(8,128)(2,1)S(1)} %fusion.2.mine), channel_id=1, source_target_pairs={{0,128},{128,0},{1,129},{129,1},{2,130},{130,2},{3,131},{131,3},{4... | collective-permute-start | bytes 589832 | tf_op jit(solution)/shard_map/ppermute | solution.py:396
  147.7 7.8 %collective-permute-start.10 = (bf16[256,256]{1,0:T(8,128)(2,1)S(1)}, bf16[256,256]{1,0:T(8,128)(2,1)S(1)}, u32[]{:S(2)}, u32[]{:S(2)}) collective-permute-start(bf16[256,256]{1,0:T(8,128)(2,1)S(1)} %reduce_sum.32), channel_id=1, source_target_pairs={{0,136},{1,137},{2,138},{3,139},{4,140},{5,141},{6,142},{7,143},{8... | collective-permute-start | bytes 393224 | tf_op jit(solution)/shard_map/ppermute | solution.py:408
